TPU v7x, 32 devices: a whole 2x2x4 slice. The times are simulated.
32 devices in a mesh: row: 2 (over y), col: 4 (over z), depth: 4 (over x, core).
Axes of the slice: x: 2, y: 2, z: 4, core: 2. Of those that a mesh axis runs over, the one named last changes fastest.
Arguments:
- tokens: bfloat16 [2048, 6144], P(('col', 'depth'), 'row'), may hold values from -6 to 6
- w_in: bfloat16 [6144, 12288], P('row', 'col'), may hold values from -0.078125 to 0.078125
- w_out: bfloat16 [12288, 6144], P('col', 'row'), may hold values from -0.0546875 to 0.0546875
- grad_out: bfloat16 [2048, 6144], P(('col', 'depth'), 'row'), may hold values from -1.5 to 1.5
Outputs:
- output: bfloat16 [2048, 6144], P(('col', 'depth'), 'row')
- grad_tokens: bfloat16 [2048, 6144], P(('col', 'depth'), 'row')
- grad_w_in: bfloat16 [6144, 12288], P('row', ('col', 'depth'))
- grad_w_out: bfloat16 [12288, 6144], P(('col', 'depth'), 'row')
All inputs are finite; a program needn't handle non-finite values.
Results may differ from a plain program's by a relative error of at most 0.029.
Values may be sent and summed in bfloat16 or wider, within the bound.
A program may use at most 192 MiB of HBM per device.

v0:
```python
import jax
import jax.numpy as jnp
from jax import lax
from jax.sharding import PartitionSpec as P


def gelu_tanh(value):
    return jax.nn.gelu(value, approximate=True)


def body(tokens, w_in, w_out, grad_out):
    full_tok = lax.all_gather(tokens, "col", axis=0, tiled=True)
    part_pre = jnp.dot(full_tok, w_in, preferred_element_type=jnp.float32)
    pre_share = lax.psum_scatter(
        part_pre.astype(jnp.bfloat16), "row", scatter_dimension=0, tiled=True
    ).astype(jnp.float32)
    act_share, backward = jax.vjp(gelu_tanh, pre_share)
    full_act = lax.all_gather(act_share.astype(jnp.bfloat16), "row", axis=0, tiled=True)
    output = lax.psum_scatter(
        jnp.dot(full_act, w_out, preferred_element_type=jnp.float32).astype(jnp.bfloat16),
        "col",
        scatter_dimension=0,
        tiled=True,
    )
    full_grad = lax.all_gather(grad_out, "col", axis=0, tiled=True)
    grad_act_share = lax.psum_scatter(
        lax.dot_general(
            full_grad, w_out, (((1,), (1,)), ((), ())), preferred_element_type=jnp.float32
        ).astype(jnp.bfloat16),
        "row",
        scatter_dimension=0,
        tiled=True,
    ).astype(jnp.float32)
    grad_pre_share = backward(grad_act_share)[0].astype(jnp.bfloat16)
    full_gpre = lax.all_gather(grad_pre_share, "row", axis=0, tiled=True)
    grad_tokens = lax.psum_scatter(
        lax.dot_general(
            full_gpre, w_in, (((1,), (1,)), ((), ())), preferred_element_type=jnp.float32
        ).astype(jnp.bfloat16),
        "col",
        scatter_dimension=0,
        tiled=True,
    )
    part_in = lax.dot_general(
        full_tok, full_gpre, (((0,), (0,)), ((), ())), preferred_element_type=jnp.float32
    )
    part_out = lax.dot_general(
        full_act, full_grad, (((0,), (0,)), ((), ())), preferred_element_type=jnp.float32
    )
    sum_in, sum_out = (
        lax.psum_scatter(
            part_in.astype(jnp.bfloat16), "depth", scatter_dimension=1, tiled=True
        ).astype(jnp.float32),
        lax.psum_scatter(
            part_out.astype(jnp.bfloat16), "depth", scatter_dimension=0, tiled=True
        ).astype(jnp.float32),
    )
    return (output, grad_tokens, sum_in.astype(jnp.bfloat16), sum_out.astype(jnp.bfloat16))


def solution(mesh):
    placed = (
        P(("col", "depth"), "row"),
        P("row", "col"),
        P("col", "row"),
        P(("col", "depth"), "row"),
    )
    return jax.shard_map(
        body,
        mesh=mesh,
        in_specs=placed,
        out_specs=(
            P(("col", "depth"), "row"),
            P(("col", "depth"), "row"),
            P("row", ("col", "depth")),
            P(("col", "depth"), "row"),
        ),
        check_vma=False,
    )
```

profile of v0, /device:TPU:0, one launch (start us, length us, event | category | flops | bytes accessed | tf_op | source)
XLA Modules:
  0.0 745.9 jit_solution(14817616923481148296)
XLA Ops:
  7.2 0.0 all-gather.9.cloned.1.call-start
  7.2 0.7 all-gather.9.cloned.1.call-update
  7.9 0.0 all-gather.5.cloned.1.call-start
  7.9 0.7 all-gather.5.cloned.1.call-update
  8.6 0.0 reduce-scatter.11.cloned.1.call-start
  8.7 67.1 %all-gather.9.cloned.1.call-done = bf16[512,3072]{1,0:T(8,128)(2,1)} async-done(((bf16[128,3072]{1,0:T(8,128)(2,1)}), bf16[512,3072]{1,0:T(8,128)(2,1)}) %all-gather.9.cloned.1.call-update) | async-done | bytes 3145744 | tf_op jit(solution)/shard_map/all_gather | solution.py:25
  75.8 15.9 %convolution_convert_fusion.2 = bf16[512,3072]{1,0:T(8,128)(2,1)} fusion(bf16[512,3072]{1,0:T(8,128)(2,1)} %all-gather.9.cloned.1.call-done, bf16[3072,3072]{1,0:T(8,128)(2,1)} %param.6), kind=kOutput, calls=%fused_computation.9 | convolution fusion | flops 9665249280 | bytes 25165824 | tf_op jit(solution)/shard_map/dot_general | solution.py:27
  91.7 0.0 reduce-scatter.11.cloned.1.call-update
  91.7 0.0 reduce-scatter.7.cloned.1.call-start
  91.7 47.8 %all-gather.5.cloned.1.call-done = bf16[512,3072]{1,0:T(8,128)(2,1)} async-done(((bf16[128,3072]{1,0:T(8,128)(2,1)}), bf16[512,3072]{1,0:T(8,128)(2,1)}) %all-gather.5.cloned.1.call-update) | async-done | bytes 3145744 | tf_op jit(solution)/shard_map/all_gather | solution.py:12
  139.6 15.8 %convolution_convert_fusion.4 = bf16[512,3072]{1,0:T(8,128)(2,1)} fusion(bf16[512,3072]{1,0:T(8,128)(2,1)} %all-gather.5.cloned.1.call-done, bf16[3072,3072]{1,0:T(8,128)(2,1)} %param.5), kind=kOutput, calls=%fused_computation.11 | convolution fusion | flops 9665249280 | bytes 25165824 | tf_op jit(solution)/shard_map/dot_general | solution.py:13
  155.4 0.0 reduce-scatter.7.cloned.1.call-update
  155.4 0.0 all-gather.11.cloned.1.call-start
  155.4 29.0 %reduce-scatter.11.cloned.1.call-done = bf16[256,3072]{1,0:T(8,128)(2,1)} async-done(((bf16[512,3072]{1,0:T(8,128)(2,1)}), bf16[256,3072]{1,0:T(8,128)(2,1)}) %reduce-scatter.11.cloned.1.call-update) | async-done | bytes 1572880 | tf_op jit(solution)/shard_map/reduce_scatter | solution.py:26
  184.4 46.1 %reduce-scatter.7.cloned.1.call-done = bf16[256,3072]{1,0:T(8,128)(2,1)} async-done(((bf16[512,3072]{1,0:T(8,128)(2,1)}), bf16[256,3072]{1,0:T(8,128)(2,1)}) %reduce-scatter.7.cloned.1.call-update) | async-done | bytes 1572880 | tf_op jit(solution)/shard_map/reduce_scatter | solution.py:14
  230.6 5.0 fusion.3
  235.6 0.0 copy-start.1
  235.6 0.0 all-gather.11.cloned.1.call-update
  235.6 0.0 all-gather.7.cloned.1.call-start
  235.6 0.5 all-gather.7.cloned.1.call-update
  236.2 0.2 reduce-scatter.15.cloned.1.call-start
  236.4 44.3 %all-gather.11.cloned.1.call-done = bf16[512,3072]{1,0:T(8,128)(2,1)} async-done(((bf16[256,3072]{1,0:T(8,128)(2,1)}), bf16[512,3072]{1,0:T(8,128)(2,1)}) %all-gather.11.cloned.1.call-update) | async-done | bytes 3145744 | tf_op jit(solution)/shard_map/all_gather | solution.py:35
  280.7 0.0 copy-done.1
  280.7 15.2 %convert_bitcast_fusion = bf16[3072,3072]{0,1:T(8,128)(2,1)} fusion(bf16[512,3072]{1,0:T(8,128)(2,1)} %all-gather.11.cloned.1.call-done, bf16[512,3072]{1,0:T(8,128)(2,1)S(1)} %copy-done.1), kind=kOutput, calls=%fused_computation | convolution fusion | flops 9673113600 | bytes 25165824 | tf_op jit(solution)/shard_map/dot_general | solution.py:44
  295.8 0.0 reduce-scatter.15.cloned.1.call-update
  295.9 0.0 reduce-scatter.9.cloned.1.call-start
  295.9 31.7 %all-gather.7.cloned.1.call-done = bf16[512,3072]{1,0:T(8,128)(2,1)} async-done(((bf16[256,3072]{1,0:T(8,128)(2,1)}), bf16[512,3072]{1,0:T(8,128)(2,1)}) %all-gather.7.cloned.1.call-update) | async-done | bytes 3145744 | tf_op jit(solution)/shard_map/all_gather | solution.py:18
  327.6 15.9 %convolution_convert_fusion.3 = bf16[512,3072]{1,0:T(8,128)(2,1)} fusion(bf16[512,3072]{1,0:T(8,128)(2,1)} %all-gather.7.cloned.1.call-done, bf16[3072,3072]{1,0:T(8,128)(2,1)} %param.6), kind=kOutput, calls=%fused_computation.10 | convolution fusion | flops 9665249280 | bytes 25165824 | tf_op jit(solution)/shard_map/dot_general | solution.py:20
  343.5 0.0 copy-start.2
  343.5 0.0 reduce-scatter.9.cloned.1.call-update
  343.5 0.0 reduce-scatter.13.cloned.1.call-start
  343.6 2.5 copy-done.2
  346.1 17.2 %convolution_convert_fusion.1 = bf16[512,3072]{1,0:T(8,128)(2,1)} fusion(bf16[512,3072]{1,0:T(8,128)(2,1)S(1)} %copy-done.2, bf16[3072,3072]{1,0:T(8,128)(2,1)} %param.5), kind=kOutput, calls=%fused_computation.8 | convolution fusion | flops 9665249280 | bytes 25165824 | tf_op jit(solution)/shard_map/dot_general | solution.py:37
  363.3 0.0 copy-start
  363.3 0.0 reduce-scatter.13.cloned.1.call-update
  363.3 0.3 reduce-scatter.17.cloned.1.call-start
  363.6 1.7 copy-done
  365.2 15.3 %convolution_convert_fusion = bf16[3072,3072]{1,0:T(8,128)(2,1)} fusion(bf16[512,3072]{1,0:T(8,128)(2,1)} %all-gather.7.cloned.1.call-done, bf16[512,3072]{1,0:T(8,128)(2,1)S(1)} %copy-done), kind=kOutput, calls=%fused_computation.1 | convolution fusion | flops 9673113600 | bytes 25165824 | tf_op jit(solution)/shard_map/dot_general | solution.py:47
  380.6 0.0 reduce-scatter.17.cloned.1.call-update
  380.6 89.1 %reduce-scatter.15.cloned.1.call-done = bf16[3072,768]{0,1:T(8,128)(2,1)} async-done(((bf16[3072,3072]{0,1:T(8,128)(2,1)}), bf16[3072,768]{0,1:T(8,128)(2,1)}) %reduce-scatter.15.cloned.1.call-update) | async-done | bytes 4718608 | tf_op jit(solution)/shard_map/reduce_scatter | solution.py:51
  469.7 6.6 copy.8
  476.3 56.7 %reduce-scatter.9.cloned.1.call-done = bf16[128,3072]{1,0:T(8,128)(2,1)} async-done(((bf16[512,3072]{1,0:T(8,128)(2,1)}), bf16[128,3072]{1,0:T(8,128)(2,1)}) %reduce-scatter.9.cloned.1.call-update) | async-done | bytes 786448 | tf_op jit(solution)/shard_map/reduce_scatter | solution.py:19
  533.0 63.3 %reduce-scatter.13.cloned.1.call-done = bf16[128,3072]{1,0:T(8,128)(2,1)} async-done(((bf16[512,3072]{1,0:T(8,128)(2,1)}), bf16[128,3072]{1,0:T(8,128)(2,1)}) %reduce-scatter.13.cloned.1.call-update) | async-done | bytes 786448 | tf_op jit(solution)/shard_map/reduce_scatter | solution.py:36
  596.3 142.7 %reduce-scatter.17.cloned.1.call-done = bf16[768,3072]{1,0:T(8,128)(2,1)} async-done(((bf16[3072,3072]{1,0:T(8,128)(2,1)}), bf16[768,3072]{1,0:T(8,128)(2,1)}) %reduce-scatter.17.cloned.1.call-update) | async-done | bytes 4718608 | tf_op jit(solution)/shard_map/reduce_scatter | solution.py:54
Async XLA Ops:
  7.2 68.6 %all-gather.9.cloned.1.call-start = ((), (), s32[]{:S(2)}) async-start(), calls=%async_computation.10 | async-start | bytes 3932160 | tf_op jit(solution)/shard_map/all_gather | solution.py:25
  7.9 131.7 %all-gather.5.cloned.1.call-start = ((), (), s32[]{:S(2)}) async-start(), calls=%async_computation.6 | async-start | bytes 3932160 | tf_op jit(solution)/shard_map/all_gather | solution.py:12
  8.6 175.8 %reduce-scatter.11.cloned.1.call-start = ((), (), s32[]{:S(2)}) async-start(), calls=%async_computation.11 | async-start | bytes 4718592 | tf_op jit(solution)/shard_map/reduce_scatter | solution.py:26
  91.7 138.9 %reduce-scatter.7.cloned.1.call-start = ((), (), s32[]{:S(2)}) async-start(), calls=%async_computation.7 | async-start | bytes 4718592 | tf_op jit(solution)/shard_map/reduce_scatter | solution.py:14
  155.4 125.3 %all-gather.11.cloned.1.call-start = ((), (), s32[]{:S(2)}) async-start(), calls=%async_computation.12 | async-start | bytes 4718592 | tf_op jit(solution)/shard_map/all_gather | solution.py:35
  235.6 45.1 %copy-start.1 = (bf16[512,3072]{1,0:T(8,128)(2,1)S(1)}, bf16[512,3072]{1,0:T(8,128)(2,1)}, u32[]{:S(2)}) copy-start(bf16[512,3072]{1,0:T(8,128)(2,1)} %all-gather.5.cloned.1.call-done) | copy-start | bytes 9437188
  235.6 92.0 %all-gather.7.cloned.1.call-start = ((), (), s32[]{:S(2)}) async-start(), calls=%async_computation.8 | async-start | bytes 4718592 | tf_op jit(solution)/shard_map/all_gather | solution.py:18
  236.2 233.6 %reduce-scatter.15.cloned.1.call-start = ((), (), s32[]{:S(2)}) async-start(), calls=%async_computation.14 | async-start | bytes 23592960 | tf_op jit(solution)/shard_map/reduce_scatter | solution.py:51
  295.9 237.2 %reduce-scatter.9.cloned.1.call-start = ((), (), s32[]{:S(2)}) async-start(), calls=%async_computation.9 | async-start | bytes 3932160 | tf_op jit(solution)/shard_map/reduce_scatter | solution.py:19
  343.5 2.6 copy-start.2
  343.5 252.8 %reduce-scatter.13.cloned.1.call-start = ((), (), s32[]{:S(2)}) async-start(), calls=%async_computation.13 | async-start | bytes 3932160 | tf_op jit(solution)/shard_map/reduce_scatter | solution.py:36
  363.3 2.0 copy-start
  363.3 375.7 %reduce-scatter.17.cloned.1.call-start = ((), (), s32[]{:S(2)}) async-start(), calls=%async_computation.15 | async-start | bytes 23592960 | tf_op jit(solution)/shard_map/reduce_scatter | solution.py:54
Sparse Core Ops, SparseCore 0:
  9.6 66.1 all-gather.8
  77.4 62.1 all-gather.4
  142.4 41.9 reduce-scatter.10
  187.2 43.3 reduce-scatter.6
  235.7 44.9 all-gather.10
  282.7 44.9 all-gather.6
  330.2 139.4 reduce-scatter.14
  472.7 60.2 reduce-scatter.8
  536.0 60.2 reduce-scatter.12
  599.5 139.4 reduce-scatter.16
where the time goes:
time: 746 us
  waiting for transfers between devices  620 us (83%)
  matrix products  95.2 us (13%)
  between operations  14.2 us (2%)
  local copies, waits for them, and re-layouts  10.8 us (1%)
    reduce_scatter x1, waiting for transfers between devices, body(): lax.psum_scatter(part_out.astype(jnp.bfloat16), 'depth', scatter_dimensio...  143 us
    reduce_scatter x1, waiting for transfers between devices, body(): lax.psum_scatter(part_in.astype(jnp.bfloat16), 'depth', scatter_dimension...  89.1 us
    all_gather x1, waiting for transfers between devices, body(): full_grad = lax.all_gather(grad_out, 'col', axis=0, tiled=True)  67.1 us
    reduce_scatter x1, waiting for transfers between devices, body(): lax.psum_scatter(lax.dot_general(full_gpre, w_in, (((1,), (1,)), ((), ())...  63.3 us
    reduce_scatter x1, waiting for transfers between devices, body(): lax.psum_scatter(jnp.dot(full_act, w_out, preferred_element_type=jnp.floa...  56.7 us
    all_gather x1, waiting for transfers between devices, body(): full_tok = lax.all_gather(tokens, 'col', axis=0, tiled=True)  47.8 us
    reduce_scatter x1, waiting for transfers between devices, body(): lax.psum_scatter(part_pre.astype(jnp.bfloat16), 'row', scatter_dimension=...  46.1 us
    all_gather x1, waiting for transfers between devices, body(): full_gpre = lax.all_gather(grad_pre_share, 'row', axis=0, tiled=True)  44.3 us
  transfers between devices with their start and end apart: 10, of which 10 were waited for; matrix products, arithmetic and copies ran while one was open for 14% of the time, Pallas kernels for 0%

commit v1 on v0

v1 whole, which is shorter than its diff:
```python
import jax
import jax.numpy as jnp
from jax import lax
from jax.sharding import PartitionSpec as P

CHUNKS = 2


def gelu_tanh(value):
    return jax.nn.gelu(value, approximate=True)


def dot(a, b, ca, cb):
    return lax.dot_general(
        a, b, (((ca,), (cb,)), ((), ())), preferred_element_type=jnp.float32
    )


def line_gather(block, n):
    right = left = block
    rights, lefts = [block], [block]
    for step in range(1, n):
        right = lax.ppermute(right, "col", [(c, c + 1) for c in range(step - 1, n - 1)])
        left = lax.ppermute(left, "col", [(c, c - 1) for c in range(1, n - step + 1)])
        rights.append(right)
        lefts.append(left)
    me = lax.axis_index("col")
    slots = [block]
    for k in range(1, n):
        slots.append(jnp.where(me + k < n, lefts[k], rights[n - k]))
    return slots


def line_reduce(parts, n):
    if n == 1:
        return parts[0]
    right = left = None
    for step in range(1, n):
        to_right, to_left = parts[n - step], parts[step]
        if right is not None:
            to_right = (to_right.astype(jnp.float32) + right.astype(jnp.float32)).astype(
                jnp.bfloat16
            )
            to_left = (to_left.astype(jnp.float32) + left.astype(jnp.float32)).astype(
                jnp.bfloat16
            )
        right = lax.ppermute(to_right, "col", [(c, c + 1) for c in range(step)])
        left = lax.ppermute(to_left, "col", [(c, c - 1) for c in range(n - step, n)])
    total = parts[0].astype(jnp.float32) + right.astype(jnp.float32) + left.astype(jnp.float32)
    return total.astype(jnp.bfloat16)


def row_sum(part, n):
    total = part.astype(jnp.float32)
    for step in range(1, n):
        other = lax.ppermute(part, "row", [(r, (r + step) % n) for r in range(n)])
        total = total + other.astype(jnp.float32)
    return total


def depth_masks(n):
    masks = [0]
    bit = n // 2
    while bit:
        masks = masks + [m ^ bit for m in masks]
        bit //= 2
    return masks


def depth_gather(mine, n):
    blocks = [mine]
    bit = n // 2
    while bit:
        blocks = blocks + [
            lax.ppermute(b, "depth", [(d, d ^ bit) for d in range(n)]) for b in blocks
        ]
        bit //= 2
    return blocks


def depth_exchange(mine, n):
    me = lax.axis_index("depth")
    width = mine.shape[1] // n
    out = []
    for m in depth_masks(n):
        piece = lax.dynamic_slice_in_dim(mine, (me ^ m) * width, width, axis=1)
        if m:
            piece = lax.ppermute(piece, "depth", [(d, d ^ m) for d in range(n)])
        out.append(piece)
    return out


def body(n_row, n_col, n_depth, tokens, w_in, w_out, grad_out):
    rows = tokens.shape[0] // CHUNKS
    cut = lambda a, j: a[j * rows : (j + 1) * rows]

    def gathered(a):
        return [
            jnp.concatenate(line_gather(cut(a, j), n_col), axis=0) for j in range(CHUNKS)
        ]

    def reduced(part):
        return line_reduce([cut(part, k) for k in range(n_col)], n_col)

    toks = gathered(tokens)
    grads = gathered(grad_out)
    acts, pulls = [], []
    for tok in toks:
        pre = row_sum(dot(tok, w_in, 1, 0).astype(jnp.bfloat16), n_row)
        act, pull = jax.vjp(gelu_tanh, pre)
        acts.append(act.astype(jnp.bfloat16))
        pulls.append(pull)
    gpres = []
    for grad, pull in zip(grads, pulls):
        gact = row_sum(dot(grad, w_out, 1, 1).astype(jnp.bfloat16), n_row)
        gpres.append(pull(gact)[0].astype(jnp.bfloat16))
    outs = [reduced(dot(act, w_out, 1, 0).astype(jnp.bfloat16)) for act in acts]
    gtoks = [reduced(dot(gpre, w_in, 1, 1).astype(jnp.bfloat16)) for gpre in gpres]

    def spread(pieces, fetch):
        return jnp.concatenate([b for p in pieces for b in fetch(p, n_depth)], axis=0)

    all_tok = spread(toks, depth_gather)
    all_grad = spread(grads, depth_gather)
    all_act = spread(acts, depth_exchange)
    all_gpre = spread(gpres, depth_exchange)
    grad_w_out = dot(all_act, all_grad, 0, 0).astype(jnp.bfloat16)
    grad_w_in = dot(all_tok, all_gpre, 0, 0).astype(jnp.bfloat16)
    return (
        jnp.concatenate(outs, axis=0),
        jnp.concatenate(gtoks, axis=0),
        grad_w_in,
        grad_w_out,
    )


def solution(mesh):
    placed = (
        P(("col", "depth"), "row"),
        P("row", "col"),
        P("col", "row"),
        P(("col", "depth"), "row"),
    )
    sizes = tuple(mesh.shape[a] for a in ("row", "col", "depth"))
    return jax.shard_map(
        lambda *args: body(*sizes, *args),
        mesh=mesh,
        in_specs=placed,
        out_specs=(
            P(("col", "depth"), "row"),
            P(("col", "depth"), "row"),
            P("row", ("col", "depth")),
            P(("col", "depth"), "row"),
        ),
        check_vma=False,
    )
```

time: 746 us -> 485 us (0.65)
  waiting for transfers between devices: 620 us -> 181 us
  starting transfers between devices: 0.81 us -> 126 us
  other arithmetic: 5.01 us -> 36 us
  local copies, waits for them, and re-layouts: 10.8 us -> 29.2 us
  between operations: 14.2 us -> 1.92 us
  matrix products: 95.2 us -> 105 us
    reduce_scatter x6 -> x0, waiting for transfers between devices: 427 us -> none  [the longest x1 143 us: body(): lax.psum_scatter(part_out.astype(jnp.bfloat16), 'depth', scatter_dimensio...]
    all_gather x4 -> x0, waiting for transfers between devices: 191 us -> none  [the longest x1 67.1 us: body(): full_grad = lax.all_gather(grad_out, 'col', axis=0, tiled=True)]
    ppermute x0 -> x76, waiting for transfers between devices: none -> 181 us  [the longest x4 91.3 us: row_sum(): other = lax.ppermute(part, 'row', [(r, (r + step) % n) for r in range(n)])]
    ppermute x0 -> x76, starting transfers between devices: none -> 126 us  [the longest x12 60.7 us: line_reduce(): right = lax.ppermute(to_right, 'col', [(c, c + 1) for c in range(step)])]
    unnamed x0 -> x11, other arithmetic: none -> 12 us
    unnamed x7 -> x78, local copies, waits for them, and re-layouts: 10.8 us -> 20.7 us
    convert_element_type x1 -> x14, other arithmetic: 5.01 us -> 14.8 us  [the longest x2 7.14 us: body(): gpres.append(pull(gact)[0].astype(jnp.bfloat16))]
    dot_general x6 -> x10, matrix products: 95.2 us -> 105 us  [dot(): lax.dot_general(a, b, (((ca,), (cb,)), ((), ())), preferred_element_type=...]
  transfers between devices with their start and end apart: 10 -> 76, of which waited for: 10 -> 28; matrix products, arithmetic and copies ran while one was open for 14% -> 31% of each run, Pallas kernels for 0% -> 0%
where the time goes in v1:
time: 485 us; the launch traced here: 478 us
  waiting for transfers between devices  181 us (37%)
  starting transfers between devices  126 us (26%)
  matrix products  105 us (22%)
  other arithmetic  36 us (7%)
  local copies, waits for them, and re-layouts  29.2 us (6%)
    dot_general x10, matrix products, dot(): lax.dot_general(a, b, (((ca,), (cb,)), ((), ())), preferred_element_type=...  105 us
    ppermute x4, waiting for transfers between devices, row_sum(): other = lax.ppermute(part, 'row', [(r, (r + step) % n) for r in range(n)])  91.3 us
    ppermute x12, starting transfers between devices, line_reduce(): right = lax.ppermute(to_right, 'col', [(c, c + 1) for c in range(step)])  60.7 us
    ppermute x12, waiting for transfers between devices, line_gather(): lax.ppermute(left, 'col', [(c, c - 1) for c in range(1, n - step + 1)])  30.1 us
    ppermute x12, waiting for transfers between devices, depth_exchange(): piece = lax.ppermute(piece, 'depth', [(d, d ^ m) for d in range(n)])  21.4 us
    ppermute x12, waiting for transfers between devices, line_reduce(): right = lax.ppermute(to_right, 'col', [(c, c + 1) for c in range(step)])  21.1 us
    unnamed x78, local copies, waits for them, and re-layouts  20.7 us
    ppermute x12, starting transfers between devices, line_gather(): lax.ppermute(right, 'col', [(c, c + 1) for c in range(step - 1, n - 1)])  19.5 us
  transfers between devices with their start and end apart: 76, of which 28 were waited for; matrix products, arithmetic and copies ran while one was open for 31% of the time, Pallas kernels for 0%

profile of v1, /device:TPU:0, one launch (start us, length us, event | category | flops | bytes accessed | tf_op | source)
XLA Modules:
  0.0 478.1 jit_solution(8169057057126465296)
XLA Ops:
  0.6 2.2 fusion.26
  2.8 4.9 %collective-permute-start.27 = (bf16[64,3072]{1,0:T(8,128)(2,1)S(1)}, bf16[64,3072]{1,0:T(8,128)(2,1)S(1)}, u32[]{:S(2)}, u32[]{:S(2)}) collective-permute-start(bf16[64,3072]{1,0:T(8,128)(2,1)S(1)} %get-tuple-element.74), channel_id=1, source_target_pairs={{0,4},{4,8},{8,12},{1,5},{5,9},{9,13},{2,6},{6,10},{10,14},{3,7},{... | collective-permute-start | bytes 1179656 | tf_op jit(solution)/shard_map/ppermute | solution.py:23
  9.1 2.1 fusion.27
  11.2 4.6 collective-permute-start.1
  17.8 3.4 collective-permute-done.26
  22.4 2.1 collective-permute-done.1
  25.9 3.8 collective-permute-done
  31.7 6.4 %collective-permute-done.30 = bf16[64,3072]{1,0:T(8,128)(2,1)S(1)} collective-permute-done((bf16[64,3072]{1,0:T(8,128)(2,1)S(1)}, bf16[64,3072]{1,0:T(8,128)(2,1)S(1)}, u32[]{:S(2)}, u32[]{:S(2)}) %collective-permute-start.30) | collective-permute-done | bytes 393248 | tf_op jit(solution)/shard_map/ppermute | solution.py:24
  40.1 6.5 %collective-permute-done.4 = bf16[64,3072]{1,0:T(8,128)(2,1)} collective-permute-done((bf16[64,3072]{1,0:T(8,128)(2,1)S(1)}, bf16[64,3072]{1,0:T(8,128)(2,1)}, u32[]{:S(2)}, u32[]{:S(2)}) %collective-permute-start.4) | collective-permute-done | bytes 393248 | tf_op jit(solution)/shard_map/ppermute | solution.py:24
  49.7 5.3 %collective-permute-done.31 = bf16[64,3072]{1,0:T(8,128)(2,1)S(1)} collective-permute-done((bf16[64,3072]{1,0:T(8,128)(2,1)S(1)}, bf16[64,3072]{1,0:T(8,128)(2,1)S(1)}, u32[]{:S(2)}, u32[]{:S(2)}) %collective-permute-start.31) | collective-permute-done | bytes 393248 | tf_op jit(solution)/shard_map/ppermute | solution.py:24
  55.9 9.4 %convolution_convert_fusion.5 = bf16[256,3072]{1,0:T(8,128)(2,1)S(1)} fusion(bf16[3072,3072]{1,0:T(8,128)(2,1)} %param.6, bf16[64,3072]{1,0:T(8,128)(2,1)S(1)} %get-tuple-element.11, bf16[64,3072]{1,0:T(8,128)(2,1)S(1)} %get-tuple-element.13, bf16[64,3072]{1,0:T(8,128)(2,1)S(1)} %get-tuple-element.15, bf16[64,3072]{1,0:T(8,128)(2,1)S(1)} %get-tuple-element.74), kind=kOutput, calls=%fused_computation.9 | convolution fusion | flops 4838916096 | bytes 22020096 | tf_op jit(solution)/shard_map/dot_general | solution.py:14
  65.3 1.6 collective-permute-start.32
  67.7 2.0 constant_dynamic-update-slice_fusion.11
  70.6 10.5 %convolution_convert_fusion.9 = bf16[256,3072]{1,0:T(8,128)(2,1)} fusion(bf16[3072,3072]{1,0:T(8,128)(2,1)} %param.5, bf16[64,3072]{1,0:T(8,128)(2,1)S(1)} %get-tuple-element.23, bf16[64,3072]{1,0:T(8,128)(2,1)S(1)} %get-tuple-element.25, bf16[64,3072]{1,0:T(8,128)(2,1)S(1)} %get-tuple-element.27, bf16[64,3072]{1,0:T(8,128)(2,1)S(1)} %copy-done.15), kind=kOutput, calls=%fused_computation.13 | convolution fusion | flops 4838916096 | bytes 22020096 | tf_op jit(solution)/shard_map/dot_general | solution.py:14
  81.7 2.2 collective-permute-start.40
  85.4 2.6 pad_maximum_fusion.2
  88.0 1.5 collective-permute-start.70
  90.8 11.9 %collective-permute-done.32 = bf16[256,3072]{1,0:T(8,128)(2,1)S(1)} collective-permute-done((bf16[256,3072]{1,0:T(8,128)(2,1)S(1)}, bf16[256,3072]{1,0:T(8,128)(2,1)S(1)}, u32[]{:S(2)}, u32[]{:S(2)}) %collective-permute-start.32) | collective-permute-done | bytes 1572896 | tf_op jit(solution)/shard_map/ppermute | solution.py:56
  102.7 30.8 %collective-permute-done.6 = bf16[256,3072]{1,0:T(8,128)(2,1)} collective-permute-done((bf16[256,3072]{1,0:T(8,128)(2,1)}, bf16[256,3072]{1,0:T(8,128)(2,1)}, u32[]{:S(2)}, u32[]{:S(2)}) %collective-permute-start.6) | collective-permute-done | bytes 1572896 | tf_op jit(solution)/shard_map/ppermute | solution.py:56
  133.5 1.5 collective-permute-start.52
  135.0 4.3 fusion.6
  139.2 9.2 %convolution_convert_fusion.4 = bf16[256,3072]{1,0:T(8,128)(2,1)S(1)} fusion(bf16[256,3072]{1,0:T(8,128)(2,1)S(1)} %get-tuple-element.28, bf16[3072,3072]{1,0:T(8,128)(2,1)} %param.5), kind=kOutput, calls=%fused_computation.8 | convolution fusion | flops 4832624640 | bytes 22020096 | tf_op jit(solution)/shard_map/dot_general | solution.py:14
  150.0 9.2 %convolution_convert_fusion.8 = bf16[256,3072]{1,0:T(8,128)(2,1)S(1)} fusion(bf16[256,3072]{1,0:T(8,128)(2,1)S(1)} %get-tuple-element.29, bf16[3072,3072]{1,0:T(8,128)(2,1)} %param.6), kind=kOutput, calls=%fused_computation.12 | convolution fusion | flops 4832624640 | bytes 22020096 | tf_op jit(solution)/shard_map/dot_general | solution.py:14
  160.7 2.7 constant_dynamic-update-slice_fusion.34
  163.4 3.6 collective-permute-done.52
  174.9 4.1 collective-permute-start.7
  183.1 3.6 collective-permute-done.7
  189.6 2.1 collective-permute-done.66
  193.0 8.4 %collective-permute-done.58 = bf16[256,768]{1,0:T(8,128)(2,1)S(1)} collective-permute-done((bf16[256,768]{1,0:T(8,128)(2,1)S(1)}, bf16[256,768]{1,0:T(8,128)(2,1)S(1)}, u32[]{:S(2)}, u32[]{:S(2)}) %collective-permute-start.58) | collective-permute-done | bytes 393248 | tf_op jit(solution)/shard_map/ppermute | solution.py:88
  201.5 4.4 collective-permute-start.34
  206.7 1.9 collective-permute-done.60
  213.9 7.9 %collective-permute-start.8 = (bf16[64,3072]{1,0:T(8,128)(2,1)S(1)}, bf16[64,3072]{1,0:T(8,128)(2,1)S(1)}, u32[]{:S(2)}, u32[]{:S(2)}) collective-permute-start(bf16[64,3072]{1,0:T(8,128)(2,1)S(1)} %get-tuple-element.62), channel_id=1, source_target_pairs={{0,4},{4,8},{1,5},{5,9},{2,6},{6,10},{3,7},{7,11},{16,20},{20,24},... | collective-permute-start | bytes 1179656 | tf_op jit(solution)/shard_map/ppermute | solution.py:47
  223.7 3.4 collective-permute-done.17
  234.0 11.8 %collective-permute-start.35 = (bf16[64,3072]{1,0:T(8,128)(2,1)}, bf16[64,3072]{1,0:T(8,128)(2,1)}, u32[]{:S(2)}, u32[]{:S(2)}) collective-permute-start(bf16[64,3072]{1,0:T(8,128)(2,1)} %get-tuple-element.48), channel_id=1, source_target_pairs={{0,4},{4,8},{8,12},{1,5},{5,9},{9,13},{2,6},{6,10},{10,14},{3,7},{... | collective-permute-start | bytes 1179656 | tf_op jit(solution)/shard_map/ppermute | solution.py:47
  245.8 1.9 constant_dynamic-update-slice_fusion.31
  255.0 6.3 %collective-permute-start.9 = (bf16[64,3072]{1,0:T(8,128)(2,1)}, bf16[64,3072]{1,0:T(8,128)(2,1)}, u32[]{:S(2)}, u32[]{:S(2)}) collective-permute-start(bf16[64,3072]{1,0:T(8,128)(2,1)} %get-tuple-element.60), channel_id=1, source_target_pairs={{0,4},{4,8},{8,12},{1,5},{5,9},{9,13},{2,6},{6,10},{10,14},{3,7},{... | collective-permute-start | bytes 1179656 | tf_op jit(solution)/shard_map/ppermute | solution.py:47
  262.5 9.4 %convolution_convert_fusion.7 = bf16[256,3072]{1,0:T(8,128)(2,1)S(1)} fusion(bf16[3072,3072]{1,0:T(8,128)(2,1)} %param.5, bf16[64,3072]{1,0:T(8,128)(2,1)S(1)} %get-tuple-element.17, bf16[64,3072]{1,0:T(8,128)(2,1)S(1)} %get-tuple-element.19, bf16[64,3072]{1,0:T(8,128)(2,1)S(1)} %get-tuple-element.21, bf16[64,3072]{1,0:T(8,128)(2,1)S(1)} %copy-done.10), kind=kOutput, calls=%fused_computation.11 | convolution fusion | flops 4838916096 | bytes 22020096 | tf_op jit(solution)/shard_map/dot_general | solution.py:14
  271.9 1.6 collective-permute-start.19
  273.5 9.2 %convolution_convert_fusion.3 = bf16[256,3072]{1,0:T(8,128)(2,1)S(1)} fusion(bf16[3072,3072]{1,0:T(8,128)(2,1)} %param.6, bf16[64,3072]{1,0:T(8,128)(2,1)} %get-tuple-element.79, bf16[64,3072]{1,0:T(8,128)(2,1)S(1)} %get-tuple-element.7, bf16[64,3072]{1,0:T(8,128)(2,1)S(1)} %get-tuple-element.9, bf16[64,3072]{1,0:T(8,128)(2,1)} %get-tuple-element.72), kind=kOutput, calls=%fused_computation.7 | convolution fusion | flops 4838916096 | bytes 22020096 | tf_op jit(solution)/shard_map/dot_general | solution.py:14
  283.3 2.0 add_convert_fusion.3
  285.3 2.0 add_convert_fusion.9
  287.4 2.2 pad_maximum_fusion.3
  293.0 16.3 %collective-permute-done.19 = bf16[256,3072]{1,0:T(8,128)(2,1)S(1)} collective-permute-done((bf16[256,3072]{1,0:T(8,128)(2,1)S(1)}, bf16[256,3072]{1,0:T(8,128)(2,1)S(1)}, u32[]{:S(2)}, u32[]{:S(2)}) %collective-permute-start.19) | collective-permute-done | bytes 1572896 | tf_op jit(solution)/shard_map/ppermute | solution.py:56
  309.2 32.4 %collective-permute-done.45 = bf16[256,3072]{1,0:T(8,128)(2,1)S(1)} collective-permute-done((bf16[256,3072]{1,0:T(8,128)(2,1)S(1)}, bf16[256,3072]{1,0:T(8,128)(2,1)S(1)}, u32[]{:S(2)}, u32[]{:S(2)}) %collective-permute-start.45) | collective-permute-done | bytes 1572896 | tf_op jit(solution)/shard_map/ppermute | solution.py:56
  341.6 2.9 fusion.13
  346.0 9.2 %convolution_convert_fusion.2 = bf16[256,3072]{1,0:T(8,128)(2,1)S(1)} fusion(bf16[256,3072]{1,0:T(8,128)(2,1)S(1)} %get-tuple-element.30, bf16[3072,3072]{1,0:T(8,128)(2,1)} %param.5), kind=kOutput, calls=%fused_computation.6 | convolution fusion | flops 4832624640 | bytes 22020096 | tf_op jit(solution)/shard_map/dot_general | solution.py:14
  356.7 9.2 %convolution_convert_fusion.6 = bf16[256,3072]{1,0:T(8,128)(2,1)S(1)} fusion(bf16[256,3072]{1,0:T(8,128)(2,1)S(1)} %get-tuple-element.31, bf16[3072,3072]{1,0:T(8,128)(2,1)} %param.6), kind=kOutput, calls=%fused_computation.10 | convolution fusion | flops 4832624640 | bytes 22020096 | tf_op jit(solution)/shard_map/dot_general | solution.py:14
  365.9 4.1 collective-permute-start.46
  370.0 2.7 constant_dynamic-update-slice_fusion.27
  376.3 2.7 constant_dynamic-update-slice_fusion.1
  379.0 4.2 collective-permute-start.20
  384.1 7.3 %collective-permute-done.20 = bf16[64,3072]{1,0:T(8,128)(2,1)S(1)} collective-permute-done((bf16[64,3072]{1,0:T(8,128)(2,1)S(1)}, bf16[64,3072]{1,0:T(8,128)(2,1)S(1)}, u32[]{:S(2)}, u32[]{:S(2)}) %collective-permute-start.20) | collective-permute-done | bytes 393248 | tf_op jit(solution)/shard_map/ppermute | solution.py:47
  393.9 4.4 collective-permute-start.47
  399.1 4.4 collective-permute-done.61
  404.1 4.5 collective-permute-done.63
  408.6 4.4 collective-permute-start.21
  414.1 2.5 collective-permute-start.48
  416.7 5.6 %collective-permute-done.21 = bf16[64,3072]{1,0:T(8,128)(2,1)S(1)} collective-permute-done((bf16[64,3072]{1,0:T(8,128)(2,1)S(1)}, bf16[64,3072]{1,0:T(8,128)(2,1)S(1)}, u32[]{:S(2)}, u32[]{:S(2)}) %collective-permute-start.21) | collective-permute-done | bytes 393248 | tf_op jit(solution)/shard_map/ppermute | solution.py:47
  423.9 5.1 %collective-permute-start.22 = (bf16[64,3072]{1,0:T(8,128)(2,1)S(1)}, bf16[64,3072]{1,0:T(8,128)(2,1)S(1)}, u32[]{:S(2)}, u32[]{:S(2)}) collective-permute-start(bf16[64,3072]{1,0:T(8,128)(2,1)S(1)} %get-tuple-element.66), channel_id=1, source_target_pairs={{0,4},{4,8},{8,12},{1,5},{5,9},{9,13},{2,6},{6,10},{10,14},{3,7},{... | collective-permute-start | bytes 1179656 | tf_op jit(solution)/shard_map/ppermute | solution.py:47
  429.0 1.7 collective-permute-done.48
  432.0 4.8 collective-permute-done.51
  439.1 5.9 %collective-permute-done.25 = bf16[64,3072]{1,0:T(8,128)(2,1)S(1)} collective-permute-done((bf16[64,3072]{1,0:T(8,128)(2,1)S(1)}, bf16[64,3072]{1,0:T(8,128)(2,1)S(1)}, u32[]{:S(2)}, u32[]{:S(2)}) %collective-permute-start.25) | collective-permute-done | bytes 393248 | tf_op jit(solution)/shard_map/ppermute | solution.py:48
  447.4 14.7 %convolution_convert_fusion = bf16[768,3072]{1,0:T(8,128)(2,1)} fusion(bf16[2048,768]{1,0:T(8,128)(2,1)S(1)} %constant_dynamic-update-slice_fusion.20, bf16[2048,3072]{1,0:T(8,128)(2,1)} %constant_dynamic-update-slice_fusion.26), kind=kOutput, calls=%fused_computation | convolution fusion | flops 9666035712 | bytes 20447232 | tf_op jit(solution)/shard_map/dot_general | solution.py:14
  463.4 14.5 %convolution_convert_fusion.1 = bf16[3072,768]{1,0:T(8,128)(2,1)} fusion(bf16[2048,3072]{1,0:T(8,128)(2,1)} %constant_dynamic-update-slice_fusion, bf16[2048,768]{1,0:T(8,128)(2,1)S(1)} %constant_dynamic-update-slice_fusion.14), kind=kOutput, calls=%fused_computation.1 | convolution fusion | flops 9666035712 | bytes 20447232 | tf_op jit(solution)/shard_map/dot_general | solution.py:14
  (221 shorter events, 86.1 us)
Async XLA Ops:
  2.8 14.2 %collective-permute-start.27 = (bf16[64,3072]{1,0:T(8,128)(2,1)S(1)}, bf16[64,3072]{1,0:T(8,128)(2,1)S(1)}, u32[]{:S(2)}, u32[]{:S(2)}) collective-permute-start(bf16[64,3072]{1,0:T(8,128)(2,1)S(1)} %get-tuple-element.74), channel_id=1, source_target_pairs={{0,4},{4,8},{8,12},{1,5},{5,9},{9,13},{2,6},{6,10},{10,14},{3,7},{... | collective-permute-start | bytes 1179656 | tf_op jit(solution)/shard_map/ppermute | solution.py:23
  7.8 13.4 %collective-permute-start.26 = (bf16[64,3072]{1,0:T(8,128)(2,1)S(1)}, bf16[64,3072]{1,0:T(8,128)(2,1)S(1)}, u32[]{:S(2)}, u32[]{:S(2)}) collective-permute-start(bf16[64,3072]{1,0:T(8,128)(2,1)S(1)} %get-tuple-element.74), channel_id=1, source_target_pairs={{4,0},{8,4},{12,8},{5,1},{9,5},{13,9},{6,2},{10,6},{14,10},{7,3},{... | collective-permute-start | bytes 1179656 | tf_op jit(solution)/shard_map/ppermute | solution.py:24
  11.2 13.3 %collective-permute-start.1 = (bf16[64,3072]{1,0:T(8,128)(2,1)S(1)}, bf16[64,3072]{1,0:T(8,128)(2,1)S(1)}, u32[]{:S(2)}, u32[]{:S(2)}) collective-permute-start(bf16[64,3072]{1,0:T(8,128)(2,1)S(1)} %get-tuple-element.77), channel_id=1, source_target_pairs={{0,4},{4,8},{8,12},{1,5},{5,9},{9,13},{2,6},{6,10},{10,14},{3,7},{... | collective-permute-start | bytes 1179656 | tf_op jit(solution)/shard_map/ppermute | solution.py:23
  15.8 13.9 %collective-permute-start = (bf16[64,3072]{1,0:T(8,128)(2,1)S(1)}, bf16[64,3072]{1,0:T(8,128)(2,1)S(1)}, u32[]{:S(2)}, u32[]{:S(2)}) collective-permute-start(bf16[64,3072]{1,0:T(8,128)(2,1)S(1)} %get-tuple-element.77), channel_id=1, source_target_pairs={{4,0},{8,4},{12,8},{5,1},{9,5},{13,9},{6,2},{10,6},{14,10},{7,3},{... | collective-permute-start | bytes 1179656 | tf_op jit(solution)/shard_map/ppermute | solution.py:24
  17.1 13.9 %collective-permute-start.28 = (bf16[64,3072]{1,0:T(8,128)(2,1)S(1)}, bf16[64,3072]{1,0:T(8,128)(2,1)S(1)}, u32[]{:S(2)}, u32[]{:S(2)}) collective-permute-start(bf16[64,3072]{1,0:T(8,128)(2,1)S(1)} %collective-permute-done.27), channel_id=1, source_target_pairs={{4,8},{8,12},{5,9},{9,13},{6,10},{10,14},{7,11},{11,15},{20,24},{2... | collective-permute-start | bytes 1179656 | tf_op jit(solution)/shard_map/ppermute | solution.py:23
  21.2 17.0 %collective-permute-start.30 = (bf16[64,3072]{1,0:T(8,128)(2,1)S(1)}, bf16[64,3072]{1,0:T(8,128)(2,1)S(1)}, u32[]{:S(2)}, u32[]{:S(2)}) collective-permute-start(bf16[64,3072]{1,0:T(8,128)(2,1)S(1)} %collective-permute-done.26), channel_id=1, source_target_pairs={{4,0},{8,4},{5,1},{9,5},{6,2},{10,6},{7,3},{11,7},{20,16},{24,20},... | collective-permute-start | bytes 1179656 | tf_op jit(solution)/shard_map/ppermute | solution.py:24
  24.5 14.9 %collective-permute-start.2 = (bf16[64,3072]{1,0:T(8,128)(2,1)S(1)}, bf16[64,3072]{1,0:T(8,128)(2,1)}, u32[]{:S(2)}, u32[]{:S(2)}) collective-permute-start(bf16[64,3072]{1,0:T(8,128)(2,1)S(1)} %collective-permute-done.1), channel_id=1, source_target_pairs={{4,8},{8,12},{5,9},{9,13},{6,10},{10,14},{7,11},{11,15},{20,24},{2... | collective-permute-start | bytes 1179656 | tf_op jit(solution)/shard_map/ppermute | solution.py:23
  29.7 17.0 %collective-permute-start.4 = (bf16[64,3072]{1,0:T(8,128)(2,1)S(1)}, bf16[64,3072]{1,0:T(8,128)(2,1)}, u32[]{:S(2)}, u32[]{:S(2)}) collective-permute-start(bf16[64,3072]{1,0:T(8,128)(2,1)S(1)} %collective-permute-done), channel_id=1, source_target_pairs={{4,0},{8,4},{5,1},{9,5},{6,2},{10,6},{7,3},{11,7},{20,16},{24,20},... | collective-permute-start | bytes 1179656 | tf_op jit(solution)/shard_map/ppermute | solution.py:24
  31.0 16.9 %collective-permute-start.29 = (bf16[64,3072]{1,0:T(8,128)(2,1)S(1)}, bf16[64,3072]{1,0:T(8,128)(2,1)S(1)}, u32[]{:S(2)}, u32[]{:S(2)}) collective-permute-start(bf16[64,3072]{1,0:T(8,128)(2,1)S(1)} %collective-permute-done.28), channel_id=1, source_target_pairs={{8,12},{9,13},{10,14},{11,15},{24,28},{25,29},{26,30},{27,31}} | collective-permute-start | bytes 1179656 | tf_op jit(solution)/shard_map/ppermute | solution.py:23
  38.1 16.9 %collective-permute-start.31 = (bf16[64,3072]{1,0:T(8,128)(2,1)S(1)}, bf16[64,3072]{1,0:T(8,128)(2,1)S(1)}, u32[]{:S(2)}, u32[]{:S(2)}) collective-permute-start(bf16[64,3072]{1,0:T(8,128)(2,1)S(1)} %collective-permute-done.30), channel_id=1, source_target_pairs={{4,0},{5,1},{6,2},{7,3},{20,16},{21,17},{22,18},{23,19}} | collective-permute-start | bytes 1179656 | tf_op jit(solution)/shard_map/ppermute | solution.py:24
  39.4 27.4 %collective-permute-start.3 = (bf16[64,3072]{1,0:T(8,128)(2,1)}, bf16[64,3072]{1,0:T(8,128)(2,1)S(1)}, u32[]{:S(2)}, u32[]{:S(2)}) collective-permute-start(bf16[64,3072]{1,0:T(8,128)(2,1)} %collective-permute-done.2), channel_id=1, source_target_pairs={{8,12},{9,13},{10,14},{11,15},{24,28},{25,29},{26,30},{27,31}} | collective-permute-start | bytes 1179656 | tf_op jit(solution)/shard_map/ppermute | solution.py:23
  46.7 23.1 %collective-permute-start.5 = (bf16[64,3072]{1,0:T(8,128)(2,1)}, bf16[64,3072]{1,0:T(8,128)(2,1)S(1)}, u32[]{:S(2)}, u32[]{:S(2)}) collective-permute-start(bf16[64,3072]{1,0:T(8,128)(2,1)} %collective-permute-done.4), channel_id=1, source_target_pairs={{4,0},{5,1},{6,2},{7,3},{20,16},{21,17},{22,18},{23,19}} | collective-permute-start | bytes 1179656 | tf_op jit(solution)/shard_map/ppermute | solution.py:24
  65.3 37.4 %collective-permute-start.32 = (bf16[256,3072]{1,0:T(8,128)(2,1)S(1)}, bf16[256,3072]{1,0:T(8,128)(2,1)S(1)}, u32[]{:S(2)}, u32[]{:S(2)}) collective-permute-start(bf16[256,3072]{1,0:T(8,128)(2,1)S(1)} %convolution_convert_fusion.5), channel_id=1, source_target_pairs={{0,16},{16,0},{1,17},{17,1},{2,18},{18,2},{3,19},{19,3},{4,20},{20... | collective-permute-start | bytes 4718600 | tf_op jit(solution)/shard_map/ppermute | solution.py:56
  81.1 52.3 %collective-permute-start.6 = (bf16[256,3072]{1,0:T(8,128)(2,1)}, bf16[256,3072]{1,0:T(8,128)(2,1)}, u32[]{:S(2)}, u32[]{:S(2)}) collective-permute-start(bf16[256,3072]{1,0:T(8,128)(2,1)} %convolution_convert_fusion.9), channel_id=1, source_target_pairs={{0,16},{16,0},{1,17},{17,1},{2,18},{18,2},{3,19},{19,3},{4,20},{20... | collective-permute-start | bytes 4718600 | tf_op jit(solution)/shard_map/ppermute | solution.py:56
  81.7 91.1 %collective-permute-start.40 = (bf16[64,3072]{1,0:T(8,128)(2,1)}, bf16[64,3072]{1,0:T(8,128)(2,1)}, u32[]{:S(2)}, u32[]{:S(2)}) collective-permute-start(bf16[64,3072]{1,0:T(8,128)(2,1)} %get-tuple-element.72), channel_id=1, source_target_pairs={{0,4},{4,8},{8,12},{1,5},{5,9},{9,13},{2,6},{6,10},{10,14},{3,7},{... | collective-permute-start | bytes 1179656 | tf_op jit(solution)/shard_map/ppermute | solution.py:23
  83.9 95.4 %collective-permute-start.39 = (bf16[64,3072]{1,0:T(8,128)(2,1)}, bf16[64,3072]{1,0:T(8,128)(2,1)}, u32[]{:S(2)}, u32[]{:S(2)}) collective-permute-start(bf16[64,3072]{1,0:T(8,128)(2,1)} %get-tuple-element.72), channel_id=1, source_target_pairs={{4,0},{8,4},{12,8},{5,1},{9,5},{13,9},{6,2},{10,6},{14,10},{7,3},{... | collective-permute-start | bytes 1179656 | tf_op jit(solution)/shard_map/ppermute | solution.py:24
  88.0 60.5 %collective-permute-start.70 = (bf16[256,3072]{1,0:T(8,128)(2,1)}, bf16[256,3072]{1,0:T(8,128)(2,1)S(1)}, u32[]{:S(2)}, u32[]{:S(2)}) collective-permute-start(bf16[256,3072]{1,0:T(8,128)(2,1)} %pad_maximum_fusion.2), channel_id=1, source_target_pairs={{0,2},{1,3},{2,0},{3,1},{4,6},{5,7},{6,4},{7,5},{8,10},{9,11},{10,... | collective-permute-start | bytes 4718600 | tf_op jit(solution)/shard_map/ppermute | solution.py:75
  102.7 56.6 %collective-permute-start.71 = (bf16[256,3072]{1,0:T(8,128)(2,1)}, bf16[256,3072]{1,0:T(8,128)(2,1)}, u32[]{:S(2)}, u32[]{:S(2)}) collective-permute-start(bf16[256,3072]{1,0:T(8,128)(2,1)} %pad_maximum_fusion.2), channel_id=1, source_target_pairs={{0,1},{1,0},{2,3},{3,2},{4,5},{5,4},{6,7},{7,6},{8,9},{9,8},{10,11... | collective-permute-start | bytes 4718600 | tf_op jit(solution)/shard_map/ppermute | solution.py:75
  133.5 33.6 %collective-permute-start.52 = (bf16[256,3072]{1,0:T(8,128)(2,1)}, bf16[256,3072]{1,0:T(8,128)(2,1)S(1)}, u32[]{:S(2)}, u32[]{:S(2)}) collective-permute-start(bf16[256,3072]{1,0:T(8,128)(2,1)} %pad_maximum_fusion), channel_id=1, source_target_pairs={{0,2},{1,3},{2,0},{3,1},{4,6},{5,7},{6,4},{7,5},{8,10},{9,11},{10,... | collective-permute-start | bytes 4718600 | tf_op jit(solution)/shard_map/ppermute | solution.py:75
  148.5 20.7 %collective-permute-start.53 = (bf16[256,3072]{1,0:T(8,128)(2,1)}, bf16[256,3072]{1,0:T(8,128)(2,1)S(1)}, u32[]{:S(2)}, u32[]{:S(2)}) collective-permute-start(bf16[256,3072]{1,0:T(8,128)(2,1)} %pad_maximum_fusion), channel_id=1, source_target_pairs={{0,1},{1,0},{2,3},{3,2},{4,5},{5,4},{6,7},{7,6},{8,9},{9,8},{10,11... | collective-permute-start | bytes 4718600 | tf_op jit(solution)/shard_map/ppermute | solution.py:75
  159.3 15.0 %collective-permute-start.33 = (bf16[64,3072]{1,0:T(8,128)(2,1)S(1)}, bf16[64,3072]{1,0:T(8,128)(2,1)S(1)}, u32[]{:S(2)}, u32[]{:S(2)}) collective-permute-start(bf16[64,3072]{1,0:T(8,128)(2,1)S(1)} %get-tuple-element.52), channel_id=1, source_target_pairs={{0,4},{1,5},{2,6},{3,7},{16,20},{17,21},{18,22},{19,23}} | collective-permute-start | bytes 1179656 | tf_op jit(solution)/shard_map/ppermute | solution.py:47
  174.9 11.8 %collective-permute-start.7 = (bf16[64,3072]{1,0:T(8,128)(2,1)S(1)}, bf16[64,3072]{1,0:T(8,128)(2,1)S(1)}, u32[]{:S(2)}, u32[]{:S(2)}) collective-permute-start(bf16[64,3072]{1,0:T(8,128)(2,1)S(1)} %get-tuple-element.64), channel_id=1, source_target_pairs={{0,4},{1,5},{2,6},{3,7},{16,20},{17,21},{18,22},{19,23}} | collective-permute-start | bytes 1179656 | tf_op jit(solution)/shard_map/ppermute | solution.py:47
  182.1 19.3 %collective-permute-start.58 = (bf16[256,768]{1,0:T(8,128)(2,1)S(1)}, bf16[256,768]{1,0:T(8,128)(2,1)S(1)}, u32[]{:S(2)}, u32[]{:S(2)}) collective-permute-start(bf16[256,768]{1,0:T(8,128)(2,1)S(1)} %get-tuple-element.46), channel_id=1, source_target_pairs={{0,2},{1,3},{2,0},{3,1},{4,6},{5,7},{6,4},{7,5},{8,10},{9,11},{10,... | collective-permute-start | bytes 1179656 | tf_op jit(solution)/shard_map/ppermute | solution.py:88
  186.7 19.2 %collective-permute-start.59 = (bf16[256,768]{1,0:T(8,128)(2,1)S(1)}, bf16[256,768]{1,0:T(8,128)(2,1)S(1)}, u32[]{:S(2)}, u32[]{:S(2)}) collective-permute-start(bf16[256,768]{1,0:T(8,128)(2,1)S(1)} %get-tuple-element.45), channel_id=1, source_target_pairs={{0,1},{1,0},{2,3},{3,2},{4,5},{5,4},{6,7},{7,6},{8,9},{9,8},{10,11... | collective-permute-start | bytes 1179656 | tf_op jit(solution)/shard_map/ppermute | solution.py:88
  186.9 21.7 %collective-permute-start.60 = (bf16[256,768]{1,0:T(8,128)(2,1)S(1)}, bf16[256,768]{1,0:T(8,128)(2,1)S(1)}, u32[]{:S(2)}, u32[]{:S(2)}) collective-permute-start(bf16[256,768]{1,0:T(8,128)(2,1)S(1)} %get-tuple-element.44), channel_id=1, source_target_pairs={{0,3},{1,2},{2,1},{3,0},{4,7},{5,6},{6,5},{7,4},{8,11},{9,10},{10,... | collective-permute-start | bytes 1179656 | tf_op jit(solution)/shard_map/ppermute | solution.py:88
  189.0 20.2 %collective-permute-start.41 = (bf16[64,3072]{1,0:T(8,128)(2,1)}, bf16[64,3072]{1,0:T(8,128)(2,1)S(1)}, u32[]{:S(2)}, u32[]{:S(2)}) collective-permute-start(bf16[64,3072]{1,0:T(8,128)(2,1)} %collective-permute-done.40), channel_id=1, source_target_pairs={{4,8},{8,12},{5,9},{9,13},{6,10},{10,14},{7,11},{11,15},{20,24},{2... | collective-permute-start | bytes 1179656 | tf_op jit(solution)/shard_map/ppermute | solution.py:23
  191.8 19.1 %collective-permute-start.43 = (bf16[64,3072]{1,0:T(8,128)(2,1)}, bf16[64,3072]{1,0:T(8,128)(2,1)S(1)}, u32[]{:S(2)}, u32[]{:S(2)}) collective-permute-start(bf16[64,3072]{1,0:T(8,128)(2,1)} %collective-permute-done.39), channel_id=1, source_target_pairs={{4,0},{8,4},{5,1},{9,5},{6,2},{10,6},{7,3},{11,7},{20,16},{24,20},... | collective-permute-start | bytes 1179656 | tf_op jit(solution)/shard_map/ppermute | solution.py:24
  201.5 11.7 %collective-permute-start.34 = (bf16[64,3072]{1,0:T(8,128)(2,1)S(1)}, bf16[64,3072]{1,0:T(8,128)(2,1)S(1)}, u32[]{:S(2)}, u32[]{:S(2)}) collective-permute-start(bf16[64,3072]{1,0:T(8,128)(2,1)S(1)} %get-tuple-element.50), channel_id=1, source_target_pairs={{0,4},{4,8},{1,5},{5,9},{2,6},{6,10},{3,7},{7,11},{16,20},{20,24},... | collective-permute-start | bytes 1179656 | tf_op jit(solution)/shard_map/ppermute | solution.py:47
  208.6 23.4 %collective-permute-start.72 = (bf16[256,3072]{1,0:T(8,128)(2,1)S(1)}, bf16[256,3072]{1,0:T(8,128)(2,1)S(1)}, u32[]{:S(2)}, u32[]{:S(2)}) collective-permute-start(bf16[256,3072]{1,0:T(8,128)(2,1)S(1)} %collective-permute-done.70), channel_id=1, source_target_pairs={{0,1},{1,0},{2,3},{3,2},{4,5},{5,4},{6,7},{7,6},{8,9},{9,8},{10,11... | collective-permute-start | bytes 4718600 | tf_op jit(solution)/shard_map/ppermute | solution.py:75
  209.2 13.7 %collective-permute-start.15 = (bf16[64,3072]{1,0:T(8,128)(2,1)S(1)}, bf16[64,3072]{1,0:T(8,128)(2,1)S(1)}, u32[]{:S(2)}, u32[]{:S(2)}) collective-permute-start(bf16[64,3072]{1,0:T(8,128)(2,1)S(1)} %collective-permute-done.14), channel_id=1, source_target_pairs={{4,8},{8,12},{5,9},{9,13},{6,10},{10,14},{7,11},{11,15},{20,24},{2... | collective-permute-start | bytes 1179656 | tf_op jit(solution)/shard_map/ppermute | solution.py:23
  210.8 16.3 %collective-permute-start.17 = (bf16[64,3072]{1,0:T(8,128)(2,1)S(1)}, bf16[64,3072]{1,0:T(8,128)(2,1)S(1)}, u32[]{:S(2)}, u32[]{:S(2)}) collective-permute-start(bf16[64,3072]{1,0:T(8,128)(2,1)S(1)} %collective-permute-done.13), channel_id=1, source_target_pairs={{4,0},{8,4},{5,1},{9,5},{6,2},{10,6},{7,3},{11,7},{20,16},{24,20},... | collective-permute-start | bytes 1179656 | tf_op jit(solution)/shard_map/ppermute | solution.py:24
  213.2 14.6 %collective-permute-start.11 = (bf16[64,3072]{1,0:T(8,128)(2,1)S(1)}, bf16[64,3072]{1,0:T(8,128)(2,1)S(1)}, u32[]{:S(2)}, u32[]{:S(2)}) collective-permute-start(bf16[64,3072]{1,0:T(8,128)(2,1)S(1)} %get-tuple-element.63), channel_id=1, source_target_pairs={{8,4},{12,8},{9,5},{13,9},{10,6},{14,10},{11,7},{15,11},{24,20},{2... | collective-permute-start | bytes 1179656 | tf_op jit(solution)/shard_map/ppermute | solution.py:48
  213.9 15.7 %collective-permute-start.8 = (bf16[64,3072]{1,0:T(8,128)(2,1)S(1)}, bf16[64,3072]{1,0:T(8,128)(2,1)S(1)}, u32[]{:S(2)}, u32[]{:S(2)}) collective-permute-start(bf16[64,3072]{1,0:T(8,128)(2,1)S(1)} %get-tuple-element.62), channel_id=1, source_target_pairs={{0,4},{4,8},{1,5},{5,9},{2,6},{6,10},{3,7},{7,11},{16,20},{20,24},... | collective-permute-start | bytes 1179656 | tf_op jit(solution)/shard_map/ppermute | solution.py:47
  222.9 11.1 %collective-permute-start.42 = (bf16[64,3072]{1,0:T(8,128)(2,1)S(1)}, bf16[64,3072]{1,0:T(8,128)(2,1)S(1)}, u32[]{:S(2)}, u32[]{:S(2)}) collective-permute-start(bf16[64,3072]{1,0:T(8,128)(2,1)S(1)} %collective-permute-done.41), channel_id=1, source_target_pairs={{8,12},{9,13},{10,14},{11,15},{24,28},{25,29},{26,30},{27,31}} | collective-permute-start | bytes 1179656 | tf_op jit(solution)/shard_map/ppermute | solution.py:23
  227.1 24.8 %collective-permute-start.16 = (bf16[64,3072]{1,0:T(8,128)(2,1)S(1)}, bf16[64,3072]{1,0:T(8,128)(2,1)S(1)}, u32[]{:S(2)}, u32[]{:S(2)}) collective-permute-start(bf16[64,3072]{1,0:T(8,128)(2,1)S(1)} %collective-permute-done.15), channel_id=1, source_target_pairs={{8,12},{9,13},{10,14},{11,15},{24,28},{25,29},{26,30},{27,31}} | collective-permute-start | bytes 1179656 | tf_op jit(solution)/shard_map/ppermute | solution.py:23
  227.8 27.2 %collective-permute-start.18 = (bf16[64,3072]{1,0:T(8,128)(2,1)S(1)}, bf16[64,3072]{1,0:T(8,128)(2,1)S(1)}, u32[]{:S(2)}, u32[]{:S(2)}) collective-permute-start(bf16[64,3072]{1,0:T(8,128)(2,1)S(1)} %collective-permute-done.17), channel_id=1, source_target_pairs={{4,0},{5,1},{6,2},{7,3},{20,16},{21,17},{22,18},{23,19}} | collective-permute-start | bytes 1179656 | tf_op jit(solution)/shard_map/ppermute | solution.py:24
  229.6 31.7 %collective-permute-start.44 = (bf16[64,3072]{1,0:T(8,128)(2,1)S(1)}, bf16[64,3072]{1,0:T(8,128)(2,1)S(1)}, u32[]{:S(2)}, u32[]{:S(2)}) collective-permute-start(bf16[64,3072]{1,0:T(8,128)(2,1)S(1)} %collective-permute-done.43), channel_id=1, source_target_pairs={{4,0},{5,1},{6,2},{7,3},{20,16},{21,17},{22,18},{23,19}} | collective-permute-start | bytes 1179656 | tf_op jit(solution)/shard_map/ppermute | solution.py:24
  232.0 16.5 %collective-permute-start.54 = (bf16[256,3072]{1,0:T(8,128)(2,1)S(1)}, bf16[256,3072]{1,0:T(8,128)(2,1)S(1)}, u32[]{:S(2)}, u32[]{:S(2)}) collective-permute-start(bf16[256,3072]{1,0:T(8,128)(2,1)S(1)} %collective-permute-done.52), channel_id=1, source_target_pairs={{0,1},{1,0},{2,3},{3,2},{4,5},{5,4},{6,7},{7,6},{8,9},{9,8},{10,11... | collective-permute-start | bytes 4718600 | tf_op jit(solution)/shard_map/ppermute | solution.py:75
  234.0 48.7 %collective-permute-start.35 = (bf16[64,3072]{1,0:T(8,128)(2,1)}, bf16[64,3072]{1,0:T(8,128)(2,1)}, u32[]{:S(2)}, u32[]{:S(2)}) collective-permute-start(bf16[64,3072]{1,0:T(8,128)(2,1)} %get-tuple-element.48), channel_id=1, source_target_pairs={{0,4},{4,8},{8,12},{1,5},{5,9},{9,13},{2,6},{6,10},{10,14},{3,7},{... | collective-permute-start | bytes 1179656 | tf_op jit(solution)/shard_map/ppermute | solution.py:47
  248.5 34.8 %collective-permute-start.38 = (bf16[64,3072]{1,0:T(8,128)(2,1)}, bf16[64,3072]{1,0:T(8,128)(2,1)}, u32[]{:S(2)}, u32[]{:S(2)}) collective-permute-start(bf16[64,3072]{1,0:T(8,128)(2,1)} %get-tuple-element.49), channel_id=1, source_target_pairs={{4,0},{8,4},{12,8},{5,1},{9,5},{13,9},{6,2},{10,6},{14,10},{7,3},{... | collective-permute-start | bytes 1179656 | tf_op jit(solution)/shard_map/ppermute | solution.py:48
  251.9 33.4 %collective-permute-start.12 = (bf16[64,3072]{1,0:T(8,128)(2,1)}, bf16[64,3072]{1,0:T(8,128)(2,1)}, u32[]{:S(2)}, u32[]{:S(2)}) collective-permute-start(bf16[64,3072]{1,0:T(8,128)(2,1)} %get-tuple-element.61), channel_id=1, source_target_pairs={{4,0},{8,4},{12,8},{5,1},{9,5},{13,9},{6,2},{10,6},{14,10},{7,3},{... | collective-permute-start | bytes 1179656 | tf_op jit(solution)/shard_map/ppermute | solution.py:48
  255.0 30.4 %collective-permute-start.9 = (bf16[64,3072]{1,0:T(8,128)(2,1)}, bf16[64,3072]{1,0:T(8,128)(2,1)}, u32[]{:S(2)}, u32[]{:S(2)}) collective-permute-start(bf16[64,3072]{1,0:T(8,128)(2,1)} %get-tuple-element.60), channel_id=1, source_target_pairs={{0,4},{4,8},{8,12},{1,5},{5,9},{9,13},{2,6},{6,10},{10,14},{3,7},{... | collective-permute-start | bytes 1179656 | tf_op jit(solution)/shard_map/ppermute | solution.py:47
  271.9 37.4 %collective-permute-start.19 = (bf16[256,3072]{1,0:T(8,128)(2,1)S(1)}, bf16[256,3072]{1,0:T(8,128)(2,1)S(1)}, u32[]{:S(2)}, u32[]{:S(2)}) collective-permute-start(bf16[256,3072]{1,0:T(8,128)(2,1)S(1)} %convolution_convert_fusion.7), channel_id=1, source_target_pairs={{0,16},{16,0},{1,17},{17,1},{2,18},{18,2},{3,19},{19,3},{4,20},{20... | collective-permute-start | bytes 4718600 | tf_op jit(solution)/shard_map/ppermute | solution.py:56
  282.8 58.8 %collective-permute-start.45 = (bf16[256,3072]{1,0:T(8,128)(2,1)S(1)}, bf16[256,3072]{1,0:T(8,128)(2,1)S(1)}, u32[]{:S(2)}, u32[]{:S(2)}) collective-permute-start(bf16[256,3072]{1,0:T(8,128)(2,1)S(1)} %convolution_convert_fusion.3), channel_id=1, source_target_pairs={{0,16},{16,0},{1,17},{17,1},{2,18},{18,2},{3,19},{19,3},{4,20},{20... | collective-permute-start | bytes 4718600 | tf_op jit(solution)/shard_map/ppermute | solution.py:56
  289.6 65.7 %collective-permute-start.73 = (bf16[256,3072]{1,0:T(8,128)(2,1)}, bf16[256,3072]{1,0:T(8,128)(2,1)S(1)}, u32[]{:S(2)}, u32[]{:S(2)}) collective-permute-start(bf16[256,3072]{1,0:T(8,128)(2,1)} %pad_maximum_fusion.3), channel_id=1, source_target_pairs={{0,2},{1,3},{2,0},{3,1},{4,6},{5,7},{6,4},{7,5},{8,10},{9,11},{10,... | collective-permute-start | bytes 4718600 | tf_op jit(solution)/shard_map/ppermute | solution.py:75
  290.2 75.7 %collective-permute-start.74 = (bf16[256,3072]{1,0:T(8,128)(2,1)}, bf16[256,3072]{1,0:T(8,128)(2,1)}, u32[]{:S(2)}, u32[]{:S(2)}) collective-permute-start(bf16[256,3072]{1,0:T(8,128)(2,1)} %pad_maximum_fusion.3), channel_id=1, source_target_pairs={{0,1},{1,0},{2,3},{3,2},{4,5},{5,4},{6,7},{7,6},{8,9},{9,8},{10,11... | collective-permute-start | bytes 4718600 | tf_op jit(solution)/shard_map/ppermute | solution.py:75
  291.6 81.2 %collective-permute-start.55 = (bf16[256,3072]{1,0:T(8,128)(2,1)}, bf16[256,3072]{1,0:T(8,128)(2,1)S(1)}, u32[]{:S(2)}, u32[]{:S(2)}) collective-permute-start(bf16[256,3072]{1,0:T(8,128)(2,1)} %pad_maximum_fusion.1), channel_id=1, source_target_pairs={{0,2},{1,3},{2,0},{3,1},{4,6},{5,7},{6,4},{7,5},{8,10},{9,11},{10,... | collective-permute-start | bytes 4718600 | tf_op jit(solution)/shard_map/ppermute | solution.py:75
  309.2 65.8 %collective-permute-start.56 = (bf16[256,3072]{1,0:T(8,128)(2,1)}, bf16[256,3072]{1,0:T(8,128)(2,1)}, u32[]{:S(2)}, u32[]{:S(2)}) collective-permute-start(bf16[256,3072]{1,0:T(8,128)(2,1)} %pad_maximum_fusion.1), channel_id=1, source_target_pairs={{0,1},{1,0},{2,3},{3,2},{4,5},{5,4},{6,7},{7,6},{8,9},{9,8},{10,11... | collective-permute-start | bytes 4718600 | tf_op jit(solution)/shard_map/ppermute | solution.py:75
  345.4 47.6 %collective-permute-start.67 = (bf16[256,768]{1,0:T(8,128)(2,1)S(1)}, bf16[256,768]{1,0:T(8,128)(2,1)S(1)}, u32[]{:S(2)}, u32[]{:S(2)}) collective-permute-start(bf16[256,768]{1,0:T(8,128)(2,1)S(1)} %get-tuple-element.34), channel_id=1, source_target_pairs={{0,2},{1,3},{2,0},{3,1},{4,6},{5,7},{6,4},{7,5},{8,10},{9,11},{10,... | collective-permute-start | bytes 1179656 | tf_op jit(solution)/shard_map/ppermute | solution.py:88
  355.3 38.5 %collective-permute-start.68 = (bf16[256,768]{1,0:T(8,128)(2,1)S(1)}, bf16[256,768]{1,0:T(8,128)(2,1)S(1)}, u32[]{:S(2)}, u32[]{:S(2)}) collective-permute-start(bf16[256,768]{1,0:T(8,128)(2,1)S(1)} %get-tuple-element.33), channel_id=1, source_target_pairs={{0,1},{1,0},{2,3},{3,2},{4,5},{5,4},{6,7},{7,6},{8,9},{9,8},{10,11... | collective-permute-start | bytes 1179656 | tf_op jit(solution)/shard_map/ppermute | solution.py:88
  365.9 13.1 %collective-permute-start.46 = (bf16[64,3072]{1,0:T(8,128)(2,1)S(1)}, bf16[64,3072]{1,0:T(8,128)(2,1)S(1)}, u32[]{:S(2)}, u32[]{:S(2)}) collective-permute-start(bf16[64,3072]{1,0:T(8,128)(2,1)S(1)} %get-tuple-element.58), channel_id=1, source_target_pairs={{0,4},{1,5},{2,6},{3,7},{16,20},{17,21},{18,22},{19,23}} | collective-permute-start | bytes 1179656 | tf_op jit(solution)/shard_map/ppermute | solution.py:47
  375.1 23.3 %collective-permute-start.69 = (bf16[256,768]{1,0:T(8,128)(2,1)S(1)}, bf16[256,768]{1,0:T(8,128)(2,1)S(1)}, u32[]{:S(2)}, u32[]{:S(2)}) collective-permute-start(bf16[256,768]{1,0:T(8,128)(2,1)S(1)} %get-tuple-element.32), channel_id=1, source_target_pairs={{0,3},{1,2},{2,1},{3,0},{4,7},{5,6},{6,5},{7,4},{8,11},{9,10},{10,... | collective-permute-start | bytes 1179656 | tf_op jit(solution)/shard_map/ppermute | solution.py:88
  379.0 12.4 %collective-permute-start.20 = (bf16[64,3072]{1,0:T(8,128)(2,1)S(1)}, bf16[64,3072]{1,0:T(8,128)(2,1)S(1)}, u32[]{:S(2)}, u32[]{:S(2)}) collective-permute-start(bf16[64,3072]{1,0:T(8,128)(2,1)S(1)} %get-tuple-element.70), channel_id=1, source_target_pairs={{0,4},{1,5},{2,6},{3,7},{16,20},{17,21},{18,22},{19,23}} | collective-permute-start | bytes 1179656 | tf_op jit(solution)/shard_map/ppermute | solution.py:47
  391.4 12.1 %collective-permute-start.61 = (bf16[256,768]{1,0:T(8,128)(2,1)S(1)}, bf16[256,768]{1,0:T(8,128)(2,1)S(1)}, u32[]{:S(2)}, u32[]{:S(2)}) collective-permute-start(bf16[256,768]{1,0:T(8,128)(2,1)S(1)} %get-tuple-element.42), channel_id=1, source_target_pairs={{0,2},{1,3},{2,0},{3,1},{4,6},{5,7},{6,4},{7,5},{8,10},{9,11},{10,... | collective-permute-start | bytes 1179656 | tf_op jit(solution)/shard_map/ppermute | solution.py:88
  393.0 15.6 %collective-permute-start.63 = (bf16[256,768]{1,0:T(8,128)(2,1)S(1)}, bf16[256,768]{1,0:T(8,128)(2,1)S(1)}, u32[]{:S(2)}, u32[]{:S(2)}) collective-permute-start(bf16[256,768]{1,0:T(8,128)(2,1)S(1)} %get-tuple-element.40), channel_id=1, source_target_pairs={{0,3},{1,2},{2,1},{3,0},{4,7},{5,6},{6,5},{7,4},{8,11},{9,10},{10,... | collective-permute-start | bytes 1179656 | tf_op jit(solution)/shard_map/ppermute | solution.py:88
  393.9 19.2 %collective-permute-start.47 = (bf16[64,3072]{1,0:T(8,128)(2,1)S(1)}, bf16[64,3072]{1,0:T(8,128)(2,1)S(1)}, u32[]{:S(2)}, u32[]{:S(2)}) collective-permute-start(bf16[64,3072]{1,0:T(8,128)(2,1)S(1)} %get-tuple-element.56), channel_id=1, source_target_pairs={{0,4},{4,8},{1,5},{5,9},{2,6},{6,10},{3,7},{7,11},{16,20},{20,24},... | collective-permute-start | bytes 1179656 | tf_op jit(solution)/shard_map/ppermute | solution.py:47
  398.3 15.6 %collective-permute-start.50 = (bf16[64,3072]{1,0:T(8,128)(2,1)S(1)}, bf16[64,3072]{1,0:T(8,128)(2,1)S(1)}, u32[]{:S(2)}, u32[]{:S(2)}) collective-permute-start(bf16[64,3072]{1,0:T(8,128)(2,1)S(1)} %get-tuple-element.57), channel_id=1, source_target_pairs={{8,4},{12,8},{9,5},{13,9},{10,6},{14,10},{11,7},{15,11},{24,20},{2... | collective-permute-start | bytes 1179656 | tf_op jit(solution)/shard_map/ppermute | solution.py:48
  403.5 42.7 %collective-permute-start.75 = (bf16[256,3072]{1,0:T(8,128)(2,1)S(1)}, bf16[256,3072]{1,0:T(8,128)(2,1)S(1)}, u32[]{:S(2)}, u32[]{:S(2)}) collective-permute-start(bf16[256,3072]{1,0:T(8,128)(2,1)S(1)} %collective-permute-done.73), channel_id=1, source_target_pairs={{0,1},{1,0},{2,3},{3,2},{4,5},{5,4},{6,7},{7,6},{8,9},{9,8},{10,11... | collective-permute-start | bytes 4718600 | tf_op jit(solution)/shard_map/ppermute | solution.py:75
  403.5 58.6 %collective-permute-start.57 = (bf16[256,3072]{1,0:T(8,128)(2,1)S(1)}, bf16[256,3072]{1,0:T(8,128)(2,1)S(1)}, u32[]{:S(2)}, u32[]{:S(2)}) collective-permute-start(bf16[256,3072]{1,0:T(8,128)(2,1)S(1)} %collective-permute-done.55), channel_id=1, source_target_pairs={{0,1},{1,0},{2,3},{3,2},{4,5},{5,4},{6,7},{7,6},{8,9},{9,8},{10,11... | collective-permute-start | bytes 4718600 | tf_op jit(solution)/shard_map/ppermute | solution.py:75
  408.6 13.6 %collective-permute-start.21 = (bf16[64,3072]{1,0:T(8,128)(2,1)S(1)}, bf16[64,3072]{1,0:T(8,128)(2,1)S(1)}, u32[]{:S(2)}, u32[]{:S(2)}) collective-permute-start(bf16[64,3072]{1,0:T(8,128)(2,1)S(1)} %get-tuple-element.68), channel_id=1, source_target_pairs={{0,4},{4,8},{1,5},{5,9},{2,6},{6,10},{3,7},{7,11},{16,20},{20,24},... | collective-permute-start | bytes 1179656 | tf_op jit(solution)/shard_map/ppermute | solution.py:47
  414.1 16.6 %collective-permute-start.48 = (bf16[64,3072]{1,0:T(8,128)(2,1)S(1)}, bf16[64,3072]{1,0:T(8,128)(2,1)S(1)}, u32[]{:S(2)}, u32[]{:S(2)}) collective-permute-start(bf16[64,3072]{1,0:T(8,128)(2,1)S(1)} %get-tuple-element.54), channel_id=1, source_target_pairs={{0,4},{4,8},{8,12},{1,5},{5,9},{9,13},{2,6},{6,10},{10,14},{3,7},{... | collective-permute-start | bytes 1179656 | tf_op jit(solution)/shard_map/ppermute | solution.py:47
  422.3 14.5 %collective-permute-start.51 = (bf16[64,3072]{1,0:T(8,128)(2,1)S(1)}, bf16[64,3072]{1,0:T(8,128)(2,1)S(1)}, u32[]{:S(2)}, u32[]{:S(2)}) collective-permute-start(bf16[64,3072]{1,0:T(8,128)(2,1)S(1)} %get-tuple-element.55), channel_id=1, source_target_pairs={{4,0},{8,4},{12,8},{5,1},{9,5},{13,9},{6,2},{10,6},{14,10},{7,3},{... | collective-permute-start | bytes 1179656 | tf_op jit(solution)/shard_map/ppermute | solution.py:48
  423.9 15.2 %collective-permute-start.22 = (bf16[64,3072]{1,0:T(8,128)(2,1)S(1)}, bf16[64,3072]{1,0:T(8,128)(2,1)S(1)}, u32[]{:S(2)}, u32[]{:S(2)}) collective-permute-start(bf16[64,3072]{1,0:T(8,128)(2,1)S(1)} %get-tuple-element.66), channel_id=1, source_target_pairs={{0,4},{4,8},{8,12},{1,5},{5,9},{9,13},{2,6},{6,10},{10,14},{3,7},{... | collective-permute-start | bytes 1179656 | tf_op jit(solution)/shard_map/ppermute | solution.py:47
  430.7 14.3 %collective-permute-start.25 = (bf16[64,3072]{1,0:T(8,128)(2,1)S(1)}, bf16[64,3072]{1,0:T(8,128)(2,1)S(1)}, u32[]{:S(2)}, u32[]{:S(2)}) collective-permute-start(bf16[64,3072]{1,0:T(8,128)(2,1)S(1)} %get-tuple-element.67), channel_id=1, source_target_pairs={{4,0},{8,4},{12,8},{5,1},{9,5},{13,9},{6,2},{10,6},{14,10},{7,3},{... | collective-permute-start | bytes 1179656 | tf_op jit(solution)/shard_map/ppermute | solution.py:48
  (40 other events, 462.5 us)

commit v2 on v1

--- a/solution.py
+++ b/solution.py
@@ -2,8 +2,6 @@
 import jax.numpy as jnp
 from jax import lax
 from jax.sharding import PartitionSpec as P
-
-CHUNKS = 2
 
 
 def gelu_tanh(value):
@@ -58,31 +56,23 @@
     return total
 
 
-def depth_masks(n):
-    masks = [0]
+def depth_high(mine, n):
+    blocks, masks = [mine], [0]
     bit = n // 2
-    while bit:
-        masks = masks + [m ^ bit for m in masks]
-        bit //= 2
-    return masks
-
-
-def depth_gather(mine, n):
-    blocks = [mine]
-    bit = n // 2
-    while bit:
+    while bit > 1:
         blocks = blocks + [
             lax.ppermute(b, "depth", [(d, d ^ bit) for d in range(n)]) for b in blocks
         ]
+        masks = masks + [m ^ bit for m in masks]
         bit //= 2
-    return blocks
+    return blocks, masks
 
 
-def depth_exchange(mine, n):
+def depth_exchange(mine, masks, n):
     me = lax.axis_index("depth")
     width = mine.shape[1] // n
     out = []
-    for m in depth_masks(n):
+    for m in masks:
         piece = lax.dynamic_slice_in_dim(mine, (me ^ m) * width, width, axis=1)
         if m:
             piece = lax.ppermute(piece, "depth", [(d, d ^ m) for d in range(n)])
@@ -90,48 +80,78 @@
     return out
 
 
+def cat(*blocks):
+    return jnp.concatenate(blocks, axis=0)
+
+
 def body(n_row, n_col, n_depth, tokens, w_in, w_out, grad_out):
-    rows = tokens.shape[0] // CHUNKS
-    cut = lambda a, j: a[j * rows : (j + 1) * rows]
+    rows = tokens.shape[0]
+    half = n_col // 2
+    tie = lax.optimization_barrier
 
-    def gathered(a):
-        return [
-            jnp.concatenate(line_gather(cut(a, j), n_col), axis=0) for j in range(CHUNKS)
-        ]
+    def fold(slots):
+        return cat(*slots[0::2]), cat(*slots[1::2])
 
-    def reduced(part):
-        return line_reduce([cut(part, k) for k in range(n_col)], n_col)
+    def unfold(even, odd):
+        slots = [None] * n_col
+        slots[0::2] = [even[k * rows : (k + 1) * rows] for k in range(half)]
+        slots[1::2] = [odd[k * rows : (k + 1) * rows] for k in range(half)]
+        return slots
 
-    toks = gathered(tokens)
-    grads = gathered(grad_out)
-    acts, pulls = [], []
-    for tok in toks:
-        pre = row_sum(dot(tok, w_in, 1, 0).astype(jnp.bfloat16), n_row)
-        act, pull = jax.vjp(gelu_tanh, pre)
-        acts.append(act.astype(jnp.bfloat16))
-        pulls.append(pull)
-    gpres = []
-    for grad, pull in zip(grads, pulls):
-        gact = row_sum(dot(grad, w_out, 1, 1).astype(jnp.bfloat16), n_row)
-        gpres.append(pull(gact)[0].astype(jnp.bfloat16))
-    outs = [reduced(dot(act, w_out, 1, 0).astype(jnp.bfloat16)) for act in acts]
-    gtoks = [reduced(dot(gpre, w_in, 1, 1).astype(jnp.bfloat16)) for gpre in gpres]
+    def own_part(part):
+        return part.astype(jnp.bfloat16)
 
-    def spread(pieces, fetch):
-        return jnp.concatenate([b for p in pieces for b in fetch(p, n_depth)], axis=0)
+    own_high, masks = depth_high(cat(tokens, grad_out), n_depth)
+    all_masks = masks + [m ^ 1 for m in masks]
 
-    all_tok = spread(toks, depth_gather)
-    all_grad = spread(grads, depth_gather)
-    all_act = spread(acts, depth_exchange)
-    all_gpre = spread(gpres, depth_exchange)
-    grad_w_out = dot(all_act, all_grad, 0, 0).astype(jnp.bfloat16)
-    grad_w_in = dot(all_tok, all_gpre, 0, 0).astype(jnp.bfloat16)
-    return (
-        jnp.concatenate(outs, axis=0),
-        jnp.concatenate(gtoks, axis=0),
-        grad_w_in,
-        grad_w_out,
+    tok_slots = line_gather(tokens, n_col)
+    tok_even, tok_odd = fold(tok_slots)
+    pre_even = row_sum(own_part(dot(tok_even, w_in, 1, 0)), n_row)
+    grad_out, tok_odd, own_high = tie((grad_out, tok_odd, own_high))
+    grad_slots = line_gather(grad_out, n_col)
+    part_odd = own_part(dot(tok_odd, w_in, 1, 0))
+    pre_odd = row_sum(part_odd, n_row)
+    act_even, pull_even = jax.vjp(gelu_tanh, pre_even)
+    act_odd, pull_odd = jax.vjp(gelu_tanh, pre_odd)
+    act_even, act_odd = own_part(act_even), own_part(act_odd)
+
+    tok_rest = cat(tok_even[rows:], tok_odd)
+    tok_high, _ = depth_high(tok_rest, n_depth)
+    grad_even, grad_odd = fold(grad_slots)
+    grad_rest = cat(grad_even[rows:], grad_odd)
+    grad_rest, tok_high = tie((grad_rest, tok_high))
+    grad_high, _ = depth_high(grad_rest, n_depth)
+
+    gact_odd_part = own_part(dot(grad_odd, w_out, 1, 1))
+    gact_even_part = own_part(dot(grad_even, w_out, 1, 1))
+    act_full, gact_odd_part, gact_even_part = tie(
+        (cat(act_even, act_odd), gact_odd_part, gact_even_part)
     )
+    gpre_odd = own_part(pull_odd(row_sum(gact_odd_part, n_row))[0])
+    gpre_even = own_part(pull_even(row_sum(gact_even_part, n_row))[0])
+
+    out_full = own_part(dot(act_full, w_out, 1, 0))
+    output = line_reduce(unfold(out_full[: half * rows], out_full[half * rows :]), n_col)
+    gtok_odd = own_part(dot(gpre_odd, w_in, 1, 1))
+    gtok_even = own_part(dot(gpre_even, w_in, 1, 1))
+    grad_tokens = line_reduce(unfold(gtok_even, gtok_odd), n_col)
+
+    def spread(own, highs):
+        high = cat(*[b for h, o in zip(highs, own) for b in (o, h)])
+        return cat(high, lax.ppermute(high, "depth", [(d, d ^ 1) for d in range(n_depth)]))
+
+    all_tok = spread([h[:rows] for h in own_high], tok_high)
+    all_grad = spread([h[rows:] for h in own_high], grad_high)
+    all_act = cat(*depth_exchange(act_full, all_masks, n_depth))
+    gpre_high = zip(
+        depth_exchange(gpre_even, all_masks, n_depth),
+        depth_exchange(gpre_odd, all_masks, n_depth),
+    )
+    all_gpre = cat(*[b for pair in gpre_high for b in pair])
+    all_act, gtok_even = tie((all_act, gtok_even))
+    grad_w_out = own_part(dot(all_act, all_grad, 0, 0))
+    grad_w_in = own_part(dot(all_tok, all_gpre, 0, 0))
+    return output, grad_tokens, grad_w_in, grad_w_out
 
 
 def solution(mesh):

time: 485 us -> 384 us (0.79)
  starting transfers between devices: 126 us -> 76.5 us
  waiting for transfers between devices: 181 us -> 134 us
    ppermute x4, waiting for transfers between devices: 91.3 us -> 7.15 us  [row_sum(): other = lax.ppermute(part, 'row', [(r, (r + step) % n) for r in range(n)])]
    ppermute x12 -> x6, starting transfers between devices: 60.7 us -> 29.9 us  [line_reduce(): right = lax.ppermute(to_right, 'col', [(c, c + 1) for c in range(step)])]
    ppermute x12 -> x6, waiting for transfers between devices: 30.1 us -> 49.9 us  [line_gather(): lax.ppermute(left, 'col', [(c, c - 1) for c in range(1, n - step + 1)])]
    ppermute x12 -> x9, waiting for transfers between devices: 21.4 us -> 40.2 us  [depth_exchange(): piece = lax.ppermute(piece, 'depth', [(d, d ^ m) for d in range(n)])]
    unnamed x11 -> x0, other arithmetic: 12 us -> none
    unnamed x78 -> x61, local copies, waits for them, and re-layouts: 20.7 us -> 9.01 us
    ppermute x12 -> x6, waiting for transfers between devices: 21.1 us -> 29.8 us  [line_reduce(): right = lax.ppermute(to_right, 'col', [(c, c + 1) for c in range(step)])]
    concatenate x4, local copies, waits for them, and re-layouts: 2.57 us -> 10.5 us  [cat(): return jnp.concatenate(blocks, axis=0)]
  transfers between devices with their start and end apart: 76 -> 42, of which waited for: 28 -> 17; matrix products, arithmetic and copies ran while one was open for 31% -> 34% of each run, Pallas kernels for 0% -> 0%
where the time goes in v2:
time: 384 us; the launch traced here: 377 us
  waiting for transfers between devices  134 us (35%)
  matrix products  103 us (27%)
  starting transfers between devices  76.5 us (20%)
  other arithmetic  36.1 us (9%)
  local copies, waits for them, and re-layouts  26.1 us (7%)
    dot_general x9, matrix products, dot(): lax.dot_general(a, b, (((ca,), (cb,)), ((), ())), preferred_element_type=...  103 us
    ppermute x6, waiting for transfers between devices, line_gather(): lax.ppermute(left, 'col', [(c, c - 1) for c in range(1, n - step + 1)])  49.9 us
    ppermute x9, waiting for transfers between devices, depth_exchange(): piece = lax.ppermute(piece, 'depth', [(d, d ^ m) for d in range(n)])  40.2 us
    ppermute x6, starting transfers between devices, line_reduce(): right = lax.ppermute(to_right, 'col', [(c, c + 1) for c in range(step)])  29.9 us
    ppermute x6, waiting for transfers between devices, line_reduce(): right = lax.ppermute(to_right, 'col', [(c, c + 1) for c in range(step)])  29.8 us
    ppermute x6, starting transfers between devices, line_gather(): lax.ppermute(right, 'col', [(c, c + 1) for c in range(step - 1, n - 1)])  18.1 us
    convert_element_type x4, other arithmetic, own_part(): return part.astype(jnp.bfloat16)  14.4 us
    concatenate x4, local copies, waits for them, and re-layouts, cat(): return jnp.concatenate(blocks, axis=0)  10.5 us
  transfers between devices with their start and end apart: 42, of which 17 were waited for; matrix products, arithmetic and copies ran while one was open for 34% of the time, Pallas kernels for 0%

profile of v2, /device:TPU:0, one launch (start us, length us, event | category | flops | bytes accessed | tf_op | source)
XLA Modules:
  0.0 377.4 jit_solution(3217025087784836056)
XLA Ops:
  0.6 1.3 collective-permute-start
  1.9 6.5 %collective-permute-start.2 = (bf16[128,3072]{1,0:T(8,128)(2,1)}, bf16[128,3072]{1,0:T(8,128)(2,1)}, u32[]{:S(2)}, u32[]{:S(2)}) collective-permute-start(bf16[128,3072]{1,0:T(8,128)(2,1)} %param.4), channel_id=1, source_target_pairs={{0,4},{4,8},{8,12},{1,5},{5,9},{9,13},{2,6},{6,10},{10,14},{3,7},{... | collective-permute-start | bytes 2359304 | tf_op jit(solution)/shard_map/ppermute | solution.py:21
  8.4 15.0 %collective-permute-done = bf16[128,3072]{1,0:T(8,128)(2,1)} collective-permute-done((bf16[128,3072]{1,0:T(8,128)(2,1)}, bf16[128,3072]{1,0:T(8,128)(2,1)}, u32[]{:S(2)}, u32[]{:S(2)}) %collective-permute-start) | collective-permute-done | bytes 786464 | tf_op jit(solution)/shard_map/ppermute | solution.py:22
  23.4 1.3 collective-permute-start.1
  24.7 1.5 collective-permute-start.3
  28.6 1.7 collective-permute-start.7
  30.4 14.0 %collective-permute-done.1 = bf16[128,3072]{1,0:T(8,128)(2,1)} collective-permute-done((bf16[128,3072]{1,0:T(8,128)(2,1)}, bf16[128,3072]{1,0:T(8,128)(2,1)}, u32[]{:S(2)}, u32[]{:S(2)}) %collective-permute-start.1) | collective-permute-done | bytes 786464 | tf_op jit(solution)/shard_map/ppermute | solution.py:22
  47.6 9.2 %convolution_convert_fusion.8 = bf16[256,3072]{1,0:T(8,128)(2,1)S(1)} fusion(bf16[3072,3072]{1,0:T(8,128)(2,1)} %param.5, bf16[128,3072]{1,0:T(8,128)(2,1)S(1)} %broadcast_select_fusion.5, bf16[128,3072]{1,0:T(8,128)(2,1)} %param.4), kind=kOutput, calls=%fused_computation.14 | convolution fusion | flops 4835770368 | bytes 22020096 | tf_op jit(solution)/shard_map/dot_general | solution.py:12
  56.8 1.4 collective-permute-start.4
  58.3 6.0 %collective-permute-done.6 = bf16[128,3072]{1,0:T(8,128)(2,1)S(1)} collective-permute-done((bf16[128,3072]{1,0:T(8,128)(2,1)}, bf16[128,3072]{1,0:T(8,128)(2,1)S(1)}, u32[]{:S(2)}, u32[]{:S(2)}) %collective-permute-start.6) | collective-permute-done | bytes 786464 | tf_op jit(solution)/shard_map/ppermute | solution.py:22
  64.4 1.3 broadcast_select_fusion.3
  65.8 6.0 %collective-permute-start.10 = (bf16[128,3072]{1,0:T(8,128)(2,1)S(1)}, bf16[128,3072]{1,0:T(8,128)(2,1)S(1)}, u32[]{:S(2)}, u32[]{:S(2)}) collective-permute-start(bf16[128,3072]{1,0:T(8,128)(2,1)S(1)} %copy-done.23), channel_id=1, source_target_pairs={{0,4},{4,8},{8,12},{1,5},{5,9},{9,13},{2,6},{6,10},{10,14},{3,7},{... | collective-permute-start | bytes 2359304 | tf_op jit(solution)/shard_map/ppermute | solution.py:21
  71.9 1.3 collective-permute-start.9
  73.2 10.3 %convolution_convert_fusion.7 = bf16[256,3072]{1,0:T(8,128)(2,1)} fusion(bf16[256,3072]{1,0:T(8,128)(2,1)S(1)} %pad_maximum_fusion.6, bf16[3072,3072]{1,0:T(8,128)(2,1)} %param.5), kind=kOutput, calls=%fused_computation.13 | convolution fusion | flops 4832624640 | bytes 22020096 | tf_op jit(solution)/shard_map/dot_general | solution.py:12
  83.7 1.6 collective-permute-start.29
  85.2 1.5 collective-permute-start.8
  86.7 1.6 fusion.31
  88.4 1.5 collective-permute-start.11
  90.4 1.3 collective-permute-start.13
  91.7 2.5 collective-permute-done.4
  94.2 1.3 multiply_convert_fusion.1
  95.5 14.4 %collective-permute-done.13 = bf16[128,3072]{1,0:T(8,128)(2,1)} collective-permute-done((bf16[128,3072]{1,0:T(8,128)(2,1)S(1)}, bf16[128,3072]{1,0:T(8,128)(2,1)}, u32[]{:S(2)}, u32[]{:S(2)}) %collective-permute-start.13) | collective-permute-done | bytes 786464 | tf_op jit(solution)/shard_map/ppermute | solution.py:22
  112.5 1.8 collective-permute-start.12
  114.3 10.2 %convolution_convert_fusion.5 = bf16[256,3072]{1,0:T(8,128)(2,1)} fusion(bf16[3072,3072]{1,0:T(8,128)(2,1)} %param.6, bf16[128,3072]{1,0:T(8,128)(2,1)S(1)} %broadcast_select_fusion.4, bf16[128,3072]{1,0:T(8,128)(2,1)} %param.7), kind=kOutput, calls=%fused_computation.11 | convolution fusion | flops 4835770368 | bytes 22020096 | tf_op jit(solution)/shard_map/dot_general | solution.py:12
  125.4 3.2 multiply_convert_fusion
  132.0 1.3 pad_maximum_fusion.4
  133.3 10.5 %convolution_convert_fusion.6 = bf16[256,3072]{1,0:T(8,128)(2,1)} fusion(bf16[3072,3072]{1,0:T(8,128)(2,1)} %param.6, bf16[128,3072]{1,0:T(8,128)(2,1)} %copy-done.13, bf16[128,3072]{1,0:T(8,128)(2,1)} %broadcast_select_fusion.2), kind=kOutput, calls=%fused_computation.12 | convolution fusion | flops 4835770368 | bytes 22020096 | tf_op jit(solution)/shard_map/dot_general | solution.py:12
  143.8 13.8 %convolution_convert_fusion.2 = bf16[512,3072]{1,0:T(8,128)(2,1)S(1)} fusion(bf16[512,3072]{1,0:T(8,128)(2,1)S(1)} %pad_maximum_fusion.2, bf16[3072,3072]{1,0:T(8,128)(2,1)} %param.6), kind=kOutput, calls=%fused_computation.8 | convolution fusion | flops 9665249280 | bytes 25165824 | tf_op jit(solution)/shard_map/dot_general | solution.py:12
  161.3 3.2 collective-permute-start.15
  165.5 2.4 constant_dynamic-update-slice_fusion.5
  167.9 1.5 fusion.32
  169.5 3.2 pad_maximum_fusion
  172.6 8.4 %collective-permute-done.15 = bf16[128,3072]{1,0:T(8,128)(2,1)S(1)} collective-permute-done((bf16[128,3072]{1,0:T(8,128)(2,1)S(1)}, bf16[128,3072]{1,0:T(8,128)(2,1)S(1)}, u32[]{:S(2)}, u32[]{:S(2)}) %collective-permute-start.15) | collective-permute-done | bytes 786464 | tf_op jit(solution)/shard_map/ppermute | solution.py:45
  181.1 1.6 constant_dynamic-update-slice_fusion.3
  183.2 1.6 fusion.14
  186.4 14.5 %collective-permute-done.39 = bf16[512,768]{1,0:T(8,128)(2,1)S(1)} collective-permute-done((bf16[512,768]{1,0:T(8,128)(2,1)S(1)}, bf16[512,768]{1,0:T(8,128)(2,1)S(1)}, u32[]{:S(2)}, u32[]{:S(2)}) %collective-permute-start.39) | collective-permute-done | bytes 786464 | tf_op jit(solution)/shard_map/ppermute | solution.py:78
  200.9 5.3 %collective-permute-start.16 = (bf16[128,3072]{1,0:T(8,128)(2,1)}, bf16[128,3072]{1,0:T(8,128)(2,1)}, u32[]{:S(2)}, u32[]{:S(2)}) collective-permute-start(bf16[128,3072]{1,0:T(8,128)(2,1)} %get-tuple-element.32), channel_id=1, source_target_pairs={{0,4},{4,8},{1,5},{5,9},{2,6},{6,10},{3,7},{7,11},{16,20},{20,24},... | collective-permute-start | bytes 2359304 | tf_op jit(solution)/shard_map/ppermute | solution.py:45
  206.2 1.8 pad_maximum_fusion.3
  208.0 5.0 %fusion.13 = bf16[256,3072]{1,0:T(8,128)(2,1)} fusion(bf16[256,3072]{1,0:T(8,128)(2,1)S(1)} %collective-permute-done.22, bf16[256,3072]{1,0:T(8,128)(2,1)S(1)} %copy-done.18, bf16[256,3072]{1,0:T(8,128)(2,1)} %collective-permute-done.8, bf16[256,3072]{1,0:T(8,128)(2,1)} %convolution_convert_fusion.7), kind=kLoop, calls=%fused_computation.28 | loop fusion | flops 20447232 | bytes 7864320 | tf_op jit(solution)/shard_map/convert_element_type | solution.py:102
  213.0 9.5 %convolution_convert_fusion.3 = bf16[256,3072]{1,0:T(8,128)(2,1)S(1)} fusion(bf16[256,3072]{1,0:T(8,128)(2,1)} %fusion.13, bf16[3072,3072]{1,0:T(8,128)(2,1)} %param.5), kind=kOutput, calls=%fused_computation.9 | convolution fusion | flops 4832624640 | bytes 22020096 | tf_op jit(solution)/shard_map/dot_general | solution.py:12
  223.7 2.3 collective-permute-start.23
  226.0 3.7 collective-permute-done.21
  229.7 1.5 collective-permute-start.26
  231.3 5.0 %fusion.6 = bf16[256,3072]{1,0:T(8,128)(2,1)} fusion(bf16[256,3072]{1,0:T(8,128)(2,1)} %collective-permute-done.21, bf16[256,3072]{1,0:T(8,128)(2,1)} %convolution_convert_fusion.5, bf16[256,3072]{1,0:T(8,128)(2,1)S(1)} %copy-done.5, bf16[256,3072]{1,0:T(8,128)(2,1)S(1)} %copy-done.3), kind=kLoop, calls=%fused_computation.21 | loop fusion | flops 20447232 | bytes 7864320 | tf_op jit(solution)/shard_map/convert_element_type | solution.py:102
  236.3 10.4 %convolution_convert_fusion.4 = bf16[256,3072]{1,0:T(8,128)(2,1)} fusion(bf16[256,3072]{1,0:T(8,128)(2,1)} %fusion.6, bf16[3072,3072]{1,0:T(8,128)(2,1)} %param.5), kind=kOutput, calls=%fused_computation.10 | convolution fusion | flops 4832624640 | bytes 22020096 | tf_op jit(solution)/shard_map/dot_general | solution.py:12
  246.6 1.6 constant_dynamic-slice_fusion.5
  250.3 1.8 fusion.16
  254.3 7.0 %collective-permute-done.31 = bf16[256,768]{1,0:T(8,128)(2,1)S(1)} collective-permute-done((bf16[256,768]{1,0:T(8,128)(2,1)S(1)}, bf16[256,768]{1,0:T(8,128)(2,1)S(1)}, u32[]{:S(2)}, u32[]{:S(2)}) %collective-permute-start.31) | collective-permute-done | bytes 393248 | tf_op jit(solution)/shard_map/ppermute | solution.py:78
  261.3 8.4 %collective-permute-done.32 = bf16[256,768]{1,0:T(8,128)(2,1)S(1)} collective-permute-done((bf16[256,768]{1,0:T(8,128)(2,1)S(1)}, bf16[256,768]{1,0:T(8,128)(2,1)S(1)}, u32[]{:S(2)}, u32[]{:S(2)}) %collective-permute-start.32) | collective-permute-done | bytes 393248 | tf_op jit(solution)/shard_map/ppermute | solution.py:78
  269.7 6.4 %collective-permute-start.24 = (bf16[128,3072]{1,0:T(8,128)(2,1)S(1)}, bf16[128,3072]{1,0:T(8,128)(2,1)S(1)}, u32[]{:S(2)}, u32[]{:S(2)}) collective-permute-start(bf16[128,3072]{1,0:T(8,128)(2,1)S(1)} %get-tuple-element.54), channel_id=1, source_target_pairs={{0,4},{4,8},{1,5},{5,9},{2,6},{6,10},{3,7},{7,11},{16,20},{20,24},... | collective-permute-start | bytes 2359304 | tf_op jit(solution)/shard_map/ppermute | solution.py:45
  277.2 1.7 add_convert_fusion.5
  280.1 10.2 %collective-permute-done.36 = bf16[256,768]{1,0:T(8,128)(2,1)S(1)} collective-permute-done((bf16[256,768]{1,0:T(8,128)(2,1)S(1)}, bf16[256,768]{1,0:T(8,128)(2,1)S(1)}, u32[]{:S(2)}, u32[]{:S(2)}) %collective-permute-start.36) | collective-permute-done | bytes 393248 | tf_op jit(solution)/shard_map/ppermute | solution.py:78
  290.3 7.5 %collective-permute-start.17 = (bf16[128,3072]{1,0:T(8,128)(2,1)S(1)}, bf16[128,3072]{1,0:T(8,128)(2,1)S(1)}, u32[]{:S(2)}, u32[]{:S(2)}) collective-permute-start(bf16[128,3072]{1,0:T(8,128)(2,1)S(1)} %get-tuple-element.30), channel_id=1, source_target_pairs={{0,4},{4,8},{8,12},{1,5},{5,9},{9,13},{2,6},{6,10},{10,14},{3,7},{... | collective-permute-start | bytes 2359304 | tf_op jit(solution)/shard_map/ppermute | solution.py:45
  297.8 1.3 collective-permute-start.20
  299.7 5.1 %collective-permute-start.25 = (bf16[128,3072]{1,0:T(8,128)(2,1)S(1)}, bf16[128,3072]{1,0:T(8,128)(2,1)S(1)}, u32[]{:S(2)}, u32[]{:S(2)}) collective-permute-start(bf16[128,3072]{1,0:T(8,128)(2,1)S(1)} %get-tuple-element.52), channel_id=1, source_target_pairs={{0,4},{4,8},{8,12},{1,5},{5,9},{9,13},{2,6},{6,10},{10,14},{3,7},{... | collective-permute-start | bytes 2359304 | tf_op jit(solution)/shard_map/ppermute | solution.py:45
  304.8 10.7 %collective-permute-done.17 = bf16[128,3072]{1,0:T(8,128)(2,1)S(1)} collective-permute-done((bf16[128,3072]{1,0:T(8,128)(2,1)S(1)}, bf16[128,3072]{1,0:T(8,128)(2,1)S(1)}, u32[]{:S(2)}, u32[]{:S(2)}) %collective-permute-start.17) | collective-permute-done | bytes 786464 | tf_op jit(solution)/shard_map/ppermute | solution.py:45
  316.8 1.6 constant_dynamic-update-slice_fusion.14
  318.4 1.9 collective-permute-done.20
  321.5 10.6 %collective-permute-done.25 = bf16[128,3072]{1,0:T(8,128)(2,1)S(1)} collective-permute-done((bf16[128,3072]{1,0:T(8,128)(2,1)S(1)}, bf16[128,3072]{1,0:T(8,128)(2,1)S(1)}, u32[]{:S(2)}, u32[]{:S(2)}) %collective-permute-start.25) | collective-permute-done | bytes 786464 | tf_op jit(solution)/shard_map/ppermute | solution.py:45
  332.1 5.1 %collective-permute-done.28 = bf16[128,3072]{1,0:T(8,128)(2,1)S(1)} collective-permute-done((bf16[128,3072]{1,0:T(8,128)(2,1)S(1)}, bf16[128,3072]{1,0:T(8,128)(2,1)S(1)}, u32[]{:S(2)}, u32[]{:S(2)}) %collective-permute-start.28) | collective-permute-done | bytes 786464 | tf_op jit(solution)/shard_map/ppermute | solution.py:46
  338.5 3.2 constant_dynamic-update-slice_fusion.2
  341.7 14.6 %convolution_convert_fusion.1 = bf16[3072,768]{1,0:T(8,128)(2,1)} fusion(bf16[2048,3072]{1,0:T(8,128)(2,1)} %constant_dynamic-update-slice_fusion.2, bf16[2048,768]{1,0:T(8,128)(2,1)S(1)} %copy-done.25), kind=kOutput, calls=%fused_computation.3 | convolution fusion | flops 9666035712 | bytes 20447232 | tf_op jit(solution)/shard_map/dot_general | solution.py:12
  356.3 6.1 %constant_dynamic-update-slice_fusion.13 = bf16[2048,3072]{1,0:T(8,128)(2,1)} fusion(bf16[2048,3072]{1,0:T(8,128)(2,1)} %constant_dynamic-update-slice_fusion.14, bf16[1024,3072]{1,0:T(8,128)(2,1)} %collective-permute-done.41), kind=kLoop, calls=%fused_computation.82 | loop fusion | bytes 12582912 | tf_op jit(solution)/shard_map/concatenate | solution.py:84
  362.4 14.6 %convolution_convert_fusion = bf16[768,3072]{1,0:T(8,128)(2,1)} fusion(bf16[2048,768]{1,0:T(8,128)(2,1)S(1)} %copy-done.14, bf16[2048,3072]{1,0:T(8,128)(2,1)} %constant_dynamic-update-slice_fusion.13), kind=kOutput, calls=%fused_computation.2 | convolution fusion | flops 9666035712 | bytes 20447232 | tf_op jit(solution)/shard_map/dot_general | solution.py:12
  (124 shorter events, 31.9 us)
Async XLA Ops:
  0.6 22.8 %collective-permute-start = (bf16[128,3072]{1,0:T(8,128)(2,1)}, bf16[128,3072]{1,0:T(8,128)(2,1)}, u32[]{:S(2)}, u32[]{:S(2)}) collective-permute-start(bf16[128,3072]{1,0:T(8,128)(2,1)} %param.4), channel_id=1, source_target_pairs={{4,0},{8,4},{12,8},{5,1},{9,5},{13,9},{6,2},{10,6},{14,10},{7,3},{... | collective-permute-start | bytes 2359304 | tf_op jit(solution)/shard_map/ppermute | solution.py:22
  1.9 22.8 %collective-permute-start.2 = (bf16[128,3072]{1,0:T(8,128)(2,1)}, bf16[128,3072]{1,0:T(8,128)(2,1)}, u32[]{:S(2)}, u32[]{:S(2)}) collective-permute-start(bf16[128,3072]{1,0:T(8,128)(2,1)} %param.4), channel_id=1, source_target_pairs={{0,4},{4,8},{8,12},{1,5},{5,9},{9,13},{2,6},{6,10},{10,14},{3,7},{... | collective-permute-start | bytes 2359304 | tf_op jit(solution)/shard_map/ppermute | solution.py:21
  23.4 20.9 %collective-permute-start.1 = (bf16[128,3072]{1,0:T(8,128)(2,1)}, bf16[128,3072]{1,0:T(8,128)(2,1)}, u32[]{:S(2)}, u32[]{:S(2)}) collective-permute-start(bf16[128,3072]{1,0:T(8,128)(2,1)} %collective-permute-done), channel_id=1, source_target_pairs={{4,0},{8,4},{5,1},{9,5},{6,2},{10,6},{7,3},{11,7},{20,16},{24,20},... | collective-permute-start | bytes 2359304 | tf_op jit(solution)/shard_map/ppermute | solution.py:22
  24.7 20.9 %collective-permute-start.3 = (bf16[128,3072]{1,0:T(8,128)(2,1)}, bf16[128,3072]{1,0:T(8,128)(2,1)}, u32[]{:S(2)}, u32[]{:S(2)}) collective-permute-start(bf16[128,3072]{1,0:T(8,128)(2,1)} %collective-permute-done.2), channel_id=1, source_target_pairs={{4,8},{8,12},{5,9},{9,13},{6,10},{10,14},{7,11},{11,15},{20,24},{2... | collective-permute-start | bytes 2359304 | tf_op jit(solution)/shard_map/ppermute | solution.py:21
  28.6 28.2 %copy-start.7 = (bf16[256,3072]{1,0:T(8,128)(2,1)}, bf16[256,3072]{1,0:T(8,128)(2,1)S(1)}, u32[]{:S(2)}) copy-start(bf16[256,3072]{1,0:T(8,128)(2,1)S(1)} %constant_dynamic-update-slice_fusion) | copy-start | bytes 4718596
  28.6 37.1 %collective-permute-start.7 = (bf16[256,3072]{1,0:T(8,128)(2,1)S(1)}, bf16[256,3072]{1,0:T(8,128)(2,1)S(1)}, u32[]{:S(2)}, u32[]{:S(2)}) collective-permute-start(bf16[256,3072]{1,0:T(8,128)(2,1)S(1)} %constant_dynamic-update-slice_fusion), channel_id=1, source_target_pairs={{0,2},{1,3},{2,0},{3,1},{4,6},{5,7},{6,4},{7,5},{8,10},{9,11},{10,... | collective-permute-start | bytes 4718600 | tf_op jit(solution)/shard_map/ppermute | solution.py:64
  44.3 19.9 %collective-permute-start.6 = (bf16[128,3072]{1,0:T(8,128)(2,1)}, bf16[128,3072]{1,0:T(8,128)(2,1)S(1)}, u32[]{:S(2)}, u32[]{:S(2)}) collective-permute-start(bf16[128,3072]{1,0:T(8,128)(2,1)} %collective-permute-done.1), channel_id=1, source_target_pairs={{4,0},{5,1},{6,2},{7,3},{20,16},{21,17},{22,18},{23,19}} | collective-permute-start | bytes 2359304 | tf_op jit(solution)/shard_map/ppermute | solution.py:22
  45.6 18.7 %collective-permute-start.5 = (bf16[128,3072]{1,0:T(8,128)(2,1)}, bf16[128,3072]{1,0:T(8,128)(2,1)S(1)}, u32[]{:S(2)}, u32[]{:S(2)}) collective-permute-start(bf16[128,3072]{1,0:T(8,128)(2,1)} %collective-permute-done.3), channel_id=1, source_target_pairs={{8,12},{9,13},{10,14},{11,15},{24,28},{25,29},{26,30},{27,31}} | collective-permute-start | bytes 2359304 | tf_op jit(solution)/shard_map/ppermute | solution.py:21
  56.8 37.4 %copy-start.2 = (bf16[256,3072]{1,0:T(8,128)(2,1)}, bf16[256,3072]{1,0:T(8,128)(2,1)S(1)}, u32[]{:S(2)}) copy-start(bf16[256,3072]{1,0:T(8,128)(2,1)S(1)} %convolution_convert_fusion.8) | copy-start | bytes 4718596
  56.8 37.4 %collective-permute-start.4 = (bf16[256,3072]{1,0:T(8,128)(2,1)S(1)}, bf16[256,3072]{1,0:T(8,128)(2,1)S(1)}, u32[]{:S(2)}, u32[]{:S(2)}) collective-permute-start(bf16[256,3072]{1,0:T(8,128)(2,1)S(1)} %convolution_convert_fusion.8), channel_id=1, source_target_pairs={{0,16},{16,0},{1,17},{17,1},{2,18},{18,2},{3,19},{19,3},{4,20},{20... | collective-permute-start | bytes 4718600 | tf_op jit(solution)/shard_map/ppermute | solution.py:54
  65.8 17.7 %copy-start.15 = (bf16[256,3072]{1,0:T(8,128)(2,1)}, bf16[256,3072]{1,0:T(8,128)(2,1)S(1)}, u32[]{:S(2)}) copy-start(bf16[256,3072]{1,0:T(8,128)(2,1)S(1)} %collective-permute-done.7) | copy-start | bytes 4718596
  65.8 22.6 %collective-permute-start.10 = (bf16[128,3072]{1,0:T(8,128)(2,1)S(1)}, bf16[128,3072]{1,0:T(8,128)(2,1)S(1)}, u32[]{:S(2)}, u32[]{:S(2)}) collective-permute-start(bf16[128,3072]{1,0:T(8,128)(2,1)S(1)} %copy-done.23), channel_id=1, source_target_pairs={{0,4},{4,8},{8,12},{1,5},{5,9},{9,13},{2,6},{6,10},{10,14},{3,7},{... | collective-permute-start | bytes 2359304 | tf_op jit(solution)/shard_map/ppermute | solution.py:21
  71.9 18.5 %collective-permute-start.9 = (bf16[128,3072]{1,0:T(8,128)(2,1)S(1)}, bf16[128,3072]{1,0:T(8,128)(2,1)S(1)}, u32[]{:S(2)}, u32[]{:S(2)}) collective-permute-start(bf16[128,3072]{1,0:T(8,128)(2,1)S(1)} %copy-done.23), channel_id=1, source_target_pairs={{4,0},{8,4},{12,8},{5,1},{9,5},{13,9},{6,2},{10,6},{14,10},{7,3},{... | collective-permute-start | bytes 2359304 | tf_op jit(solution)/shard_map/ppermute | solution.py:22
  83.5 3.2 copy-start.8
  83.7 60.1 %collective-permute-start.29 = (bf16[384,3072]{1,0:T(8,128)(2,1)S(1)}, bf16[384,3072]{1,0:T(8,128)(2,1)S(1)}, u32[]{:S(2)}, u32[]{:S(2)}) collective-permute-start(bf16[384,3072]{1,0:T(8,128)(2,1)S(1)} %pad_maximum_fusion.5), channel_id=1, source_target_pairs={{0,2},{1,3},{2,0},{3,1},{4,6},{5,7},{6,4},{7,5},{8,10},{9,11},{10,... | collective-permute-start | bytes 7077896 | tf_op jit(solution)/shard_map/ppermute | solution.py:64
  85.2 40.2 %collective-permute-start.8 = (bf16[256,3072]{1,0:T(8,128)(2,1)}, bf16[256,3072]{1,0:T(8,128)(2,1)}, u32[]{:S(2)}, u32[]{:S(2)}) collective-permute-start(bf16[256,3072]{1,0:T(8,128)(2,1)} %convolution_convert_fusion.7), channel_id=1, source_target_pairs={{0,16},{16,0},{1,17},{17,1},{2,18},{18,2},{3,19},{19,3},{4,20},{20... | collective-permute-start | bytes 4718600 | tf_op jit(solution)/shard_map/ppermute | solution.py:54
  88.4 24.1 %copy-start.21 = (bf16[128,3072]{1,0:T(8,128)(2,1)}, bf16[128,3072]{1,0:T(8,128)(2,1)S(1)}, u32[]{:S(2)}) copy-start(bf16[128,3072]{1,0:T(8,128)(2,1)S(1)} %collective-permute-done.10) | copy-start | bytes 2359300
  88.4 22.9 %collective-permute-start.11 = (bf16[128,3072]{1,0:T(8,128)(2,1)S(1)}, bf16[128,3072]{1,0:T(8,128)(2,1)}, u32[]{:S(2)}, u32[]{:S(2)}) collective-permute-start(bf16[128,3072]{1,0:T(8,128)(2,1)S(1)} %collective-permute-done.10), channel_id=1, source_target_pairs={{4,8},{8,12},{5,9},{9,13},{6,10},{10,14},{7,11},{11,15},{20,24},{2... | collective-permute-start | bytes 2359304 | tf_op jit(solution)/shard_map/ppermute | solution.py:21
  90.4 20.8 %copy-start.19 = (bf16[128,3072]{1,0:T(8,128)(2,1)}, bf16[128,3072]{1,0:T(8,128)(2,1)S(1)}, u32[]{:S(2)}) copy-start(bf16[128,3072]{1,0:T(8,128)(2,1)S(1)} %collective-permute-done.9) | copy-start | bytes 2359300
  90.4 19.5 %collective-permute-start.13 = (bf16[128,3072]{1,0:T(8,128)(2,1)S(1)}, bf16[128,3072]{1,0:T(8,128)(2,1)}, u32[]{:S(2)}, u32[]{:S(2)}) collective-permute-start(bf16[128,3072]{1,0:T(8,128)(2,1)S(1)} %collective-permute-done.9), channel_id=1, source_target_pairs={{4,0},{8,4},{5,1},{9,5},{6,2},{10,6},{7,3},{11,7},{20,16},{24,20},... | collective-permute-start | bytes 2359304 | tf_op jit(solution)/shard_map/ppermute | solution.py:22
  94.2 18.2 %copy-start.4 = (bf16[256,3072]{1,0:T(8,128)(2,1)}, bf16[256,3072]{1,0:T(8,128)(2,1)S(1)}, u32[]{:S(2)}) copy-start(bf16[256,3072]{1,0:T(8,128)(2,1)S(1)} %collective-permute-done.4) | copy-start | bytes 4718596
  109.9 18.9 %collective-permute-start.14 = (bf16[128,3072]{1,0:T(8,128)(2,1)}, bf16[128,3072]{1,0:T(8,128)(2,1)}, u32[]{:S(2)}, u32[]{:S(2)}) collective-permute-start(bf16[128,3072]{1,0:T(8,128)(2,1)} %collective-permute-done.13), channel_id=1, source_target_pairs={{4,0},{5,1},{6,2},{7,3},{20,16},{21,17},{22,18},{23,19}} | collective-permute-start | bytes 2359304 | tf_op jit(solution)/shard_map/ppermute | solution.py:22
  112.5 11.9 %copy-start.11 = (bf16[128,3072]{1,0:T(8,128)(2,1)}, bf16[128,3072]{1,0:T(8,128)(2,1)S(1)}, u32[]{:S(2)}) copy-start(bf16[128,3072]{1,0:T(8,128)(2,1)S(1)} %broadcast_select_fusion.4) | copy-start | bytes 2359300
  112.5 18.4 %collective-permute-start.12 = (bf16[128,3072]{1,0:T(8,128)(2,1)}, bf16[128,3072]{1,0:T(8,128)(2,1)}, u32[]{:S(2)}, u32[]{:S(2)}) collective-permute-start(bf16[128,3072]{1,0:T(8,128)(2,1)} %collective-permute-done.11), channel_id=1, source_target_pairs={{8,12},{9,13},{10,14},{11,15},{24,28},{25,29},{26,30},{27,31}} | collective-permute-start | bytes 2359304 | tf_op jit(solution)/shard_map/ppermute | solution.py:21
  128.5 2.4 copy-start.20
  128.8 3.3 copy-start.12
  157.6 25.6 %copy-start = (bf16[512,3072]{1,0:T(8,128)(2,1)}, bf16[512,3072]{1,0:T(8,128)(2,1)S(1)}, u32[]{:S(2)}) copy-start(bf16[512,3072]{1,0:T(8,128)(2,1)S(1)} %convolution_convert_fusion.2) | copy-start | bytes 9437188
  157.6 2.5 copy-start.18
  158.0 26.8 %collective-permute-start.37 = (bf16[512,768]{1,0:T(8,128)(2,1)S(1)}, bf16[512,768]{1,0:T(8,128)(2,1)S(1)}, u32[]{:S(2)}, u32[]{:S(2)}) collective-permute-start(bf16[512,768]{1,0:T(8,128)(2,1)S(1)} %get-tuple-element.29), channel_id=1, source_target_pairs={{0,2},{1,3},{2,0},{3,1},{4,6},{5,7},{6,4},{7,5},{8,10},{9,11},{10,... | collective-permute-start | bytes 2359304 | tf_op jit(solution)/shard_map/ppermute | solution.py:78
  159.1 26.9 %collective-permute-start.38 = (bf16[512,768]{1,0:T(8,128)(2,1)S(1)}, bf16[512,768]{1,0:T(8,128)(2,1)S(1)}, u32[]{:S(2)}, u32[]{:S(2)}) collective-permute-start(bf16[512,768]{1,0:T(8,128)(2,1)S(1)} %get-tuple-element.28), channel_id=1, source_target_pairs={{0,1},{1,0},{2,3},{3,2},{4,5},{5,4},{6,7},{7,6},{8,9},{9,8},{10,11... | collective-permute-start | bytes 2359304 | tf_op jit(solution)/shard_map/ppermute | solution.py:78
  160.2 47.8 %collective-permute-start.22 = (bf16[256,3072]{1,0:T(8,128)(2,1)S(1)}, bf16[256,3072]{1,0:T(8,128)(2,1)S(1)}, u32[]{:S(2)}, u32[]{:S(2)}) collective-permute-start(bf16[256,3072]{1,0:T(8,128)(2,1)S(1)} %copy-done.18), channel_id=1, source_target_pairs={{0,16},{16,0},{1,17},{17,1},{2,18},{18,2},{3,19},{19,3},{4,20},{20... | collective-permute-start | bytes 4718600 | tf_op jit(solution)/shard_map/ppermute | solution.py:54
  161.3 19.8 %collective-permute-start.15 = (bf16[128,3072]{1,0:T(8,128)(2,1)S(1)}, bf16[128,3072]{1,0:T(8,128)(2,1)S(1)}, u32[]{:S(2)}, u32[]{:S(2)}) collective-permute-start(bf16[128,3072]{1,0:T(8,128)(2,1)S(1)} %get-tuple-element.34), channel_id=1, source_target_pairs={{0,4},{1,5},{2,6},{3,7},{16,20},{17,21},{18,22},{19,23}} | collective-permute-start | bytes 2359304 | tf_op jit(solution)/shard_map/ppermute | solution.py:45
  164.6 18.1 %collective-permute-start.18 = (bf16[128,3072]{1,0:T(8,128)(2,1)S(1)}, bf16[128,3072]{1,0:T(8,128)(2,1)S(1)}, u32[]{:S(2)}, u32[]{:S(2)}) collective-permute-start(bf16[128,3072]{1,0:T(8,128)(2,1)S(1)} %get-tuple-element.35), channel_id=1, source_target_pairs={{12,8},{13,9},{14,10},{15,11},{28,24},{29,25},{30,26},{31,27}} | collective-permute-start | bytes 2359304 | tf_op jit(solution)/shard_map/ppermute | solution.py:46
  165.5 2.5 copy-start.16
  181.1 19.8 %collective-permute-start.39 = (bf16[512,768]{1,0:T(8,128)(2,1)S(1)}, bf16[512,768]{1,0:T(8,128)(2,1)S(1)}, u32[]{:S(2)}, u32[]{:S(2)}) collective-permute-start(bf16[512,768]{1,0:T(8,128)(2,1)S(1)} %get-tuple-element.27), channel_id=1, source_target_pairs={{0,3},{1,2},{2,1},{3,0},{4,7},{5,6},{6,5},{7,4},{8,11},{9,10},{10,... | collective-permute-start | bytes 2359304 | tf_op jit(solution)/shard_map/ppermute | solution.py:78
  182.7 70.5 %collective-permute-start.40 = (bf16[384,3072]{1,0:T(8,128)(2,1)S(1)}, bf16[384,3072]{1,0:T(8,128)(2,1)S(1)}, u32[]{:S(2)}, u32[]{:S(2)}) collective-permute-start(bf16[384,3072]{1,0:T(8,128)(2,1)S(1)} %pad_maximum_fusion.4), channel_id=1, source_target_pairs={{0,2},{1,3},{2,0},{3,1},{4,6},{5,7},{6,4},{7,5},{8,10},{9,11},{10,... | collective-permute-start | bytes 7077896 | tf_op jit(solution)/shard_map/ppermute | solution.py:64
  184.8 44.9 %collective-permute-start.21 = (bf16[256,3072]{1,0:T(8,128)(2,1)}, bf16[256,3072]{1,0:T(8,128)(2,1)}, u32[]{:S(2)}, u32[]{:S(2)}) collective-permute-start(bf16[256,3072]{1,0:T(8,128)(2,1)} %convolution_convert_fusion.5), channel_id=1, source_target_pairs={{0,16},{16,0},{1,17},{17,1},{2,18},{18,2},{3,19},{19,3},{4,20},{20... | collective-permute-start | bytes 4718600 | tf_op jit(solution)/shard_map/ppermute | solution.py:54
  186.0 152.5 %collective-permute-start.30 = (bf16[1024,3072]{1,0:T(8,128)(2,1)}, bf16[1024,3072]{1,0:T(8,128)(2,1)S(1)}, u32[]{:S(2)}, u32[]{:S(2)}) collective-permute-start(bf16[1024,3072]{1,0:T(8,128)(2,1)} %pad_maximum_fusion), channel_id=1, source_target_pairs={{0,1},{1,0},{2,3},{3,2},{4,5},{5,4},{6,7},{7,6},{8,9},{9,8},{10,11... | collective-permute-start | bytes 18874376 | tf_op jit(solution)/shard_map/ppermute | solution.py:141
  200.9 51.2 %collective-permute-start.16 = (bf16[128,3072]{1,0:T(8,128)(2,1)}, bf16[128,3072]{1,0:T(8,128)(2,1)}, u32[]{:S(2)}, u32[]{:S(2)}) collective-permute-start(bf16[128,3072]{1,0:T(8,128)(2,1)} %get-tuple-element.32), channel_id=1, source_target_pairs={{0,4},{4,8},{1,5},{5,9},{2,6},{6,10},{3,7},{7,11},{16,20},{20,24},... | collective-permute-start | bytes 2359304 | tf_op jit(solution)/shard_map/ppermute | solution.py:45
  222.4 8.8 %copy-start.3 = (bf16[256,3072]{1,0:T(8,128)(2,1)S(1)}, bf16[256,3072]{1,0:T(8,128)(2,1)}, u32[]{:S(2)}) copy-start(bf16[256,3072]{1,0:T(8,128)(2,1)} %copy-done.2) | copy-start | bytes 4718596
  222.4 8.8 %copy-start.5 = (bf16[256,3072]{1,0:T(8,128)(2,1)S(1)}, bf16[256,3072]{1,0:T(8,128)(2,1)}, u32[]{:S(2)}) copy-start(bf16[256,3072]{1,0:T(8,128)(2,1)} %copy-done.4) | copy-start | bytes 4718596
  223.7 24.5 %collective-permute-start.23 = (bf16[128,3072]{1,0:T(8,128)(2,1)}, bf16[128,3072]{1,0:T(8,128)(2,1)}, u32[]{:S(2)}, u32[]{:S(2)}) collective-permute-start(bf16[128,3072]{1,0:T(8,128)(2,1)} %get-tuple-element.56), channel_id=1, source_target_pairs={{0,4},{1,5},{2,6},{3,7},{16,20},{17,21},{18,22},{19,23}} | collective-permute-start | bytes 2359304 | tf_op jit(solution)/shard_map/ppermute | solution.py:45
  229.7 19.5 %collective-permute-start.26 = (bf16[128,3072]{1,0:T(8,128)(2,1)}, bf16[128,3072]{1,0:T(8,128)(2,1)}, u32[]{:S(2)}, u32[]{:S(2)}) collective-permute-start(bf16[128,3072]{1,0:T(8,128)(2,1)} %get-tuple-element.57), channel_id=1, source_target_pairs={{12,8},{13,9},{14,10},{15,11},{28,24},{29,25},{30,26},{31,27}} | collective-permute-start | bytes 2359304 | tf_op jit(solution)/shard_map/ppermute | solution.py:46
  246.6 3.6 copy-start.17
  248.3 4.9 %collective-permute-start.19 = (bf16[128,3072]{1,0:T(8,128)(2,1)}, bf16[128,3072]{1,0:T(8,128)(2,1)S(1)}, u32[]{:S(2)}, u32[]{:S(2)}) collective-permute-start(bf16[128,3072]{1,0:T(8,128)(2,1)} %get-tuple-element.33), channel_id=1, source_target_pairs={{8,4},{12,8},{9,5},{13,9},{10,6},{14,10},{11,7},{15,11},{24,20},{2... | collective-permute-start | bytes 2359304 | tf_op jit(solution)/shard_map/ppermute | solution.py:46
  249.0 4.7 %copy-start.9 = (bf16[128,3072]{1,0:T(8,128)(2,1)S(1)}, bf16[128,3072]{1,0:T(8,128)(2,1)}, u32[]{:S(2)}) copy-start(bf16[128,3072]{1,0:T(8,128)(2,1)} %get-tuple-element.36) | copy-start | bytes 2359300
  249.0 4.7 %copy-start.10 = (bf16[128,3072]{1,0:T(8,128)(2,1)S(1)}, bf16[128,3072]{1,0:T(8,128)(2,1)}, u32[]{:S(2)}) copy-start(bf16[128,3072]{1,0:T(8,128)(2,1)} %get-tuple-element.40) | copy-start | bytes 2359300
  249.2 12.1 %collective-permute-start.31 = (bf16[256,768]{1,0:T(8,128)(2,1)S(1)}, bf16[256,768]{1,0:T(8,128)(2,1)S(1)}, u32[]{:S(2)}, u32[]{:S(2)}) collective-permute-start(bf16[256,768]{1,0:T(8,128)(2,1)S(1)} %get-tuple-element.50), channel_id=1, source_target_pairs={{0,2},{1,3},{2,0},{3,1},{4,6},{5,7},{6,4},{7,5},{8,10},{9,11},{10,... | collective-permute-start | bytes 1179656 | tf_op jit(solution)/shard_map/ppermute | solution.py:78
  252.1 17.6 %collective-permute-start.32 = (bf16[256,768]{1,0:T(8,128)(2,1)S(1)}, bf16[256,768]{1,0:T(8,128)(2,1)S(1)}, u32[]{:S(2)}, u32[]{:S(2)}) collective-permute-start(bf16[256,768]{1,0:T(8,128)(2,1)S(1)} %get-tuple-element.46), channel_id=1, source_target_pairs={{0,2},{1,3},{2,0},{3,1},{4,6},{5,7},{6,4},{7,5},{8,10},{9,11},{10,... | collective-permute-start | bytes 1179656 | tf_op jit(solution)/shard_map/ppermute | solution.py:78
  253.2 16.5 %collective-permute-start.33 = (bf16[256,768]{1,0:T(8,128)(2,1)S(1)}, bf16[256,768]{1,0:T(8,128)(2,1)S(1)}, u32[]{:S(2)}, u32[]{:S(2)}) collective-permute-start(bf16[256,768]{1,0:T(8,128)(2,1)S(1)} %get-tuple-element.49), channel_id=1, source_target_pairs={{0,1},{1,0},{2,3},{3,2},{4,5},{5,4},{6,7},{7,6},{8,9},{9,8},{10,11... | collective-permute-start | bytes 1179656 | tf_op jit(solution)/shard_map/ppermute | solution.py:78
  253.2 23.0 %collective-permute-start.34 = (bf16[256,768]{1,0:T(8,128)(2,1)S(1)}, bf16[256,768]{1,0:T(8,128)(2,1)S(1)}, u32[]{:S(2)}, u32[]{:S(2)}) collective-permute-start(bf16[256,768]{1,0:T(8,128)(2,1)S(1)} %get-tuple-element.45), channel_id=1, source_target_pairs={{0,1},{1,0},{2,3},{3,2},{4,5},{5,4},{6,7},{7,6},{8,9},{9,8},{10,11... | collective-permute-start | bytes 1179656 | tf_op jit(solution)/shard_map/ppermute | solution.py:78
  253.7 23.5 %copy-start.1 = (bf16[512,3072]{1,0:T(8,128)(2,1)S(1)}, bf16[512,3072]{1,0:T(8,128)(2,1)}, u32[]{:S(2)}) copy-start(bf16[512,3072]{1,0:T(8,128)(2,1)} %copy-done) | copy-start | bytes 9437188
  261.3 17.6 %collective-permute-start.35 = (bf16[256,768]{1,0:T(8,128)(2,1)S(1)}, bf16[256,768]{1,0:T(8,128)(2,1)S(1)}, u32[]{:S(2)}, u32[]{:S(2)}) collective-permute-start(bf16[256,768]{1,0:T(8,128)(2,1)S(1)} %get-tuple-element.48), channel_id=1, source_target_pairs={{0,3},{1,2},{2,1},{3,0},{4,7},{5,6},{6,5},{7,4},{8,11},{9,10},{10,... | collective-permute-start | bytes 1179656 | tf_op jit(solution)/shard_map/ppermute | solution.py:78
  269.7 86.6 %collective-permute-start.41 = (bf16[1024,3072]{1,0:T(8,128)(2,1)S(1)}, bf16[1024,3072]{1,0:T(8,128)(2,1)}, u32[]{:S(2)}, u32[]{:S(2)}) collective-permute-start(bf16[1024,3072]{1,0:T(8,128)(2,1)S(1)} %pad_maximum_fusion.1), channel_id=1, source_target_pairs={{0,1},{1,0},{2,3},{3,2},{4,5},{5,4},{6,7},{7,6},{8,9},{9,8},{10,11... | collective-permute-start | bytes 18874376 | tf_op jit(solution)/shard_map/ppermute | solution.py:141
  269.7 28.1 %collective-permute-start.24 = (bf16[128,3072]{1,0:T(8,128)(2,1)S(1)}, bf16[128,3072]{1,0:T(8,128)(2,1)S(1)}, u32[]{:S(2)}, u32[]{:S(2)}) collective-permute-start(bf16[128,3072]{1,0:T(8,128)(2,1)S(1)} %get-tuple-element.54), channel_id=1, source_target_pairs={{0,4},{4,8},{1,5},{5,9},{2,6},{6,10},{3,7},{7,11},{16,20},{20,24},... | collective-permute-start | bytes 2359304 | tf_op jit(solution)/shard_map/ppermute | solution.py:45
  276.2 22.9 %collective-permute-start.27 = (bf16[128,3072]{1,0:T(8,128)(2,1)S(1)}, bf16[128,3072]{1,0:T(8,128)(2,1)S(1)}, u32[]{:S(2)}, u32[]{:S(2)}) collective-permute-start(bf16[128,3072]{1,0:T(8,128)(2,1)S(1)} %get-tuple-element.55), channel_id=1, source_target_pairs={{8,4},{12,8},{9,5},{13,9},{10,6},{14,10},{11,7},{15,11},{24,20},{2... | collective-permute-start | bytes 2359304 | tf_op jit(solution)/shard_map/ppermute | solution.py:46
  278.9 11.3 %collective-permute-start.36 = (bf16[256,768]{1,0:T(8,128)(2,1)S(1)}, bf16[256,768]{1,0:T(8,128)(2,1)S(1)}, u32[]{:S(2)}, u32[]{:S(2)}) collective-permute-start(bf16[256,768]{1,0:T(8,128)(2,1)S(1)} %get-tuple-element.44), channel_id=1, source_target_pairs={{0,3},{1,2},{2,1},{3,0},{4,7},{5,6},{6,5},{7,4},{8,11},{9,10},{10,... | collective-permute-start | bytes 1179656 | tf_op jit(solution)/shard_map/ppermute | solution.py:78
  290.3 25.3 %collective-permute-start.17 = (bf16[128,3072]{1,0:T(8,128)(2,1)S(1)}, bf16[128,3072]{1,0:T(8,128)(2,1)S(1)}, u32[]{:S(2)}, u32[]{:S(2)}) collective-permute-start(bf16[128,3072]{1,0:T(8,128)(2,1)S(1)} %get-tuple-element.30), channel_id=1, source_target_pairs={{0,4},{4,8},{8,12},{1,5},{5,9},{9,13},{2,6},{6,10},{10,14},{3,7},{... | collective-permute-start | bytes 2359304 | tf_op jit(solution)/shard_map/ppermute | solution.py:45
  297.8 20.6 %copy-start.24 = (bf16[2048,768]{1,0:T(8,128)(2,1)}, bf16[2048,768]{1,0:T(8,128)(2,1)S(1)}, u32[]{:S(2)}) copy-start(bf16[2048,768]{1,0:T(8,128)(2,1)S(1)} %constant_dynamic-update-slice_fusion.7) | copy-start | bytes 9437188
  297.8 22.5 %collective-permute-start.20 = (bf16[128,3072]{1,0:T(8,128)(2,1)S(1)}, bf16[128,3072]{1,0:T(8,128)(2,1)S(1)}, u32[]{:S(2)}, u32[]{:S(2)}) collective-permute-start(bf16[128,3072]{1,0:T(8,128)(2,1)S(1)} %get-tuple-element.31), channel_id=1, source_target_pairs={{4,0},{8,4},{12,8},{5,1},{9,5},{13,9},{6,2},{10,6},{14,10},{7,3},{... | collective-permute-start | bytes 2359304 | tf_op jit(solution)/shard_map/ppermute | solution.py:46
  299.7 32.4 %collective-permute-start.25 = (bf16[128,3072]{1,0:T(8,128)(2,1)S(1)}, bf16[128,3072]{1,0:T(8,128)(2,1)S(1)}, u32[]{:S(2)}, u32[]{:S(2)}) collective-permute-start(bf16[128,3072]{1,0:T(8,128)(2,1)S(1)} %get-tuple-element.52), channel_id=1, source_target_pairs={{0,4},{4,8},{8,12},{1,5},{5,9},{9,13},{2,6},{6,10},{10,14},{3,7},{... | collective-permute-start | bytes 2359304 | tf_op jit(solution)/shard_map/ppermute | solution.py:45
  315.5 21.7 %collective-permute-start.28 = (bf16[128,3072]{1,0:T(8,128)(2,1)S(1)}, bf16[128,3072]{1,0:T(8,128)(2,1)S(1)}, u32[]{:S(2)}, u32[]{:S(2)}) collective-permute-start(bf16[128,3072]{1,0:T(8,128)(2,1)S(1)} %get-tuple-element.53), channel_id=1, source_target_pairs={{4,0},{8,4},{12,8},{5,1},{9,5},{13,9},{6,2},{10,6},{14,10},{7,3},{... | collective-permute-start | bytes 2359304 | tf_op jit(solution)/shard_map/ppermute | solution.py:46
  338.5 3.2 copy-start.25
  356.3 6.1 %copy-start.14 = (bf16[2048,768]{1,0:T(8,128)(2,1)S(1)}, bf16[2048,768]{1,0:T(8,128)(2,1)}, u32[]{:S(2)}) copy-start(bf16[2048,768]{1,0:T(8,128)(2,1)} %pad_maximum_fusion.3) | copy-start | bytes 9437188
  (4 other events, 6.1 us)

commit v3 on v2

v3 whole, which is shorter than its diff:
```python
import jax
import jax.numpy as jnp
from jax import lax
from jax.sharding import PartitionSpec as P


def gelu_tanh(value):
    return jax.nn.gelu(value, approximate=True)


def dot(a, b, ca, cb):
    return lax.dot_general(
        a, b, (((ca,), (cb,)), ((), ())), preferred_element_type=jnp.float32
    )


def line_gather(block, n, beside=()):
    right = left = block
    rights, lefts = [block], [block]
    me = lax.axis_index("col")
    slot = lambda k: jnp.where(me + k < n, lefts[k], rights[n - k])
    done = []
    for step in range(1, n):
        other = beside[step - 1](slot) if step <= len(beside) else None
        right = lax.ppermute(right, "col", [(c, c + 1) for c in range(step - 1, n - 1)])
        left = lax.ppermute(left, "col", [(c, c - 1) for c in range(1, n - step + 1)])
        if other is not None:
            right, left, other = lax.optimization_barrier((right, left, other))
        done.append(other)
        rights.append(right)
        lefts.append(left)
    return [block] + [slot(k) for k in range(1, n)], done


def line_reduce(parts, n, beside=None):
    if n == 1:
        return parts[0]
    right = left = None
    for step in range(1, n):
        to_right, to_left = parts[n - step], parts[step]
        if right is not None:
            to_right = (to_right.astype(jnp.float32) + right.astype(jnp.float32)).astype(
                jnp.bfloat16
            )
            to_left = (to_left.astype(jnp.float32) + left.astype(jnp.float32)).astype(
                jnp.bfloat16
            )
        right = lax.ppermute(to_right, "col", [(c, c + 1) for c in range(step)])
        left = lax.ppermute(to_left, "col", [(c, c - 1) for c in range(n - step, n)])
        if step == 1 and beside is not None:
            right, left, beside = lax.optimization_barrier((right, left, beside))
    total = parts[0].astype(jnp.float32) + right.astype(jnp.float32) + left.astype(jnp.float32)
    total = total.astype(jnp.bfloat16)
    return total if beside is None else (total, beside)


def row_sum(part, n):
    total = part.astype(jnp.float32)
    for step in range(1, n):
        other = lax.ppermute(part, "row", [(r, (r + step) % n) for r in range(n)])
        total = total + other.astype(jnp.float32)
    return total


def depth_masks(n):
    masks, bit = [0], n // 2
    while bit > 1:
        masks = masks + [m ^ bit for m in masks]
        bit //= 2
    return masks


def depth_high(mine, n):
    blocks, bit = [mine], n // 2
    while bit > 1:
        blocks = blocks + [
            lax.ppermute(b, "depth", [(d, d ^ bit) for d in range(n)]) for b in blocks
        ]
        bit //= 2
    return blocks


def high_columns(mine, masks, n):
    me = lax.axis_index("depth")
    width = 2 * mine.shape[1] // n
    out = []
    for m in masks:
        piece = lax.dynamic_slice_in_dim(mine, ((me ^ m) // 2) * width, width, axis=1)
        if m:
            piece = lax.ppermute(piece, "depth", [(d, d ^ m) for d in range(n)])
        out.append(piece)
    return out


def core_exchange(high, n):
    core = lax.axis_index("depth") % 2
    width = high.shape[1] // 2
    mine = lax.dynamic_slice_in_dim(high, core * width, width, axis=1)
    other = lax.dynamic_slice_in_dim(high, (1 - core) * width, width, axis=1)
    other = lax.ppermute(other, "depth", [(d, d ^ 1) for d in range(n)])
    first = core == 0
    return cat(jnp.where(first, mine, other), jnp.where(first, other, mine))


def core_gather(high, n):
    pairs = [[d, d + 1] for d in range(0, n, 2)]
    return lax.all_gather(high, "depth", axis=0, tiled=True, axis_index_groups=pairs)


def cat(*blocks):
    return jnp.concatenate(blocks, axis=0)


def body(n_row, n_col, n_depth, tokens, w_in, w_out, grad_out):
    rows = tokens.shape[0]
    half = n_col // 2
    tie = lax.optimization_barrier

    def fold(slots):
        return cat(*slots[0::2]), cat(*slots[1::2])

    def unfold(even, odd):
        slots = [None] * n_col
        slots[0::2] = [even[k * rows : (k + 1) * rows] for k in range(half)]
        slots[1::2] = [odd[k * rows : (k + 1) * rows] for k in range(half)]
        return slots

    def own_part(part):
        return part.astype(jnp.bfloat16)

    step_high = lambda block: depth_high(block, n_depth)
    masks = depth_masks(n_depth)

    tok_slots, tok_high = line_gather(
        tokens,
        n_col,
        [lambda slot: step_high(tokens), lambda slot: step_high(grad_out), lambda slot: step_high(slot(2))],
    )
    tok_own, grad_own, tok_two = tok_high
    tok_even, tok_odd = fold(tok_slots)
    pre_even = row_sum(own_part(dot(tok_even, w_in, 1, 0)), n_row)
    grad_out, tok_odd = tie((grad_out, tok_odd))
    tok_odd_high = step_high(tok_odd)
    part_odd = own_part(dot(tok_odd, w_in, 1, 0))
    pre_odd = row_sum(part_odd, n_row)
    grad_slots, grad_high = line_gather(
        grad_out, n_col, [lambda slot: None, lambda slot: None, lambda slot: step_high(slot(2))]
    )
    grad_two = grad_high[2]
    act_even, pull_even = jax.vjp(gelu_tanh, pre_even)
    act_odd, pull_odd = jax.vjp(gelu_tanh, pre_odd)
    act_even, act_odd = own_part(act_even), own_part(act_odd)
    grad_even, grad_odd = fold(grad_slots)
    grad_odd_high = step_high(grad_odd)

    out_even = own_part(dot(act_even, w_out, 1, 0))
    grad_even_in, out_even = tie((grad_even, out_even))
    gact_even = row_sum(own_part(dot(grad_even_in, w_out, 1, 1)), n_row)
    out_odd = own_part(dot(act_odd, w_out, 1, 0))
    grad_odd_in, out_odd = tie((grad_odd, out_odd))
    gact_odd = row_sum(own_part(dot(grad_odd_in, w_out, 1, 1)), n_row)
    output = line_reduce(unfold(out_even, out_odd), n_col)

    gpre_even = own_part(pull_even(gact_even)[0])
    gpre_odd = own_part(pull_odd(gact_odd)[0])
    gtok_even = own_part(dot(gpre_even, w_in, 1, 1))
    gtok_odd = own_part(dot(gpre_odd, w_in, 1, 1))

    def high_rows(own, two, odd_high, even, odd):
        blocks = [even, odd]
        for k in range(1, len(masks)):
            blocks += [own[k], two[k], odd_high[k]]
        return cat(*blocks)

    all_tok = core_gather(high_rows(tok_own, tok_two, tok_odd_high, tok_even, tok_odd), n_depth)
    all_grad = core_gather(
        high_rows(grad_own, grad_two, grad_odd_high, grad_even, grad_odd), n_depth
    )
    act_high = high_columns(cat(act_even, act_odd), masks, n_depth)
    all_act = core_exchange(cat(*act_high), n_depth)
    gpre_high = zip(
        high_columns(gpre_even, masks, n_depth), high_columns(gpre_odd, masks, n_depth)
    )
    all_gpre = core_exchange(cat(*[b for pair in gpre_high for b in pair]), n_depth)
    grad_w_out = own_part(dot(all_act, all_grad, 0, 0))
    grad_tokens, grad_w_out = line_reduce(unfold(gtok_even, gtok_odd), n_col, grad_w_out)
    grad_w_in = own_part(dot(all_tok, all_gpre, 0, 0))
    return output, grad_tokens, grad_w_in, grad_w_out


def solution(mesh):
    placed = (
        P(("col", "depth"), "row"),
        P("row", "col"),
        P("col", "row"),
        P(("col", "depth"), "row"),
    )
    sizes = tuple(mesh.shape[a] for a in ("row", "col", "depth"))
    return jax.shard_map(
        lambda *args: body(*sizes, *args),
        mesh=mesh,
        in_specs=placed,
        out_specs=(
            P(("col", "depth"), "row"),
            P(("col", "depth"), "row"),
            P("row", ("col", "depth")),
            P(("col", "depth"), "row"),
        ),
        check_vma=False,
    )
```

time: 384 us -> 431 us (1.12)
  waiting for transfers between devices: 134 us -> 165 us
  between operations: 1.74 us -> 14.9 us
  matrix products: 103 us -> 116 us
  starting transfers between devices: 76.5 us -> 63.5 us
  other arithmetic: 36.1 us -> 46.1 us
  local copies, waits for them, and re-layouts: 26.1 us -> 20.9 us
    ppermute x3 -> x6, waiting for transfers between devices: 0.01 us -> 58.3 us  [depth_high(): lax.ppermute(b, 'depth', [(d, d ^ bit) for d in range(n)])]
    ppermute x11 -> x5, waiting for transfers between devices: 40.2 us -> 3.85 us  [the longest x3 3.85 us: high_columns(): piece = lax.ppermute(piece, 'depth', [(d, d ^ m) for d in range(n)])]
    ppermute x4, waiting for transfers between devices: 7.15 us -> 32.5 us  [row_sum(): other = lax.ppermute(part, 'row', [(r, (r + step) % n) for r in range(n)])]
    ppermute x6, waiting for transfers between devices: 29.8 us -> 10.2 us  [line_reduce(): right = lax.ppermute(to_right, 'col', [(c, c + 1) for c in range(step)])]
    ppermute x6, waiting for transfers between devices: 0.02 us -> 13.7 us  [line_gather(): lax.ppermute(right, 'col', [(c, c + 1) for c in range(step - 1, n - 1)])]
    dot_general x9 -> x10, matrix products: 103 us -> 116 us  [dot(): lax.dot_general(a, b, (((ca,), (cb,)), ((), ())), preferred_element_type=...]
    ppermute x6, waiting for transfers between devices: 49.9 us -> 43.1 us  [line_gather(): lax.ppermute(left, 'col', [(c, c - 1) for c in range(1, n - step + 1)])]
    concatenate x4 -> x2, local copies, waits for them, and re-layouts: 10.5 us -> 3.92 us  [cat(): return jnp.concatenate(blocks, axis=0)]
  transfers between devices with their start and end apart: 42 -> 41, of which waited for: 17 -> 18; matrix products, arithmetic and copies ran while one was open for 34% -> 40% of each run, Pallas kernels for 0% -> 0%
where the time goes in v3:
time: 431 us; the launch traced here: 426 us
  waiting for transfers between devices  165 us (38%)
  matrix products  116 us (27%)
  starting transfers between devices  63.5 us (15%)
  other arithmetic  46.1 us (11%)
  local copies, waits for them, and re-layouts  20.9 us (5%)
  between operations  14.9 us (3%)
    dot_general x10, matrix products, dot(): lax.dot_general(a, b, (((ca,), (cb,)), ((), ())), preferred_element_type=...  116 us
    ppermute x6, waiting for transfers between devices, depth_high(): lax.ppermute(b, 'depth', [(d, d ^ bit) for d in range(n)])  58.3 us
    ppermute x6, waiting for transfers between devices, line_gather(): lax.ppermute(left, 'col', [(c, c - 1) for c in range(1, n - step + 1)])  43.1 us
    ppermute x4, waiting for transfers between devices, row_sum(): other = lax.ppermute(part, 'row', [(r, (r + step) % n) for r in range(n)])  32.5 us
    ppermute x6, starting transfers between devices, line_reduce(): right = lax.ppermute(to_right, 'col', [(c, c + 1) for c in range(step)])  23.7 us
    ppermute x6, waiting for transfers between devices, line_gather(): lax.ppermute(right, 'col', [(c, c + 1) for c in range(step - 1, n - 1)])  13.7 us
    unnamed x57, local copies, waits for them, and re-layouts  13.2 us
    ppermute x6, starting transfers between devices, line_gather(): lax.ppermute(right, 'col', [(c, c + 1) for c in range(step - 1, n - 1)])  12.4 us
  transfers between devices with their start and end apart: 41, of which 18 were waited for; matrix products, arithmetic and copies ran while one was open for 40% of the time, Pallas kernels for 0%

profile of v3, /device:TPU:0, one launch (start us, length us, event | category | flops | bytes accessed | tf_op | source)
XLA Modules:
  0.0 426.4 jit_solution(8302370150154284225)
XLA Ops:
  7.2 5.0 %collective-permute-start = (bf16[128,3072]{1,0:T(8,128)(2,1)}, bf16[128,3072]{1,0:T(8,128)(2,1)S(1)}, u32[]{:S(2)}, u32[]{:S(2)}) collective-permute-start(bf16[128,3072]{1,0:T(8,128)(2,1)} %param.4), channel_id=1, source_target_pairs={{0,4},{4,8},{8,12},{1,5},{5,9},{9,13},{2,6},{6,10},{10,14},{3,7},{... | collective-permute-start | bytes 2359304 | tf_op jit(solution)/shard_map/ppermute | solution.py:25
  12.2 1.3 collective-permute-start.1
  13.5 1.6 collective-permute-start.2
  15.6 13.7 %collective-permute-done = bf16[128,3072]{1,0:T(8,128)(2,1)S(1)} collective-permute-done((bf16[128,3072]{1,0:T(8,128)(2,1)}, bf16[128,3072]{1,0:T(8,128)(2,1)S(1)}, u32[]{:S(2)}, u32[]{:S(2)}) %collective-permute-start) | collective-permute-done | bytes 786464 | tf_op jit(solution)/shard_map/ppermute | solution.py:25
  29.2 4.1 collective-permute-done.1
  35.8 1.3 collective-permute-start.4
  37.1 2.1 constant_dynamic-update-slice_fusion.12
  39.2 10.4 %collective-permute-done.5 = bf16[128,3072]{1,0:T(8,128)(2,1)S(1)} collective-permute-done((bf16[128,3072]{1,0:T(8,128)(2,1)}, bf16[128,3072]{1,0:T(8,128)(2,1)S(1)}, u32[]{:S(2)}, u32[]{:S(2)}) %collective-permute-start.5) | collective-permute-done | bytes 786464 | tf_op jit(solution)/shard_map/ppermute | solution.py:77
  49.6 7.7 %collective-permute-done.4 = bf16[128,3072]{1,0:T(8,128)(2,1)} collective-permute-done((bf16[128,3072]{1,0:T(8,128)(2,1)S(1)}, bf16[128,3072]{1,0:T(8,128)(2,1)}, u32[]{:S(2)}, u32[]{:S(2)}) %collective-permute-start.4) | collective-permute-done | bytes 786464 | tf_op jit(solution)/shard_map/ppermute | solution.py:26
  57.3 2.5 constant_dynamic-update-slice_fusion.11
  59.9 1.5 collective-permute-start.8
  62.1 1.3 collective-permute-start.7
  63.4 11.9 %collective-permute-done.8 = bf16[128,3072]{1,0:T(8,128)(2,1)} collective-permute-done((bf16[128,3072]{1,0:T(8,128)(2,1)}, bf16[128,3072]{1,0:T(8,128)(2,1)}, u32[]{:S(2)}, u32[]{:S(2)}) %collective-permute-start.8) | collective-permute-done | bytes 786464 | tf_op jit(solution)/shard_map/ppermute | solution.py:77
  75.3 3.8 collective-permute-done.7
  80.6 1.3 collective-permute-start.9
  81.9 4.6 %collective-permute-start.11 = (bf16[128,3072]{1,0:T(8,128)(2,1)S(1)}, bf16[128,3072]{1,0:T(8,128)(2,1)S(1)}, u32[]{:S(2)}, u32[]{:S(2)}) collective-permute-start(bf16[128,3072]{1,0:T(8,128)(2,1)S(1)} %copy-done.13), channel_id=1, source_target_pairs={{0,4},{4,8},{8,12},{1,5},{5,9},{9,13},{2,6},{6,10},{10,14},{3,7},{... | collective-permute-start | bytes 2359304 | tf_op jit(solution)/shard_map/ppermute | solution.py:25
  86.5 11.8 %collective-permute-done.9 = bf16[128,3072]{1,0:T(8,128)(2,1)S(1)} collective-permute-done((bf16[128,3072]{1,0:T(8,128)(2,1)S(1)}, bf16[128,3072]{1,0:T(8,128)(2,1)S(1)}, u32[]{:S(2)}, u32[]{:S(2)}) %collective-permute-start.9) | collective-permute-done | bytes 786464 | tf_op jit(solution)/shard_map/ppermute | solution.py:26
  101.2 12.6 %collective-permute-done.10 = bf16[128,3072]{1,0:T(8,128)(2,1)S(1)} collective-permute-done((bf16[128,3072]{1,0:T(8,128)(2,1)S(1)}, bf16[128,3072]{1,0:T(8,128)(2,1)S(1)}, u32[]{:S(2)}, u32[]{:S(2)}) %collective-permute-start.10) | collective-permute-done | bytes 786464 | tf_op jit(solution)/shard_map/ppermute | solution.py:26
  115.7 1.3 collective-permute-start.15
  117.0 10.0 %collective-permute-done.16 = bf16[128,3072]{1,0:T(8,128)(2,1)S(1)} collective-permute-done((bf16[128,3072]{1,0:T(8,128)(2,1)S(1)}, bf16[128,3072]{1,0:T(8,128)(2,1)S(1)}, u32[]{:S(2)}, u32[]{:S(2)}) %collective-permute-start.16) | collective-permute-done | bytes 786464 | tf_op jit(solution)/shard_map/ppermute | solution.py:77
  127.0 3.1 collective-permute-done.15
  133.5 1.5 collective-permute-start.30
  137.0 25.0 %collective-permute-done.30 = bf16[256,3072]{1,0:T(8,128)(2,1)S(1)} collective-permute-done((bf16[256,3072]{1,0:T(8,128)(2,1)S(1)}, bf16[256,3072]{1,0:T(8,128)(2,1)S(1)}, u32[]{:S(2)}, u32[]{:S(2)}) %collective-permute-start.30) | collective-permute-done | bytes 1572896 | tf_op jit(solution)/shard_map/ppermute | solution.py:77
  163.5 11.3 %convolution_convert_fusion.9 = bf16[256,3072]{1,0:T(8,128)(2,1)S(1)} fusion(bf16[3072,3072]{1,0:T(8,128)(2,1)} %param.5, bf16[128,3072]{1,0:T(8,128)(2,1)} %get-tuple-element.47, bf16[128,3072]{1,0:T(8,128)(2,1)} %param.4), kind=kOutput, calls=%fused_computation.13 | convolution fusion | flops 4835770368 | bytes 22020096 | tf_op jit(solution)/shard_map/dot_general | solution.py:12
  176.1 11.6 %convolution_convert_fusion.7 = bf16[256,3072]{1,0:T(8,128)(2,1)S(1)} fusion(bf16[256,3072]{1,0:T(8,128)(2,1)S(1)} %pad_maximum_fusion.1, bf16[3072,3072]{1,0:T(8,128)(2,1)} %param.5), kind=kOutput, calls=%fused_computation.11 | convolution fusion | flops 4832624640 | bytes 22020096 | tf_op jit(solution)/shard_map/dot_general | solution.py:12
  191.5 2.1 constant_dynamic-update-slice_fusion.8
  193.6 18.6 %collective-permute-done.13 = bf16[256,3072]{1,0:T(8,128)(2,1)S(1)} collective-permute-done((bf16[256,3072]{1,0:T(8,128)(2,1)S(1)}, bf16[256,3072]{1,0:T(8,128)(2,1)S(1)}, u32[]{:S(2)}, u32[]{:S(2)}) %collective-permute-start.13) | collective-permute-done | bytes 1572896 | tf_op jit(solution)/shard_map/ppermute | solution.py:60
  213.5 10.4 %convolution_convert_fusion.8 = bf16[256,3072]{1,0:T(8,128)(2,1)} fusion(bf16[256,3072]{1,0:T(8,128)(2,1)S(1)} %multiply_convert_fusion.1, bf16[3072,3072]{1,0:T(8,128)(2,1)} %param.6), kind=kOutput, calls=%fused_computation.12 | convolution fusion | flops 4832624640 | bytes 22020096 | tf_op jit(solution)/shard_map/dot_general | solution.py:12
  224.0 10.4 %convolution_convert_fusion.5 = bf16[256,3072]{1,0:T(8,128)(2,1)} fusion(bf16[256,3072]{1,0:T(8,128)(2,1)S(1)} %pad_maximum_fusion.2, bf16[3072,3072]{1,0:T(8,128)(2,1)} %param.6), kind=kOutput, calls=%fused_computation.9 | convolution fusion | flops 4832624640 | bytes 22020096 | tf_op jit(solution)/shard_map/dot_general | solution.py:12
  235.5 10.4 %collective-permute-done.17 = bf16[256,3072]{1,0:T(8,128)(2,1)S(1)} collective-permute-done((bf16[256,3072]{1,0:T(8,128)(2,1)S(1)}, bf16[256,3072]{1,0:T(8,128)(2,1)S(1)}, u32[]{:S(2)}, u32[]{:S(2)}) %collective-permute-start.17) | collective-permute-done | bytes 1572896 | tf_op jit(solution)/shard_map/ppermute | solution.py:60
  247.2 1.6 fusion.26
  248.9 2.7 constant_dynamic-update-slice_fusion.7
  251.5 9.8 %convolution_convert_fusion.6 = bf16[256,3072]{1,0:T(8,128)(2,1)S(1)} fusion(bf16[256,3072]{1,0:T(8,128)(2,1)} %copy-done.12, bf16[3072,3072]{1,0:T(8,128)(2,1)} %param.6), kind=kOutput, calls=%fused_computation.10 | convolution fusion | flops 4832624640 | bytes 22020096 | tf_op jit(solution)/shard_map/dot_general | solution.py:12
  261.4 11.8 %convolution_convert_fusion.3 = bf16[256,3072]{1,0:T(8,128)(2,1)S(1)} fusion(bf16[256,3072]{1,0:T(8,128)(2,1)} %copy-done.14, bf16[3072,3072]{1,0:T(8,128)(2,1)} %param.6), kind=kOutput, calls=%fused_computation.7 | convolution fusion | flops 4832624640 | bytes 22020096 | tf_op jit(solution)/shard_map/dot_general | solution.py:12
  273.9 1.6 collective-permute-start.18
  276.3 3.5 collective-permute-done.24
  279.7 4.1 fusion.6
  284.9 1.4 fusion.24
  286.5 1.6 fusion.20
  288.1 3.7 collective-permute-start.19
  291.9 1.7 collective-permute-start.22
  293.6 10.3 %convolution_convert_fusion.4 = bf16[256,3072]{1,0:T(8,128)(2,1)} fusion(bf16[256,3072]{1,0:T(8,128)(2,1)S(1)} %fusion.6, bf16[3072,3072]{1,0:T(8,128)(2,1)} %param.5), kind=kOutput, calls=%fused_computation.8 | convolution fusion | flops 4832624640 | bytes 22020096 | tf_op jit(solution)/shard_map/dot_general | solution.py:12
  303.9 3.9 fusion.13
  307.8 9.2 %convolution_convert_fusion.2 = bf16[256,3072]{1,0:T(8,128)(2,1)S(1)} fusion(bf16[256,3072]{1,0:T(8,128)(2,1)S(1)} %fusion.13, bf16[3072,3072]{1,0:T(8,128)(2,1)} %param.5), kind=kOutput, calls=%fused_computation.6 | convolution fusion | flops 4832624640 | bytes 22020096 | tf_op jit(solution)/shard_map/dot_general | solution.py:12
  317.1 2.4 collective-permute-start.37
  319.6 1.3 fusion.34
  320.9 4.0 collective-permute-start.26
  324.9 1.5 collective-permute-start.27
  326.4 3.1 add_convert_fusion.5
  329.5 2.2 collective-permute-start.20
  331.7 3.8 collective-permute-done.37
  336.8 5.0 %pad_maximum_fusion = bf16[1024,1536]{1,0:T(8,128)(2,1)S(1)} fusion(bf16[256,1536]{1,0:T(8,128)(2,1)S(1)} %collective-permute-done.37, bf16[256,1536]{1,0:T(8,128)(2,1)} %collective-permute-done.36, bf16[256,1536]{1,0:T(8,128)(2,1)S(1)} %get-tuple-element.62, bf16[256,1536]{1,0:T(8,128)(2,1)S(1)} %get-tuple-element.60), kind=kLoop, calls=%fused_computation.39 | loop fusion | flops 12582912 | bytes 6291456 | tf_op jit(solution)/shard_map/concatenate | solution.py:111
  341.8 1.7 copy-done
  344.7 4.3 broadcast_select_fusion.3
  349.0 15.4 %convolution_convert_fusion.1 = bf16[768,3072]{1,0:T(8,128)(2,1)} fusion(bf16[2048,3072]{1,0:T(8,128)(2,1)} %all-gather.3.cloned.1.call-done, bf16[1024,768]{1,0:T(8,128)(2,1)} %get-tuple-element.57, bf16[1024,768]{1,0:T(8,128)(2,1)} %get-tuple-element.56), kind=kOutput, calls=%fused_computation.1 | convolution fusion | flops 9672327168 | bytes 20447232 | tf_op jit(solution)/shard_map/dot_general | solution.py:12
  364.5 2.0 fusion.22
  366.5 4.6 %collective-permute-start.31 = (bf16[128,3072]{1,0:T(8,128)(2,1)S(1)}, bf16[128,3072]{1,0:T(8,128)(2,1)S(1)}, u32[]{:S(2)}, u32[]{:S(2)}) collective-permute-start(bf16[128,3072]{1,0:T(8,128)(2,1)S(1)} %get-tuple-element.66), channel_id=1, source_target_pairs={{0,4},{4,8},{1,5},{5,9},{2,6},{6,10},{3,7},{7,11},{16,20},{20,24},... | collective-permute-start | bytes 2359304 | tf_op jit(solution)/shard_map/ppermute | solution.py:48
  371.9 2.6 add_convert_fusion.3
  374.5 3.7 broadcast_select_fusion.1
  378.2 10.2 %collective-permute-done.31 = bf16[128,3072]{1,0:T(8,128)(2,1)S(1)} collective-permute-done((bf16[128,3072]{1,0:T(8,128)(2,1)S(1)}, bf16[128,3072]{1,0:T(8,128)(2,1)S(1)}, u32[]{:S(2)}, u32[]{:S(2)}) %collective-permute-start.31) | collective-permute-done | bytes 786464 | tf_op jit(solution)/shard_map/ppermute | solution.py:48
  388.4 1.8 add_convert_fusion.2
  390.1 7.5 %collective-permute-start.32 = (bf16[128,3072]{1,0:T(8,128)(2,1)}, bf16[128,3072]{1,0:T(8,128)(2,1)S(1)}, u32[]{:S(2)}, u32[]{:S(2)}) collective-permute-start(bf16[128,3072]{1,0:T(8,128)(2,1)} %get-tuple-element.64), channel_id=1, source_target_pairs={{0,4},{4,8},{8,12},{1,5},{5,9},{9,13},{2,6},{6,10},{10,14},{3,7},{... | collective-permute-start | bytes 2359304 | tf_op jit(solution)/shard_map/ppermute | solution.py:48
  399.0 15.7 %convolution_convert_fusion = bf16[3072,768]{1,0:T(8,128)(2,1)} fusion(bf16[2048,3072]{1,0:T(8,128)(2,1)} %all-gather.5.cloned.1.call-done, bf16[1024,768]{1,0:T(8,128)(2,1)} %get-tuple-element.55, bf16[1024,768]{1,0:T(8,128)(2,1)} %get-tuple-element.54), kind=kOutput, calls=%fused_computation | convolution fusion | flops 9672327168 | bytes 20447232 | tf_op jit(solution)/shard_map/dot_general | solution.py:12
  414.6 3.5 collective-permute-done.34
  (117 shorter events, 34.5 us)
Async XLA Ops:
  7.2 341.8 %all-gather.3.cloned.1.call-start = ((), (), s32[]{:S(2)}) async-start(), calls=%async_computation | async-start | bytes 18874368 | tf_op jit(solution)/shard_map/all_gather | solution.py:107
  7.2 22.0 %collective-permute-start = (bf16[128,3072]{1,0:T(8,128)(2,1)}, bf16[128,3072]{1,0:T(8,128)(2,1)S(1)}, u32[]{:S(2)}, u32[]{:S(2)}) collective-permute-start(bf16[128,3072]{1,0:T(8,128)(2,1)} %param.4), channel_id=1, source_target_pairs={{0,4},{4,8},{8,12},{1,5},{5,9},{9,13},{2,6},{6,10},{10,14},{3,7},{... | collective-permute-start | bytes 2359304 | tf_op jit(solution)/shard_map/ppermute | solution.py:25
  12.2 21.1 %collective-permute-start.1 = (bf16[128,3072]{1,0:T(8,128)(2,1)}, bf16[128,3072]{1,0:T(8,128)(2,1)S(1)}, u32[]{:S(2)}, u32[]{:S(2)}) collective-permute-start(bf16[128,3072]{1,0:T(8,128)(2,1)} %param.4), channel_id=1, source_target_pairs={{4,0},{8,4},{12,8},{5,1},{9,5},{13,9},{6,2},{10,6},{14,10},{7,3},{... | collective-permute-start | bytes 2359304 | tf_op jit(solution)/shard_map/ppermute | solution.py:26
  13.5 20.7 %collective-permute-start.2 = (bf16[128,3072]{1,0:T(8,128)(2,1)}, bf16[128,3072]{1,0:T(8,128)(2,1)S(1)}, u32[]{:S(2)}, u32[]{:S(2)}) collective-permute-start(bf16[128,3072]{1,0:T(8,128)(2,1)} %param.4), channel_id=1, source_target_pairs={{0,2},{1,3},{2,0},{3,1},{4,6},{5,7},{6,4},{7,5},{8,10},{9,11},{10,... | collective-permute-start | bytes 2359304 | tf_op jit(solution)/shard_map/ppermute | solution.py:77
  15.1 34.6 %collective-permute-start.5 = (bf16[128,3072]{1,0:T(8,128)(2,1)}, bf16[128,3072]{1,0:T(8,128)(2,1)S(1)}, u32[]{:S(2)}, u32[]{:S(2)}) collective-permute-start(bf16[128,3072]{1,0:T(8,128)(2,1)} %param.7), channel_id=1, source_target_pairs={{0,2},{1,3},{2,0},{3,1},{4,6},{5,7},{6,4},{7,5},{8,10},{9,11},{10,... | collective-permute-start | bytes 2359304 | tf_op jit(solution)/shard_map/ppermute | solution.py:77
  35.1 14.5 %collective-permute-start.3 = (bf16[128,3072]{1,0:T(8,128)(2,1)S(1)}, bf16[128,3072]{1,0:T(8,128)(2,1)S(1)}, u32[]{:S(2)}, u32[]{:S(2)}) collective-permute-start(bf16[128,3072]{1,0:T(8,128)(2,1)S(1)} %collective-permute-done), channel_id=1, source_target_pairs={{4,8},{8,12},{5,9},{9,13},{6,10},{10,14},{7,11},{11,15},{20,24},{2... | collective-permute-start | bytes 2359304 | tf_op jit(solution)/shard_map/ppermute | solution.py:25
  35.8 21.5 %collective-permute-start.4 = (bf16[128,3072]{1,0:T(8,128)(2,1)S(1)}, bf16[128,3072]{1,0:T(8,128)(2,1)}, u32[]{:S(2)}, u32[]{:S(2)}) collective-permute-start(bf16[128,3072]{1,0:T(8,128)(2,1)S(1)} %collective-permute-done.1), channel_id=1, source_target_pairs={{4,0},{8,4},{5,1},{9,5},{6,2},{10,6},{7,3},{11,7},{20,16},{24,20},... | collective-permute-start | bytes 2359304 | tf_op jit(solution)/shard_map/ppermute | solution.py:26
  49.6 13.7 %copy-start.22 = (bf16[128,3072]{1,0:T(8,128)(2,1)}, bf16[128,3072]{1,0:T(8,128)(2,1)S(1)}, u32[]{:S(2)}) copy-start(bf16[128,3072]{1,0:T(8,128)(2,1)S(1)} %collective-permute-done.5) | copy-start | bytes 2359300
  49.6 10.2 %copy-start.24 = (bf16[128,3072]{1,0:T(8,128)(2,1)}, bf16[128,3072]{1,0:T(8,128)(2,1)S(1)}, u32[]{:S(2)}) copy-start(bf16[128,3072]{1,0:T(8,128)(2,1)S(1)} %collective-permute-done.3) | copy-start | bytes 2359300
  59.9 15.5 %collective-permute-start.8 = (bf16[128,3072]{1,0:T(8,128)(2,1)}, bf16[128,3072]{1,0:T(8,128)(2,1)}, u32[]{:S(2)}, u32[]{:S(2)}) collective-permute-start(bf16[128,3072]{1,0:T(8,128)(2,1)} %get-tuple-element.47), channel_id=1, source_target_pairs={{0,2},{1,3},{2,0},{3,1},{4,6},{5,7},{6,4},{7,5},{8,10},{9,11},{10,... | collective-permute-start | bytes 2359304 | tf_op jit(solution)/shard_map/ppermute | solution.py:77
  61.4 14.0 %collective-permute-start.6 = (bf16[128,3072]{1,0:T(8,128)(2,1)}, bf16[128,3072]{1,0:T(8,128)(2,1)S(1)}, u32[]{:S(2)}, u32[]{:S(2)}) collective-permute-start(bf16[128,3072]{1,0:T(8,128)(2,1)} %copy-done.24), channel_id=1, source_target_pairs={{8,12},{9,13},{10,14},{11,15},{24,28},{25,29},{26,30},{27,31}} | collective-permute-start | bytes 2359304 | tf_op jit(solution)/shard_map/ppermute | solution.py:25
  62.1 17.1 %collective-permute-start.7 = (bf16[128,3072]{1,0:T(8,128)(2,1)}, bf16[128,3072]{1,0:T(8,128)(2,1)}, u32[]{:S(2)}, u32[]{:S(2)}) collective-permute-start(bf16[128,3072]{1,0:T(8,128)(2,1)} %collective-permute-done.4), channel_id=1, source_target_pairs={{4,0},{5,1},{6,2},{7,3},{20,16},{21,17},{22,18},{23,19}} | collective-permute-start | bytes 2359304 | tf_op jit(solution)/shard_map/ppermute | solution.py:26
  63.4 17.2 %copy-start.13 = (bf16[128,3072]{1,0:T(8,128)(2,1)S(1)}, bf16[128,3072]{1,0:T(8,128)(2,1)}, u32[]{:S(2)}) copy-start(bf16[128,3072]{1,0:T(8,128)(2,1)} %param.7) | copy-start | bytes 2359300
  80.6 17.7 %collective-permute-start.9 = (bf16[128,3072]{1,0:T(8,128)(2,1)S(1)}, bf16[128,3072]{1,0:T(8,128)(2,1)S(1)}, u32[]{:S(2)}, u32[]{:S(2)}) collective-permute-start(bf16[128,3072]{1,0:T(8,128)(2,1)S(1)} %copy-done.13), channel_id=1, source_target_pairs={{4,0},{8,4},{12,8},{5,1},{9,5},{13,9},{6,2},{10,6},{14,10},{7,3},{... | collective-permute-start | bytes 2359304 | tf_op jit(solution)/shard_map/ppermute | solution.py:26
  81.9 17.7 %collective-permute-start.11 = (bf16[128,3072]{1,0:T(8,128)(2,1)S(1)}, bf16[128,3072]{1,0:T(8,128)(2,1)S(1)}, u32[]{:S(2)}, u32[]{:S(2)}) collective-permute-start(bf16[128,3072]{1,0:T(8,128)(2,1)S(1)} %copy-done.13), channel_id=1, source_target_pairs={{0,4},{4,8},{8,12},{1,5},{5,9},{9,13},{2,6},{6,10},{10,14},{3,7},{... | collective-permute-start | bytes 2359304 | tf_op jit(solution)/shard_map/ppermute | solution.py:25
  98.3 15.6 %collective-permute-start.10 = (bf16[128,3072]{1,0:T(8,128)(2,1)S(1)}, bf16[128,3072]{1,0:T(8,128)(2,1)S(1)}, u32[]{:S(2)}, u32[]{:S(2)}) collective-permute-start(bf16[128,3072]{1,0:T(8,128)(2,1)S(1)} %collective-permute-done.9), channel_id=1, source_target_pairs={{4,0},{8,4},{5,1},{9,5},{6,2},{10,6},{7,3},{11,7},{20,16},{24,20},... | collective-permute-start | bytes 2359304 | tf_op jit(solution)/shard_map/ppermute | solution.py:26
  99.6 14.3 %collective-permute-start.12 = (bf16[128,3072]{1,0:T(8,128)(2,1)S(1)}, bf16[128,3072]{1,0:T(8,128)(2,1)S(1)}, u32[]{:S(2)}, u32[]{:S(2)}) collective-permute-start(bf16[128,3072]{1,0:T(8,128)(2,1)S(1)} %collective-permute-done.11), channel_id=1, source_target_pairs={{4,8},{8,12},{5,9},{9,13},{6,10},{10,14},{7,11},{11,15},{20,24},{2... | collective-permute-start | bytes 2359304 | tf_op jit(solution)/shard_map/ppermute | solution.py:25
  115.0 12.0 %collective-permute-start.16 = (bf16[128,3072]{1,0:T(8,128)(2,1)S(1)}, bf16[128,3072]{1,0:T(8,128)(2,1)S(1)}, u32[]{:S(2)}, u32[]{:S(2)}) collective-permute-start(bf16[128,3072]{1,0:T(8,128)(2,1)S(1)} %get-tuple-element.53), channel_id=1, source_target_pairs={{0,2},{1,3},{2,0},{3,1},{4,6},{5,7},{6,4},{7,5},{8,10},{9,11},{10,... | collective-permute-start | bytes 2359304 | tf_op jit(solution)/shard_map/ppermute | solution.py:77
  115.0 12.0 %collective-permute-start.14 = (bf16[128,3072]{1,0:T(8,128)(2,1)S(1)}, bf16[128,3072]{1,0:T(8,128)(2,1)S(1)}, u32[]{:S(2)}, u32[]{:S(2)}) collective-permute-start(bf16[128,3072]{1,0:T(8,128)(2,1)S(1)} %collective-permute-done.12), channel_id=1, source_target_pairs={{8,12},{9,13},{10,14},{11,15},{24,28},{25,29},{26,30},{27,31}} | collective-permute-start | bytes 2359304 | tf_op jit(solution)/shard_map/ppermute | solution.py:25
  115.7 14.4 %collective-permute-start.15 = (bf16[128,3072]{1,0:T(8,128)(2,1)S(1)}, bf16[128,3072]{1,0:T(8,128)(2,1)S(1)}, u32[]{:S(2)}, u32[]{:S(2)}) collective-permute-start(bf16[128,3072]{1,0:T(8,128)(2,1)S(1)} %collective-permute-done.10), channel_id=1, source_target_pairs={{4,0},{5,1},{6,2},{7,3},{20,16},{21,17},{22,18},{23,19}} | collective-permute-start | bytes 2359304 | tf_op jit(solution)/shard_map/ppermute | solution.py:26
  131.2 3.8 copy-start.23
  133.5 28.4 %collective-permute-start.30 = (bf16[256,3072]{1,0:T(8,128)(2,1)S(1)}, bf16[256,3072]{1,0:T(8,128)(2,1)S(1)}, u32[]{:S(2)}, u32[]{:S(2)}) collective-permute-start(bf16[256,3072]{1,0:T(8,128)(2,1)S(1)} %pad_maximum_fusion.3), channel_id=1, source_target_pairs={{0,2},{1,3},{2,0},{3,1},{4,6},{5,7},{6,4},{7,5},{8,10},{9,11},{10,... | collective-permute-start | bytes 4718600 | tf_op jit(solution)/shard_map/ppermute | solution.py:77
  163.2 235.7 %all-gather.5.cloned.1.call-start = ((), (), s32[]{:S(2)}) async-start(), calls=%async_computation.1 | async-start | bytes 18874368 | tf_op jit(solution)/shard_map/all_gather | solution.py:107
  174.8 37.4 %copy-start.8 = (bf16[256,3072]{1,0:T(8,128)(2,1)}, bf16[256,3072]{1,0:T(8,128)(2,1)S(1)}, u32[]{:S(2)}) copy-start(bf16[256,3072]{1,0:T(8,128)(2,1)S(1)} %convolution_convert_fusion.9) | copy-start | bytes 4718596
  174.8 37.4 %collective-permute-start.13 = (bf16[256,3072]{1,0:T(8,128)(2,1)S(1)}, bf16[256,3072]{1,0:T(8,128)(2,1)S(1)}, u32[]{:S(2)}, u32[]{:S(2)}) collective-permute-start(bf16[256,3072]{1,0:T(8,128)(2,1)S(1)} %convolution_convert_fusion.9), channel_id=1, source_target_pairs={{0,16},{16,0},{1,17},{17,1},{2,18},{18,2},{3,19},{19,3},{4,20},{20... | collective-permute-start | bytes 4718600 | tf_op jit(solution)/shard_map/ppermute | solution.py:60
  187.6 58.3 %copy-start.4 = (bf16[256,3072]{1,0:T(8,128)(2,1)}, bf16[256,3072]{1,0:T(8,128)(2,1)S(1)}, u32[]{:S(2)}) copy-start(bf16[256,3072]{1,0:T(8,128)(2,1)S(1)} %convolution_convert_fusion.7) | copy-start | bytes 4718596
  187.6 2.9 copy-start.21
  187.6 61.2 %collective-permute-start.35 = (bf16[256,3072]{1,0:T(8,128)(2,1)S(1)}, bf16[256,3072]{1,0:T(8,128)(2,1)}, u32[]{:S(2)}, u32[]{:S(2)}) collective-permute-start(bf16[256,3072]{1,0:T(8,128)(2,1)S(1)} %pad_maximum_fusion.1), channel_id=1, source_target_pairs={{0,2},{1,3},{2,0},{3,1},{4,6},{5,7},{6,4},{7,5},{8,10},{9,11},{10,... | collective-permute-start | bytes 4718600 | tf_op jit(solution)/shard_map/ppermute | solution.py:77
  188.2 57.7 %collective-permute-start.17 = (bf16[256,3072]{1,0:T(8,128)(2,1)S(1)}, bf16[256,3072]{1,0:T(8,128)(2,1)S(1)}, u32[]{:S(2)}, u32[]{:S(2)}) collective-permute-start(bf16[256,3072]{1,0:T(8,128)(2,1)S(1)} %convolution_convert_fusion.7), channel_id=1, source_target_pairs={{0,16},{16,0},{1,17},{17,1},{2,18},{18,2},{3,19},{19,3},{4,20},{20... | collective-permute-start | bytes 4718600 | tf_op jit(solution)/shard_map/ppermute | solution.py:60
  212.2 11.7 %copy-start.10 = (bf16[256,3072]{1,0:T(8,128)(2,1)}, bf16[256,3072]{1,0:T(8,128)(2,1)S(1)}, u32[]{:S(2)}) copy-start(bf16[256,3072]{1,0:T(8,128)(2,1)S(1)} %collective-permute-done.13) | copy-start | bytes 4718596
  234.4 45.4 %collective-permute-start.24 = (bf16[256,3072]{1,0:T(8,128)(2,1)}, bf16[256,3072]{1,0:T(8,128)(2,1)}, u32[]{:S(2)}, u32[]{:S(2)}) collective-permute-start(bf16[256,3072]{1,0:T(8,128)(2,1)} %convolution_convert_fusion.5), channel_id=1, source_target_pairs={{0,16},{16,0},{1,17},{17,1},{2,18},{18,2},{3,19},{19,3},{4,20},{20... | collective-permute-start | bytes 4718600 | tf_op jit(solution)/shard_map/ppermute | solution.py:60
  245.9 2.9 copy-start.6
  247.2 1.7 copy-start.12
  248.9 36.0 %collective-permute-start.28 = (bf16[512,1536]{1,0:T(8,128)(2,1)}, bf16[512,1536]{1,0:T(8,128)(2,1)}, u32[]{:S(2)}, u32[]{:S(2)}) collective-permute-start(bf16[512,1536]{1,0:T(8,128)(2,1)} %get-tuple-element.58), channel_id=1, source_target_pairs={{0,2},{1,3},{2,0},{3,1},{4,6},{5,7},{6,4},{7,5},{8,10},{9,11},{10,... | collective-permute-start | bytes 4718600 | tf_op jit(solution)/shard_map/ppermute | solution.py:90
  261.4 12.5 %copy-start.2 = (bf16[256,3072]{1,0:T(8,128)(2,1)}, bf16[256,3072]{1,0:T(8,128)(2,1)S(1)}, u32[]{:S(2)}) copy-start(bf16[256,3072]{1,0:T(8,128)(2,1)S(1)} %convolution_convert_fusion.6) | copy-start | bytes 4718596
  273.2 10.7 %copy-start.18 = (bf16[256,3072]{1,0:T(8,128)(2,1)}, bf16[256,3072]{1,0:T(8,128)(2,1)S(1)}, u32[]{:S(2)}) copy-start(bf16[256,3072]{1,0:T(8,128)(2,1)S(1)} %convolution_convert_fusion.3) | copy-start | bytes 4718596
  273.2 6.5 %copy-start.9 = (bf16[256,3072]{1,0:T(8,128)(2,1)S(1)}, bf16[256,3072]{1,0:T(8,128)(2,1)}, u32[]{:S(2)}) copy-start(bf16[256,3072]{1,0:T(8,128)(2,1)} %copy-done.8) | copy-start | bytes 4718596
  273.2 6.5 %copy-start.11 = (bf16[256,3072]{1,0:T(8,128)(2,1)S(1)}, bf16[256,3072]{1,0:T(8,128)(2,1)}, u32[]{:S(2)}) copy-start(bf16[256,3072]{1,0:T(8,128)(2,1)} %copy-done.10) | copy-start | bytes 4718596
  273.2 30.7 %collective-permute-start.25 = (bf16[256,3072]{1,0:T(8,128)(2,1)S(1)}, bf16[256,3072]{1,0:T(8,128)(2,1)}, u32[]{:S(2)}, u32[]{:S(2)}) collective-permute-start(bf16[256,3072]{1,0:T(8,128)(2,1)S(1)} %convolution_convert_fusion.3), channel_id=1, source_target_pairs={{0,16},{16,0},{1,17},{17,1},{2,18},{18,2},{3,19},{19,3},{4,20},{20... | collective-permute-start | bytes 4718600 | tf_op jit(solution)/shard_map/ppermute | solution.py:60
  273.9 12.4 %collective-permute-start.18 = (bf16[128,3072]{1,0:T(8,128)(2,1)S(1)}, bf16[128,3072]{1,0:T(8,128)(2,1)S(1)}, u32[]{:S(2)}, u32[]{:S(2)}) collective-permute-start(bf16[128,3072]{1,0:T(8,128)(2,1)S(1)} %get-tuple-element.74), channel_id=1, source_target_pairs={{0,4},{1,5},{2,6},{3,7},{16,20},{17,21},{18,22},{19,23}} | collective-permute-start | bytes 2359304 | tf_op jit(solution)/shard_map/ppermute | solution.py:48
  275.6 10.8 %collective-permute-start.21 = (bf16[128,3072]{1,0:T(8,128)(2,1)S(1)}, bf16[128,3072]{1,0:T(8,128)(2,1)S(1)}, u32[]{:S(2)}, u32[]{:S(2)}) collective-permute-start(bf16[128,3072]{1,0:T(8,128)(2,1)S(1)} %get-tuple-element.75), channel_id=1, source_target_pairs={{12,8},{13,9},{14,10},{15,11},{28,24},{29,25},{30,26},{31,27}} | collective-permute-start | bytes 2359304 | tf_op jit(solution)/shard_map/ppermute | solution.py:49
  284.9 1.6 copy-start.15
  284.9 44.6 %collective-permute-start.36 = (bf16[256,1536]{1,0:T(8,128)(2,1)}, bf16[256,1536]{1,0:T(8,128)(2,1)}, u32[]{:S(2)}, u32[]{:S(2)}) collective-permute-start(bf16[256,1536]{1,0:T(8,128)(2,1)} %get-tuple-element.61), channel_id=1, source_target_pairs={{0,2},{1,3},{2,0},{3,1},{4,6},{5,7},{6,4},{7,5},{8,10},{9,11},{10,... | collective-permute-start | bytes 2359304 | tf_op jit(solution)/shard_map/ppermute | solution.py:90
  286.3 58.5 %collective-permute-start.29 = (bf16[1024,768]{1,0:T(8,128)(2,1)S(1)}, bf16[1024,768]{1,0:T(8,128)(2,1)}, u32[]{:S(2)}, u32[]{:S(2)}) collective-permute-start(bf16[1024,768]{1,0:T(8,128)(2,1)S(1)} %fusion.24), channel_id=1, source_target_pairs={{0,1},{1,0},{2,3},{3,2},{4,5},{5,4},{6,7},{7,6},{8,9},{9,8},{10,11... | collective-permute-start | bytes 4718600 | tf_op jit(solution)/shard_map/ppermute | solution.py:100
  288.1 32.7 %collective-permute-start.19 = (bf16[128,3072]{1,0:T(8,128)(2,1)}, bf16[128,3072]{1,0:T(8,128)(2,1)}, u32[]{:S(2)}, u32[]{:S(2)}) collective-permute-start(bf16[128,3072]{1,0:T(8,128)(2,1)} %get-tuple-element.72), channel_id=1, source_target_pairs={{0,4},{4,8},{1,5},{5,9},{2,6},{6,10},{3,7},{7,11},{16,20},{20,24},... | collective-permute-start | bytes 2359304 | tf_op jit(solution)/shard_map/ppermute | solution.py:48
  291.9 12.0 %copy-start.5 = (bf16[256,3072]{1,0:T(8,128)(2,1)S(1)}, bf16[256,3072]{1,0:T(8,128)(2,1)}, u32[]{:S(2)}) copy-start(bf16[256,3072]{1,0:T(8,128)(2,1)} %copy-done.4) | copy-start | bytes 4718596
  291.9 12.0 %copy-start.7 = (bf16[256,3072]{1,0:T(8,128)(2,1)S(1)}, bf16[256,3072]{1,0:T(8,128)(2,1)}, u32[]{:S(2)}) copy-start(bf16[256,3072]{1,0:T(8,128)(2,1)} %copy-done.6) | copy-start | bytes 4718596
  291.9 12.0 %copy-start.19 = (bf16[256,3072]{1,0:T(8,128)(2,1)S(1)}, bf16[256,3072]{1,0:T(8,128)(2,1)}, u32[]{:S(2)}) copy-start(bf16[256,3072]{1,0:T(8,128)(2,1)} %copy-done.18) | copy-start | bytes 4718596
  291.9 33.0 %collective-permute-start.22 = (bf16[128,3072]{1,0:T(8,128)(2,1)}, bf16[128,3072]{1,0:T(8,128)(2,1)}, u32[]{:S(2)}, u32[]{:S(2)}) collective-permute-start(bf16[128,3072]{1,0:T(8,128)(2,1)} %get-tuple-element.73), channel_id=1, source_target_pairs={{8,4},{12,8},{9,5},{13,9},{10,6},{14,10},{11,7},{15,11},{24,20},{2... | collective-permute-start | bytes 2359304 | tf_op jit(solution)/shard_map/ppermute | solution.py:49
  317.0 9.4 %copy-start.3 = (bf16[256,3072]{1,0:T(8,128)(2,1)S(1)}, bf16[256,3072]{1,0:T(8,128)(2,1)}, u32[]{:S(2)}) copy-start(bf16[256,3072]{1,0:T(8,128)(2,1)} %copy-done.2) | copy-start | bytes 4718596
  317.1 18.4 %collective-permute-start.37 = (bf16[256,1536]{1,0:T(8,128)(2,1)S(1)}, bf16[256,1536]{1,0:T(8,128)(2,1)S(1)}, u32[]{:S(2)}, u32[]{:S(2)}) collective-permute-start(bf16[256,1536]{1,0:T(8,128)(2,1)S(1)} %get-tuple-element.63), channel_id=1, source_target_pairs={{0,2},{1,3},{2,0},{3,1},{4,6},{5,7},{6,4},{7,5},{8,10},{9,11},{10,... | collective-permute-start | bytes 2359304 | tf_op jit(solution)/shard_map/ppermute | solution.py:90
  320.9 43.6 %collective-permute-start.26 = (bf16[128,3072]{1,0:T(8,128)(2,1)}, bf16[128,3072]{1,0:T(8,128)(2,1)}, u32[]{:S(2)}, u32[]{:S(2)}) collective-permute-start(bf16[128,3072]{1,0:T(8,128)(2,1)} %get-tuple-element.69), channel_id=1, source_target_pairs={{0,4},{1,5},{2,6},{3,7},{16,20},{17,21},{18,22},{19,23}} | collective-permute-start | bytes 2359304 | tf_op jit(solution)/shard_map/ppermute | solution.py:48
  324.9 39.6 %collective-permute-start.27 = (bf16[128,3072]{1,0:T(8,128)(2,1)}, bf16[128,3072]{1,0:T(8,128)(2,1)}, u32[]{:S(2)}, u32[]{:S(2)}) collective-permute-start(bf16[128,3072]{1,0:T(8,128)(2,1)} %get-tuple-element.68), channel_id=1, source_target_pairs={{12,8},{13,9},{14,10},{15,11},{28,24},{29,25},{30,26},{31,27}} | collective-permute-start | bytes 2359304 | tf_op jit(solution)/shard_map/ppermute | solution.py:49
  329.5 42.3 %collective-permute-start.20 = (bf16[128,3072]{1,0:T(8,128)(2,1)}, bf16[128,3072]{1,0:T(8,128)(2,1)}, u32[]{:S(2)}, u32[]{:S(2)}) collective-permute-start(bf16[128,3072]{1,0:T(8,128)(2,1)} %get-tuple-element.70), channel_id=1, source_target_pairs={{0,4},{4,8},{8,12},{1,5},{5,9},{9,13},{2,6},{6,10},{10,14},{3,7},{... | collective-permute-start | bytes 2359304 | tf_op jit(solution)/shard_map/ppermute | solution.py:48
  335.5 36.3 %collective-permute-start.23 = (bf16[128,3072]{1,0:T(8,128)(2,1)}, bf16[128,3072]{1,0:T(8,128)(2,1)}, u32[]{:S(2)}, u32[]{:S(2)}) collective-permute-start(bf16[128,3072]{1,0:T(8,128)(2,1)} %get-tuple-element.71), channel_id=1, source_target_pairs={{4,0},{8,4},{12,8},{5,1},{9,5},{13,9},{6,2},{10,6},{14,10},{7,3},{... | collective-permute-start | bytes 2359304 | tf_op jit(solution)/shard_map/ppermute | solution.py:49
  341.8 1.7 copy-start
  344.7 29.7 %collective-permute-start.38 = (bf16[1024,768]{1,0:T(8,128)(2,1)}, bf16[1024,768]{1,0:T(8,128)(2,1)}, u32[]{:S(2)}, u32[]{:S(2)}) collective-permute-start(bf16[1024,768]{1,0:T(8,128)(2,1)} %constant_dynamic-slice_fusion), channel_id=1, source_target_pairs={{0,1},{1,0},{2,3},{3,2},{4,5},{5,4},{6,7},{7,6},{8,9},{9,8},{10,11... | collective-permute-start | bytes 4718600 | tf_op jit(solution)/shard_map/ppermute | solution.py:100
  349.0 15.5 %copy-start.17 = (bf16[256,3072]{1,0:T(8,128)(2,1)S(1)}, bf16[256,3072]{1,0:T(8,128)(2,1)}, u32[]{:S(2)}) copy-start(bf16[256,3072]{1,0:T(8,128)(2,1)} %convolution_convert_fusion.4) | copy-start | bytes 4718596
  349.0 22.8 %copy-start.16 = (bf16[256,3072]{1,0:T(8,128)(2,1)S(1)}, bf16[256,3072]{1,0:T(8,128)(2,1)}, u32[]{:S(2)}) copy-start(bf16[256,3072]{1,0:T(8,128)(2,1)} %convolution_convert_fusion.8) | copy-start | bytes 4718596
  364.4 10.0 %copy-start.1 = (bf16[1024,1536]{1,0:T(8,128)(2,1)S(1)}, bf16[1024,1536]{1,0:T(8,128)(2,1)}, u32[]{:S(2)}) copy-start(bf16[1024,1536]{1,0:T(8,128)(2,1)} %copy-done) | copy-start | bytes 9437188
  366.5 21.9 %collective-permute-start.31 = (bf16[128,3072]{1,0:T(8,128)(2,1)S(1)}, bf16[128,3072]{1,0:T(8,128)(2,1)S(1)}, u32[]{:S(2)}, u32[]{:S(2)}) collective-permute-start(bf16[128,3072]{1,0:T(8,128)(2,1)S(1)} %get-tuple-element.66), channel_id=1, source_target_pairs={{0,4},{4,8},{1,5},{5,9},{2,6},{6,10},{3,7},{7,11},{16,20},{20,24},... | collective-permute-start | bytes 2359304 | tf_op jit(solution)/shard_map/ppermute | solution.py:48
  371.1 17.3 %collective-permute-start.33 = (bf16[128,3072]{1,0:T(8,128)(2,1)S(1)}, bf16[128,3072]{1,0:T(8,128)(2,1)S(1)}, u32[]{:S(2)}, u32[]{:S(2)}) collective-permute-start(bf16[128,3072]{1,0:T(8,128)(2,1)S(1)} %get-tuple-element.67), channel_id=1, source_target_pairs={{8,4},{12,8},{9,5},{13,9},{10,6},{14,10},{11,7},{15,11},{24,20},{2... | collective-permute-start | bytes 2359304 | tf_op jit(solution)/shard_map/ppermute | solution.py:49
  390.1 24.5 %collective-permute-start.32 = (bf16[128,3072]{1,0:T(8,128)(2,1)}, bf16[128,3072]{1,0:T(8,128)(2,1)S(1)}, u32[]{:S(2)}, u32[]{:S(2)}) collective-permute-start(bf16[128,3072]{1,0:T(8,128)(2,1)} %get-tuple-element.64), channel_id=1, source_target_pairs={{0,4},{4,8},{8,12},{1,5},{5,9},{9,13},{2,6},{6,10},{10,14},{3,7},{... | collective-permute-start | bytes 2359304 | tf_op jit(solution)/shard_map/ppermute | solution.py:48
  397.6 20.5 %collective-permute-start.34 = (bf16[128,3072]{1,0:T(8,128)(2,1)}, bf16[128,3072]{1,0:T(8,128)(2,1)S(1)}, u32[]{:S(2)}, u32[]{:S(2)}) collective-permute-start(bf16[128,3072]{1,0:T(8,128)(2,1)} %get-tuple-element.65), channel_id=1, source_target_pairs={{4,0},{8,4},{12,8},{5,1},{9,5},{13,9},{6,2},{10,6},{14,10},{7,3},{... | collective-permute-start | bytes 2359304 | tf_op jit(solution)/shard_map/ppermute | solution.py:49
  (2 other events, 2.0 us)
Sparse Core Ops, SparseCore 0:
  163.4 23.6 all-gather.2
  261.5 23.9 all-gather.4

commit v4 on v3

--- a/solution.py
+++ b/solution.py
@@ -32,12 +32,12 @@
     return [block] + [slot(k) for k in range(1, n)], done
 
 
-def line_reduce(parts, n, beside=None):
+def line_reduce(parts, n, hooks):
     if n == 1:
-        return parts[0]
+        return parts(0)
     right = left = None
     for step in range(1, n):
-        to_right, to_left = parts[n - step], parts[step]
+        to_right, to_left = parts(n - step), parts(step)
         if right is not None:
             to_right = (to_right.astype(jnp.float32) + right.astype(jnp.float32)).astype(
                 jnp.bfloat16
@@ -47,11 +47,11 @@
             )
         right = lax.ppermute(to_right, "col", [(c, c + 1) for c in range(step)])
         left = lax.ppermute(to_left, "col", [(c, c - 1) for c in range(n - step, n)])
-        if step == 1 and beside is not None:
-            right, left, beside = lax.optimization_barrier((right, left, beside))
-    total = parts[0].astype(jnp.float32) + right.astype(jnp.float32) + left.astype(jnp.float32)
+        if step in hooks:
+            right, left = hooks[step](right, left)
+    total = parts(0).astype(jnp.float32) + right.astype(jnp.float32) + left.astype(jnp.float32)
     total = total.astype(jnp.bfloat16)
-    return total if beside is None else (total, beside)
+    return total
 
 
 def row_sum(part, n):
@@ -113,17 +113,16 @@
 
 def body(n_row, n_col, n_depth, tokens, w_in, w_out, grad_out):
     rows = tokens.shape[0]
-    half = n_col // 2
     tie = lax.optimization_barrier
 
     def fold(slots):
         return cat(*slots[0::2]), cat(*slots[1::2])
 
-    def unfold(even, odd):
-        slots = [None] * n_col
-        slots[0::2] = [even[k * rows : (k + 1) * rows] for k in range(half)]
-        slots[1::2] = [odd[k * rows : (k + 1) * rows] for k in range(half)]
-        return slots
+    def slot_of(held):
+        def slot(k):
+            return held["odd" if k % 2 else "even"][k // 2 * rows : (k // 2 + 1) * rows]
+
+        return slot
 
     def own_part(part):
         return part.astype(jnp.bfloat16)
@@ -138,14 +137,17 @@
     )
     tok_own, grad_own, tok_two = tok_high
     tok_even, tok_odd = fold(tok_slots)
-    pre_even = row_sum(own_part(dot(tok_even, w_in, 1, 0)), n_row)
+    part_even = own_part(dot(tok_even, w_in, 1, 0))
+    pre_even = row_sum(part_even, n_row)
     grad_out, tok_odd = tie((grad_out, tok_odd))
     tok_odd_high = step_high(tok_odd)
-    part_odd = own_part(dot(tok_odd, w_in, 1, 0))
+    tok_odd_in, _ = tie((tok_odd, part_even))
+    part_odd = own_part(dot(tok_odd_in, w_in, 1, 0))
     pre_odd = row_sum(part_odd, n_row)
     grad_slots, grad_high = line_gather(
-        grad_out, n_col, [lambda slot: None, lambda slot: None, lambda slot: step_high(slot(2))]
-    )
+        grad_out, n_col, [lambda slot: part_odd, lambda slot: (pre_even, tok_odd_high), lambda slot: step_high(slot(2))]
+    )
+    pre_even, tok_odd_high = grad_high[1]
     grad_two = grad_high[2]
     act_even, pull_even = jax.vjp(gelu_tanh, pre_even)
     act_odd, pull_odd = jax.vjp(gelu_tanh, pre_odd)
@@ -154,16 +156,26 @@
     grad_odd_high = step_high(grad_odd)
 
     out_even = own_part(dot(act_even, w_out, 1, 0))
-    grad_even_in, out_even = tie((grad_even, out_even))
-    gact_even = row_sum(own_part(dot(grad_even_in, w_out, 1, 1)), n_row)
+    grad_odd_in, out_even = tie((grad_odd, out_even))
+    gact_odd_part = own_part(dot(grad_odd_in, w_out, 1, 1))
+    gact_odd = row_sum(gact_odd_part, n_row)
+    act_odd, _ = tie((act_odd, gact_odd_part))
     out_odd = own_part(dot(act_odd, w_out, 1, 0))
-    grad_odd_in, out_odd = tie((grad_odd, out_odd))
-    gact_odd = row_sum(own_part(dot(grad_odd_in, w_out, 1, 1)), n_row)
-    output = line_reduce(unfold(out_even, out_odd), n_col)
-
-    gpre_even = own_part(pull_even(gact_even)[0])
+    grad_even_in, out_odd = tie((grad_even, out_odd))
+    gact_even_part = own_part(dot(grad_even_in, w_out, 1, 1))
+    gact_even = row_sum(gact_even_part, n_row)
+    held = {"gact_odd": gact_odd}
+
+    def out_hook(right, left):
+        right, left, held["gact_odd"] = tie((right, left, held["gact_odd"]))
+        return right, left
+
+    output = line_reduce(slot_of({"even": out_even, "odd": out_odd}), n_col, {1: out_hook})
+    gact_odd = held["gact_odd"]
+    gact_odd, grad_odd_high, _ = tie((gact_odd, grad_odd_high, gact_even_part))
+    act_high = high_columns(cat(act_even, act_odd), masks, n_depth)
+
     gpre_odd = own_part(pull_odd(gact_odd)[0])
-    gtok_even = own_part(dot(gpre_even, w_in, 1, 1))
     gtok_odd = own_part(dot(gpre_odd, w_in, 1, 1))
 
     def high_rows(own, two, odd_high, even, odd):
@@ -176,16 +188,28 @@
     all_grad = core_gather(
         high_rows(grad_own, grad_two, grad_odd_high, grad_even, grad_odd), n_depth
     )
-    act_high = high_columns(cat(act_even, act_odd), masks, n_depth)
-    all_act = core_exchange(cat(*act_high), n_depth)
-    gpre_high = zip(
-        high_columns(gpre_even, masks, n_depth), high_columns(gpre_odd, masks, n_depth)
-    )
+    gtok = {"odd": gtok_odd}
+    odd_high = high_columns(gpre_odd, masks, n_depth)
+
+    def first_hook(right, left):
+        right, left, gact, act_all = tie((right, left, gact_even, act_high))
+        gpre_even = own_part(pull_even(gact)[0])
+        gtok["even"] = own_part(dot(gpre_even, w_in, 1, 1))
+        gtok["even_high"] = high_columns(gpre_even, masks, n_depth)
+        all_act = core_exchange(cat(*act_all), n_depth)
+        gtok["w_out"] = own_part(dot(all_act, all_grad, 0, 0))
+        return right, left
+
+    def later_hook(right, left):
+        right, left, gtok["w_out"] = tie((right, left, gtok["w_out"]))
+        return right, left
+
+    hooks = {1: first_hook, 2: later_hook}
+    grad_tokens = line_reduce(slot_of(gtok), n_col, hooks)
+    gpre_high = zip(gtok["even_high"], odd_high)
     all_gpre = core_exchange(cat(*[b for pair in gpre_high for b in pair]), n_depth)
-    grad_w_out = own_part(dot(all_act, all_grad, 0, 0))
-    grad_tokens, grad_w_out = line_reduce(unfold(gtok_even, gtok_odd), n_col, grad_w_out)
     grad_w_in = own_part(dot(all_tok, all_gpre, 0, 0))
-    return output, grad_tokens, grad_w_in, grad_w_out
+    return output, grad_tokens, grad_w_in, gtok["w_out"]
 
 
 def solution(mesh):

time: 431 us -> 333 us (0.77)
  waiting for transfers between devices: 165 us -> 75.7 us
  matrix products: 116 us -> 107 us
  other arithmetic: 46.1 us -> 38.7 us
  starting transfers between devices: 63.5 us -> 68.7 us
    ppermute x6, waiting for transfers between devices: 58.3 us -> 12.9 us  [depth_high(): lax.ppermute(b, 'depth', [(d, d ^ bit) for d in range(n)])]
    ppermute x6, waiting for transfers between devices: 43.1 us -> 19.8 us  [line_gather(): lax.ppermute(left, 'col', [(c, c - 1) for c in range(1, n - step + 1)])]
    ppermute x4, waiting for transfers between devices: 32.5 us -> 16.2 us  [row_sum(): other = lax.ppermute(part, 'row', [(r, (r + step) % n) for r in range(n)])]
    ppermute x6, waiting for transfers between devices: 10.2 us -> 0.02 us  [line_reduce(): right = lax.ppermute(to_right, 'col', [(c, c + 1) for c in range(step)])]
    ppermute x3, waiting for transfers between devices: 3.85 us -> 13.1 us  [high_columns(): piece = lax.ppermute(piece, 'depth', [(d, d ^ m) for d in range(n)])]
    dot_general x10, matrix products: 116 us -> 107 us  [dot(): lax.dot_general(a, b, (((ca,), (cb,)), ((), ())), preferred_element_type=...]
    unnamed x57 -> x70, local copies, waits for them, and re-layouts: 13.2 us -> 16.9 us
  transfers between devices with their start and end apart: 41 -> 41, of which waited for: 18 -> 14; matrix products, arithmetic and copies ran while one was open for 40% -> 47% of each run, Pallas kernels for 0% -> 0%
where the time goes in v4:
time: 333 us; the launch traced here: 327 us
  matrix products  107 us (32%)
  waiting for transfers between devices  75.7 us (23%)
  starting transfers between devices  68.7 us (21%)
  other arithmetic  38.7 us (12%)
  local copies, waits for them, and re-layouts  21.9 us (7%)
  between operations  15 us (5%)
    dot_general x10, matrix products, dot(): lax.dot_general(a, b, (((ca,), (cb,)), ((), ())), preferred_element_type=...  107 us
    ppermute x6, starting transfers between devices, line_reduce(): right = lax.ppermute(to_right, 'col', [(c, c + 1) for c in range(step)])  22 us
    ppermute x6, waiting for transfers between devices, line_gather(): lax.ppermute(left, 'col', [(c, c - 1) for c in range(1, n - step + 1)])  19.8 us
    unnamed x70, local copies, waits for them, and re-layouts  16.9 us
    ppermute x4, waiting for transfers between devices, row_sum(): other = lax.ppermute(part, 'row', [(r, (r + step) % n) for r in range(n)])  16.2 us
    ppermute x6, waiting for transfers between devices, line_gather(): lax.ppermute(right, 'col', [(c, c + 1) for c in range(step - 1, n - 1)])  13.7 us
    ppermute x6, starting transfers between devices, line_gather(): lax.ppermute(right, 'col', [(c, c + 1) for c in range(step - 1, n - 1)])  13.1 us
    ppermute x3, waiting for transfers between devices, high_columns(): piece = lax.ppermute(piece, 'depth', [(d, d ^ m) for d in range(n)])  13.1 us
  transfers between devices with their start and end apart: 41, of which 14 were waited for; matrix products, arithmetic and copies ran while one was open for 47% of the time, Pallas kernels for 0%

profile of v4, /device:TPU:0, one launch (start us, length us, event | category | flops | bytes accessed | tf_op | source)
XLA Modules:
  0.0 327.0 jit_solution(4561248106858108077)
XLA Ops:
  7.2 5.1 %collective-permute-start = (bf16[128,3072]{1,0:T(8,128)(2,1)}, bf16[128,3072]{1,0:T(8,128)(2,1)S(1)}, u32[]{:S(2)}, u32[]{:S(2)}) collective-permute-start(bf16[128,3072]{1,0:T(8,128)(2,1)} %param.4), channel_id=1, source_target_pairs={{0,4},{4,8},{8,12},{1,5},{5,9},{9,13},{2,6},{6,10},{10,14},{3,7},{... | collective-permute-start | bytes 2359304 | tf_op jit(solution)/shard_map/ppermute | solution.py:25
  12.3 1.3 collective-permute-start.1
  13.6 1.6 collective-permute-start.2
  15.7 13.7 %collective-permute-done = bf16[128,3072]{1,0:T(8,128)(2,1)S(1)} collective-permute-done((bf16[128,3072]{1,0:T(8,128)(2,1)}, bf16[128,3072]{1,0:T(8,128)(2,1)S(1)}, u32[]{:S(2)}, u32[]{:S(2)}) %collective-permute-start) | collective-permute-done | bytes 786464 | tf_op jit(solution)/shard_map/ppermute | solution.py:25
  29.4 4.1 %collective-permute-done.1 = bf16[128,3072]{1,0:T(8,128)(2,1)S(1)} collective-permute-done((bf16[128,3072]{1,0:T(8,128)(2,1)}, bf16[128,3072]{1,0:T(8,128)(2,1)S(1)}, u32[]{:S(2)}, u32[]{:S(2)}) %collective-permute-start.1) | collective-permute-done | bytes 786464 | tf_op jit(solution)/shard_map/ppermute | solution.py:26
  34.4 1.6 collective-permute-start.3
  37.2 2.1 constant_dynamic-update-slice_fusion.14
  39.3 10.5 %collective-permute-done.5 = bf16[128,3072]{1,0:T(8,128)(2,1)} collective-permute-done((bf16[128,3072]{1,0:T(8,128)(2,1)}, bf16[128,3072]{1,0:T(8,128)(2,1)}, u32[]{:S(2)}, u32[]{:S(2)}) %collective-permute-start.5) | collective-permute-done | bytes 786464 | tf_op jit(solution)/shard_map/ppermute | solution.py:77
  49.9 7.6 %collective-permute-done.4 = bf16[128,3072]{1,0:T(8,128)(2,1)} collective-permute-done((bf16[128,3072]{1,0:T(8,128)(2,1)S(1)}, bf16[128,3072]{1,0:T(8,128)(2,1)}, u32[]{:S(2)}, u32[]{:S(2)}) %collective-permute-start.4) | collective-permute-done | bytes 786464 | tf_op jit(solution)/shard_map/ppermute | solution.py:26
  58.1 1.3 collective-permute-start.7
  59.4 2.2 constant_dynamic-update-slice_fusion.13
  61.6 1.5 collective-permute-start.8
  63.1 9.2 %convolution_convert_fusion.9 = bf16[256,3072]{1,0:T(8,128)(2,1)S(1)} fusion(bf16[3072,3072]{1,0:T(8,128)(2,1)} %param.5, bf16[128,3072]{1,0:T(8,128)(2,1)S(1)} %get-tuple-element.83, bf16[128,3072]{1,0:T(8,128)(2,1)S(1)} %copy-done.20), kind=kOutput, calls=%fused_computation.13 | convolution fusion | flops 4835770368 | bytes 22020096 | tf_op jit(solution)/shard_map/dot_general | solution.py:12
  72.4 1.6 collective-permute-start.13
  74.0 1.4 collective-permute-done.7
  75.4 1.4 collective-permute-done.8
  77.8 4.4 %collective-permute-start.9 = (bf16[128,3072]{1,0:T(8,128)(2,1)S(1)}, bf16[128,3072]{1,0:T(8,128)(2,1)S(1)}, u32[]{:S(2)}, u32[]{:S(2)}) collective-permute-start(bf16[128,3072]{1,0:T(8,128)(2,1)S(1)} %copy-done.12), channel_id=1, source_target_pairs={{0,4},{4,8},{8,12},{1,5},{5,9},{9,13},{2,6},{6,10},{10,14},{3,7},{... | collective-permute-start | bytes 2359304 | tf_op jit(solution)/shard_map/ppermute | solution.py:25
  82.2 1.3 collective-permute-start.10
  83.5 1.6 collective-permute-start.14
  85.0 9.2 %convolution_convert_fusion.8 = bf16[256,3072]{1,0:T(8,128)(2,1)S(1)} fusion(bf16[256,3072]{1,0:T(8,128)(2,1)S(1)} %pad_maximum_fusion.1, bf16[3072,3072]{1,0:T(8,128)(2,1)} %param.5), kind=kOutput, calls=%fused_computation.12 | convolution fusion | flops 4832624640 | bytes 22020096 | tf_op jit(solution)/shard_map/dot_general | solution.py:12
  94.3 1.6 collective-permute-start.18
  99.9 9.8 %collective-permute-done.13 = bf16[256,3072]{1,0:T(8,128)(2,1)S(1)} collective-permute-done((bf16[256,3072]{1,0:T(8,128)(2,1)S(1)}, bf16[256,3072]{1,0:T(8,128)(2,1)S(1)}, u32[]{:S(2)}, u32[]{:S(2)}) %collective-permute-start.13) | collective-permute-done | bytes 1572896 | tf_op jit(solution)/shard_map/ppermute | solution.py:60
  110.3 5.6 %collective-permute-done.12 = bf16[128,3072]{1,0:T(8,128)(2,1)S(1)} collective-permute-done((bf16[128,3072]{1,0:T(8,128)(2,1)S(1)}, bf16[128,3072]{1,0:T(8,128)(2,1)S(1)}, u32[]{:S(2)}, u32[]{:S(2)}) %collective-permute-start.12) | collective-permute-done | bytes 786464 | tf_op jit(solution)/shard_map/ppermute | solution.py:26
  117.1 1.5 collective-permute-start.16
  119.8 1.8 collective-permute-start.17
  122.5 10.9 %convolution_convert_fusion.7 = bf16[256,3072]{1,0:T(8,128)(2,1)} fusion(bf16[256,3072]{1,0:T(8,128)(2,1)S(1)} %multiply_convert_fusion.1, bf16[3072,3072]{1,0:T(8,128)(2,1)} %param.6), kind=kOutput, calls=%fused_computation.11 | convolution fusion | flops 4832624640 | bytes 22020096 | tf_op jit(solution)/shard_map/dot_general | solution.py:12
  133.5 4.4 %collective-permute-done.18 = bf16[256,3072]{1,0:T(8,128)(2,1)S(1)} collective-permute-done((bf16[256,3072]{1,0:T(8,128)(2,1)S(1)}, bf16[256,3072]{1,0:T(8,128)(2,1)S(1)}, u32[]{:S(2)}, u32[]{:S(2)}) %collective-permute-start.18) | collective-permute-done | bytes 1572896 | tf_op jit(solution)/shard_map/ppermute | solution.py:60
  139.2 1.4 constant_dynamic-update-slice_fusion.6
  142.5 9.2 %convolution_convert_fusion.6 = bf16[256,3072]{1,0:T(8,128)(2,1)S(1)} fusion(bf16[256,3072]{1,0:T(8,128)(2,1)S(1)} %pad_maximum_fusion.2, bf16[3072,3072]{1,0:T(8,128)(2,1)} %param.6), kind=kOutput, calls=%fused_computation.10 | convolution fusion | flops 4832624640 | bytes 22020096 | tf_op jit(solution)/shard_map/dot_general | solution.py:12
  151.7 1.6 collective-permute-start.21
  153.3 9.2 %convolution_convert_fusion.5 = bf16[256,3072]{1,0:T(8,128)(2,1)S(1)} fusion(bf16[256,3072]{1,0:T(8,128)(2,1)S(1)} %multiply_convert_fusion, bf16[3072,3072]{1,0:T(8,128)(2,1)} %param.6), kind=kOutput, calls=%fused_computation.9 | convolution fusion | flops 4832624640 | bytes 22020096 | tf_op jit(solution)/shard_map/dot_general | solution.py:12
  164.7 5.2 %collective-permute-start.19 = (bf16[128,3072]{1,0:T(8,128)(2,1)}, bf16[128,3072]{1,0:T(8,128)(2,1)}, u32[]{:S(2)}, u32[]{:S(2)}) collective-permute-start(bf16[128,3072]{1,0:T(8,128)(2,1)} %get-tuple-element.111), channel_id=1, source_target_pairs={{0,4},{1,5},{2,6},{3,7},{16,20},{17,21},{18,22},{19,23}} | collective-permute-start | bytes 2359304 | tf_op jit(solution)/shard_map/ppermute | solution.py:48
  169.9 1.9 collective-permute-start.20
  171.8 10.4 %convolution_convert_fusion.4 = bf16[256,3072]{1,0:T(8,128)(2,1)} fusion(bf16[256,3072]{1,0:T(8,128)(2,1)S(1)} %pad_maximum_fusion.3, bf16[3072,3072]{1,0:T(8,128)(2,1)} %param.6), kind=kOutput, calls=%fused_computation.8 | convolution fusion | flops 4832624640 | bytes 22020096 | tf_op jit(solution)/shard_map/dot_general | solution.py:12
  182.2 2.1 constant_dynamic-update-slice_fusion.4
  185.3 2.2 convert_add_fusion.1
  188.9 2.8 constant_dynamic-update-slice_fusion.12
  195.5 4.4 %fusion.24 = (bf16[512,1536]{1,0:T(8,128)(2,1)}, bf16[512,1536]{1,0:T(8,128)(2,1)S(1)}) fusion(s32[]{:T(128)S(6)} %select_n.106, bf16[256,3072]{1,0:T(8,128)(2,1)} %copy-done.10, bf16[256,3072]{1,0:T(8,128)(2,1)} %copy-done.11, s32[]{:T(128)S(6)} %select_n.104), kind=kLoop, calls=%fused_computation.53 | loop fusion | flops 6291456 | bytes 6291464 | tf_op jit(solution)/shard_map/concatenate | solution.py:111
  199.9 1.6 collective-permute-start.30
  201.5 3.3 %fusion.20 = (bf16[128,3072]{1,0:T(8,128)(2,1)}, bf16[128,3072]{1,0:T(8,128)(2,1)}) fusion(bf16[128,3072]{1,0:T(8,128)(2,1)} %collective-permute-done.19, bf16[256,3072]{1,0:T(8,128)(2,1)S(1)} %copy-done.16, bf16[128,3072]{1,0:T(8,128)(2,1)} %collective-permute-done.20), kind=kLoop, calls=%fused_computation.49 | loop fusion | flops 2752512 | bytes 3932160 | tf_op jit(solution)/shard_map/convert_element_type | solution.py:42
  204.8 1.9 collective-permute-start.22
  206.7 1.6 collective-permute-start.24
  208.3 2.4 fusion.13
  210.7 9.2 %convolution_convert_fusion.3 = bf16[256,3072]{1,0:T(8,128)(2,1)S(1)} fusion(bf16[256,3072]{1,0:T(8,128)(2,1)S(1)} %fusion.13, bf16[3072,3072]{1,0:T(8,128)(2,1)} %param.5), kind=kOutput, calls=%fused_computation.7 | convolution fusion | flops 4832624640 | bytes 22020096 | tf_op jit(solution)/shard_map/dot_general | solution.py:12
  220.1 2.0 collective-permute-start.27
  223.0 1.9 collective-permute-done.29
  226.4 8.1 %collective-permute-done.30 = bf16[512,1536]{1,0:T(8,128)(2,1)S(1)} collective-permute-done((bf16[512,1536]{1,0:T(8,128)(2,1)}, bf16[512,1536]{1,0:T(8,128)(2,1)S(1)}, u32[]{:S(2)}, u32[]{:S(2)}) %collective-permute-start.30) | collective-permute-done | bytes 1572896 | tf_op jit(solution)/shard_map/ppermute | solution.py:90
  234.5 1.6 collective-permute-start.37
  237.2 2.1 fusion.6
  239.3 9.2 %convolution_convert_fusion.2 = bf16[256,3072]{1,0:T(8,128)(2,1)S(1)} fusion(bf16[256,3072]{1,0:T(8,128)(2,1)S(1)} %fusion.6, bf16[3072,3072]{1,0:T(8,128)(2,1)} %param.5), kind=kOutput, calls=%fused_computation.6 | convolution fusion | flops 4832624640 | bytes 22020096 | tf_op jit(solution)/shard_map/dot_general | solution.py:12
  249.2 1.3 copy-done.3
  250.5 1.7 add_convert_fusion.5
  253.5 4.6 %collective-permute-start.23 = (bf16[128,3072]{1,0:T(8,128)(2,1)S(1)}, bf16[128,3072]{1,0:T(8,128)(2,1)S(1)}, u32[]{:S(2)}, u32[]{:S(2)}) collective-permute-start(bf16[128,3072]{1,0:T(8,128)(2,1)S(1)} %get-tuple-element.106), channel_id=1, source_target_pairs={{0,4},{4,8},{8,12},{1,5},{5,9},{9,13},{2,6},{6,10},{10,14},{3,7},{... | collective-permute-start | bytes 2359304 | tf_op jit(solution)/shard_map/ppermute | solution.py:48
  258.5 5.0 %collective-permute-done.36 = bf16[256,1536]{1,0:T(8,128)(2,1)S(1)} collective-permute-done((bf16[256,1536]{1,0:T(8,128)(2,1)S(1)}, bf16[256,1536]{1,0:T(8,128)(2,1)S(1)}, u32[]{:S(2)}, u32[]{:S(2)}) %collective-permute-start.36) | collective-permute-done | bytes 786464 | tf_op jit(solution)/shard_map/ppermute | solution.py:90
  265.1 1.6 fusion.23
  266.8 2.7 collective-permute-start.31
  269.5 2.0 collective-permute-start.32
  272.7 2.2 broadcast_select_fusion.3
  275.0 1.8 broadcast_select_fusion.1
  276.8 15.4 %convolution_convert_fusion.1 = bf16[768,3072]{1,0:T(8,128)(2,1)} fusion(bf16[2048,3072]{1,0:T(8,128)(2,1)} %all-gather.3.cloned.1.call-done, bf16[1024,768]{1,0:T(8,128)(2,1)} %get-tuple-element.93, bf16[1024,768]{1,0:T(8,128)(2,1)} %get-tuple-element.92), kind=kOutput, calls=%fused_computation.1 | convolution fusion | flops 9672327168 | bytes 20447232 | tf_op jit(solution)/shard_map/dot_general | solution.py:12
  292.2 3.1 add_convert_fusion.2
  296.6 5.6 %collective-permute-start.34 = (bf16[128,3072]{1,0:T(8,128)(2,1)}, bf16[128,3072]{1,0:T(8,128)(2,1)}, u32[]{:S(2)}, u32[]{:S(2)}) collective-permute-start(bf16[128,3072]{1,0:T(8,128)(2,1)} %get-tuple-element.100), channel_id=1, source_target_pairs={{0,4},{4,8},{8,12},{1,5},{5,9},{9,13},{2,6},{6,10},{10,14},{3,7},{... | collective-permute-start | bytes 2359304 | tf_op jit(solution)/shard_map/ppermute | solution.py:48
  302.3 15.0 %convolution_convert_fusion = bf16[3072,768]{1,0:T(8,128)(2,1)} fusion(bf16[2048,3072]{1,0:T(8,128)(2,1)} %all-gather.5.cloned.1.call-done, bf16[1024,768]{1,0:T(8,128)(2,1)} %get-tuple-element.91, bf16[1024,768]{1,0:T(8,128)(2,1)S(1)} %get-tuple-element.90), kind=kOutput, calls=%fused_computation | convolution fusion | flops 9672327168 | bytes 20447232 | tf_op jit(solution)/shard_map/dot_general | solution.py:12
  317.3 2.6 add_convert_fusion
  (134 shorter events, 34.0 us)
Async XLA Ops:
  7.2 56.0 %copy-start.20 = (bf16[128,3072]{1,0:T(8,128)(2,1)S(1)}, bf16[128,3072]{1,0:T(8,128)(2,1)}, u32[]{:S(2)}) copy-start(bf16[128,3072]{1,0:T(8,128)(2,1)} %param.4) | copy-start | bytes 2359300
  7.2 269.6 %all-gather.3.cloned.1.call-start = ((), (), s32[]{:S(2)}) async-start(), calls=%async_computation | async-start | bytes 18874368 | tf_op jit(solution)/shard_map/all_gather | solution.py:107
  7.2 22.2 %collective-permute-start = (bf16[128,3072]{1,0:T(8,128)(2,1)}, bf16[128,3072]{1,0:T(8,128)(2,1)S(1)}, u32[]{:S(2)}, u32[]{:S(2)}) collective-permute-start(bf16[128,3072]{1,0:T(8,128)(2,1)} %param.4), channel_id=1, source_target_pairs={{0,4},{4,8},{8,12},{1,5},{5,9},{9,13},{2,6},{6,10},{10,14},{3,7},{... | collective-permute-start | bytes 2359304 | tf_op jit(solution)/shard_map/ppermute | solution.py:25
  12.3 21.1 %collective-permute-start.1 = (bf16[128,3072]{1,0:T(8,128)(2,1)}, bf16[128,3072]{1,0:T(8,128)(2,1)S(1)}, u32[]{:S(2)}, u32[]{:S(2)}) collective-permute-start(bf16[128,3072]{1,0:T(8,128)(2,1)} %param.4), channel_id=1, source_target_pairs={{4,0},{8,4},{12,8},{5,1},{9,5},{13,9},{6,2},{10,6},{14,10},{7,3},{... | collective-permute-start | bytes 2359304 | tf_op jit(solution)/shard_map/ppermute | solution.py:26
  13.6 20.7 %collective-permute-start.2 = (bf16[128,3072]{1,0:T(8,128)(2,1)}, bf16[128,3072]{1,0:T(8,128)(2,1)S(1)}, u32[]{:S(2)}, u32[]{:S(2)}) collective-permute-start(bf16[128,3072]{1,0:T(8,128)(2,1)} %param.4), channel_id=1, source_target_pairs={{0,2},{1,3},{2,0},{3,1},{4,6},{5,7},{6,4},{7,5},{8,10},{9,11},{10,... | collective-permute-start | bytes 2359304 | tf_op jit(solution)/shard_map/ppermute | solution.py:77
  15.2 34.7 %collective-permute-start.5 = (bf16[128,3072]{1,0:T(8,128)(2,1)}, bf16[128,3072]{1,0:T(8,128)(2,1)}, u32[]{:S(2)}, u32[]{:S(2)}) collective-permute-start(bf16[128,3072]{1,0:T(8,128)(2,1)} %param.7), channel_id=1, source_target_pairs={{0,2},{1,3},{2,0},{3,1},{4,6},{5,7},{6,4},{7,5},{8,10},{9,11},{10,... | collective-permute-start | bytes 2359304 | tf_op jit(solution)/shard_map/ppermute | solution.py:77
  34.4 38.0 %copy-start.21 = (bf16[128,3072]{1,0:T(8,128)(2,1)}, bf16[128,3072]{1,0:T(8,128)(2,1)S(1)}, u32[]{:S(2)}) copy-start(bf16[128,3072]{1,0:T(8,128)(2,1)S(1)} %collective-permute-done.2) | copy-start | bytes 2359300
  34.4 15.5 %collective-permute-start.3 = (bf16[128,3072]{1,0:T(8,128)(2,1)S(1)}, bf16[128,3072]{1,0:T(8,128)(2,1)}, u32[]{:S(2)}, u32[]{:S(2)}) collective-permute-start(bf16[128,3072]{1,0:T(8,128)(2,1)S(1)} %collective-permute-done), channel_id=1, source_target_pairs={{4,8},{8,12},{5,9},{9,13},{6,10},{10,14},{7,11},{11,15},{20,24},{2... | collective-permute-start | bytes 2359304 | tf_op jit(solution)/shard_map/ppermute | solution.py:25
  35.9 21.5 %collective-permute-start.4 = (bf16[128,3072]{1,0:T(8,128)(2,1)S(1)}, bf16[128,3072]{1,0:T(8,128)(2,1)}, u32[]{:S(2)}, u32[]{:S(2)}) collective-permute-start(bf16[128,3072]{1,0:T(8,128)(2,1)S(1)} %collective-permute-done.1), channel_id=1, source_target_pairs={{4,0},{8,4},{5,1},{9,5},{6,2},{10,6},{7,3},{11,7},{20,16},{24,20},... | collective-permute-start | bytes 2359304 | tf_op jit(solution)/shard_map/ppermute | solution.py:26
  57.4 16.5 %collective-permute-start.6 = (bf16[128,3072]{1,0:T(8,128)(2,1)}, bf16[128,3072]{1,0:T(8,128)(2,1)S(1)}, u32[]{:S(2)}, u32[]{:S(2)}) collective-permute-start(bf16[128,3072]{1,0:T(8,128)(2,1)} %collective-permute-done.3), channel_id=1, source_target_pairs={{8,12},{9,13},{10,14},{11,15},{24,28},{25,29},{26,30},{27,31}} | collective-permute-start | bytes 2359304 | tf_op jit(solution)/shard_map/ppermute | solution.py:25
  58.1 17.3 %collective-permute-start.7 = (bf16[128,3072]{1,0:T(8,128)(2,1)}, bf16[128,3072]{1,0:T(8,128)(2,1)S(1)}, u32[]{:S(2)}, u32[]{:S(2)}) collective-permute-start(bf16[128,3072]{1,0:T(8,128)(2,1)} %collective-permute-done.4), channel_id=1, source_target_pairs={{4,0},{5,1},{6,2},{7,3},{20,16},{21,17},{22,18},{23,19}} | collective-permute-start | bytes 2359304 | tf_op jit(solution)/shard_map/ppermute | solution.py:26
  61.6 15.2 %collective-permute-start.8 = (bf16[128,3072]{1,0:T(8,128)(2,1)S(1)}, bf16[128,3072]{1,0:T(8,128)(2,1)S(1)}, u32[]{:S(2)}, u32[]{:S(2)}) collective-permute-start(bf16[128,3072]{1,0:T(8,128)(2,1)S(1)} %get-tuple-element.83), channel_id=1, source_target_pairs={{0,2},{1,3},{2,0},{3,1},{4,6},{5,7},{6,4},{7,5},{8,10},{9,11},{10,... | collective-permute-start | bytes 2359304 | tf_op jit(solution)/shard_map/ppermute | solution.py:77
  72.4 5.4 %copy-start.12 = (bf16[128,3072]{1,0:T(8,128)(2,1)S(1)}, bf16[128,3072]{1,0:T(8,128)(2,1)}, u32[]{:S(2)}) copy-start(bf16[128,3072]{1,0:T(8,128)(2,1)} %param.7) | copy-start | bytes 2359300
  72.4 37.4 %collective-permute-start.13 = (bf16[256,3072]{1,0:T(8,128)(2,1)S(1)}, bf16[256,3072]{1,0:T(8,128)(2,1)S(1)}, u32[]{:S(2)}, u32[]{:S(2)}) collective-permute-start(bf16[256,3072]{1,0:T(8,128)(2,1)S(1)} %convolution_convert_fusion.9), channel_id=1, source_target_pairs={{0,16},{16,0},{1,17},{17,1},{2,18},{18,2},{3,19},{19,3},{4,20},{20... | collective-permute-start | bytes 4718600 | tf_op jit(solution)/shard_map/ppermute | solution.py:60
  77.8 16.5 %copy-start.1 = (bf16[256,3072]{1,0:T(8,128)(2,1)}, bf16[256,3072]{1,0:T(8,128)(2,1)S(1)}, u32[]{:S(2)}) copy-start(bf16[256,3072]{1,0:T(8,128)(2,1)S(1)} %pad_maximum_fusion.1) | copy-start | bytes 4718596
  77.8 19.0 %collective-permute-start.9 = (bf16[128,3072]{1,0:T(8,128)(2,1)S(1)}, bf16[128,3072]{1,0:T(8,128)(2,1)S(1)}, u32[]{:S(2)}, u32[]{:S(2)}) collective-permute-start(bf16[128,3072]{1,0:T(8,128)(2,1)S(1)} %copy-done.12), channel_id=1, source_target_pairs={{0,4},{4,8},{8,12},{1,5},{5,9},{9,13},{2,6},{6,10},{10,14},{3,7},{... | collective-permute-start | bytes 2359304 | tf_op jit(solution)/shard_map/ppermute | solution.py:25
  82.2 15.8 %collective-permute-start.10 = (bf16[128,3072]{1,0:T(8,128)(2,1)S(1)}, bf16[128,3072]{1,0:T(8,128)(2,1)S(1)}, u32[]{:S(2)}, u32[]{:S(2)}) collective-permute-start(bf16[128,3072]{1,0:T(8,128)(2,1)S(1)} %copy-done.12), channel_id=1, source_target_pairs={{4,0},{8,4},{12,8},{5,1},{9,5},{13,9},{6,2},{10,6},{14,10},{7,3},{... | collective-permute-start | bytes 2359304 | tf_op jit(solution)/shard_map/ppermute | solution.py:26
  83.5 32.4 %collective-permute-start.14 = (bf16[256,3072]{1,0:T(8,128)(2,1)S(1)}, bf16[256,3072]{1,0:T(8,128)(2,1)S(1)}, u32[]{:S(2)}, u32[]{:S(2)}) collective-permute-start(bf16[256,3072]{1,0:T(8,128)(2,1)S(1)} %pad_maximum_fusion.1), channel_id=1, source_target_pairs={{0,2},{1,3},{2,0},{3,1},{4,6},{5,7},{6,4},{7,5},{8,10},{9,11},{10,... | collective-permute-start | bytes 4718600 | tf_op jit(solution)/shard_map/ppermute | solution.py:77
  94.3 43.6 %copy-start.6 = (bf16[256,3072]{1,0:T(8,128)(2,1)}, bf16[256,3072]{1,0:T(8,128)(2,1)S(1)}, u32[]{:S(2)}) copy-start(bf16[256,3072]{1,0:T(8,128)(2,1)S(1)} %convolution_convert_fusion.8) | copy-start | bytes 4718596
  94.3 43.6 %collective-permute-start.18 = (bf16[256,3072]{1,0:T(8,128)(2,1)S(1)}, bf16[256,3072]{1,0:T(8,128)(2,1)S(1)}, u32[]{:S(2)}, u32[]{:S(2)}) collective-permute-start(bf16[256,3072]{1,0:T(8,128)(2,1)S(1)} %convolution_convert_fusion.8), channel_id=1, source_target_pairs={{0,16},{16,0},{1,17},{17,1},{2,18},{18,2},{3,19},{19,3},{4,20},{20... | collective-permute-start | bytes 4718600 | tf_op jit(solution)/shard_map/ppermute | solution.py:60
  97.9 12.4 %collective-permute-start.11 = (bf16[128,3072]{1,0:T(8,128)(2,1)S(1)}, bf16[128,3072]{1,0:T(8,128)(2,1)S(1)}, u32[]{:S(2)}, u32[]{:S(2)}) collective-permute-start(bf16[128,3072]{1,0:T(8,128)(2,1)S(1)} %collective-permute-done.9), channel_id=1, source_target_pairs={{4,8},{8,12},{5,9},{9,13},{6,10},{10,14},{7,11},{11,15},{20,24},{2... | collective-permute-start | bytes 2359304 | tf_op jit(solution)/shard_map/ppermute | solution.py:25
  98.6 17.3 %collective-permute-start.12 = (bf16[128,3072]{1,0:T(8,128)(2,1)S(1)}, bf16[128,3072]{1,0:T(8,128)(2,1)S(1)}, u32[]{:S(2)}, u32[]{:S(2)}) collective-permute-start(bf16[128,3072]{1,0:T(8,128)(2,1)S(1)} %collective-permute-done.10), channel_id=1, source_target_pairs={{4,0},{8,4},{5,1},{9,5},{6,2},{10,6},{7,3},{11,7},{20,16},{24,20},... | collective-permute-start | bytes 2359304 | tf_op jit(solution)/shard_map/ppermute | solution.py:26
  115.9 23.3 %collective-permute-start.15 = (bf16[128,3072]{1,0:T(8,128)(2,1)S(1)}, bf16[128,3072]{1,0:T(8,128)(2,1)S(1)}, u32[]{:S(2)}, u32[]{:S(2)}) collective-permute-start(bf16[128,3072]{1,0:T(8,128)(2,1)S(1)} %collective-permute-done.11), channel_id=1, source_target_pairs={{8,12},{9,13},{10,14},{11,15},{24,28},{25,29},{26,30},{27,31}} | collective-permute-start | bytes 2359304 | tf_op jit(solution)/shard_map/ppermute | solution.py:25
  117.1 22.1 %collective-permute-start.16 = (bf16[128,3072]{1,0:T(8,128)(2,1)S(1)}, bf16[128,3072]{1,0:T(8,128)(2,1)S(1)}, u32[]{:S(2)}, u32[]{:S(2)}) collective-permute-start(bf16[128,3072]{1,0:T(8,128)(2,1)S(1)} %collective-permute-done.12), channel_id=1, source_target_pairs={{4,0},{5,1},{6,2},{7,3},{20,16},{21,17},{22,18},{23,19}} | collective-permute-start | bytes 2359304 | tf_op jit(solution)/shard_map/ppermute | solution.py:26
  119.8 19.4 %collective-permute-start.17 = (bf16[128,3072]{1,0:T(8,128)(2,1)S(1)}, bf16[128,3072]{1,0:T(8,128)(2,1)S(1)}, u32[]{:S(2)}, u32[]{:S(2)}) collective-permute-start(bf16[128,3072]{1,0:T(8,128)(2,1)S(1)} %get-tuple-element.89), channel_id=1, source_target_pairs={{0,2},{1,3},{2,0},{3,1},{4,6},{5,7},{6,4},{7,5},{8,10},{9,11},{10,... | collective-permute-start | bytes 2359304 | tf_op jit(solution)/shard_map/ppermute | solution.py:77
  122.5 10.9 %copy-start.10 = (bf16[256,3072]{1,0:T(8,128)(2,1)}, bf16[256,3072]{1,0:T(8,128)(2,1)S(1)}, u32[]{:S(2)}) copy-start(bf16[256,3072]{1,0:T(8,128)(2,1)S(1)} %multiply_convert_fusion.1) | copy-start | bytes 4718596
  137.9 2.7 copy-start.8
  139.2 14.1 %copy-start.11 = (bf16[256,3072]{1,0:T(8,128)(2,1)}, bf16[256,3072]{1,0:T(8,128)(2,1)S(1)}, u32[]{:S(2)}) copy-start(bf16[256,3072]{1,0:T(8,128)(2,1)S(1)} %multiply_convert_fusion) | copy-start | bytes 4718596
  139.2 2.6 copy-start.25
  141.9 45.6 %collective-permute-start.26 = (bf16[256,3072]{1,0:T(8,128)(2,1)S(1)}, bf16[256,3072]{1,0:T(8,128)(2,1)S(1)}, u32[]{:S(2)}, u32[]{:S(2)}) collective-permute-start(bf16[256,3072]{1,0:T(8,128)(2,1)S(1)} %pad_maximum_fusion.2), channel_id=1, source_target_pairs={{0,2},{1,3},{2,0},{3,1},{4,6},{5,7},{6,4},{7,5},{8,10},{9,11},{10,... | collective-permute-start | bytes 4718600 | tf_op jit(solution)/shard_map/ppermute | solution.py:77
  151.7 33.6 %collective-permute-start.21 = (bf16[256,3072]{1,0:T(8,128)(2,1)S(1)}, bf16[256,3072]{1,0:T(8,128)(2,1)S(1)}, u32[]{:S(2)}, u32[]{:S(2)}) collective-permute-start(bf16[256,3072]{1,0:T(8,128)(2,1)S(1)} %convolution_convert_fusion.6), channel_id=1, source_target_pairs={{0,16},{16,0},{1,17},{17,1},{2,18},{18,2},{3,19},{19,3},{4,20},{20... | collective-permute-start | bytes 4718600 | tf_op jit(solution)/shard_map/ppermute | solution.py:60
  164.7 22.8 %collective-permute-start.19 = (bf16[128,3072]{1,0:T(8,128)(2,1)}, bf16[128,3072]{1,0:T(8,128)(2,1)}, u32[]{:S(2)}, u32[]{:S(2)}) collective-permute-start(bf16[128,3072]{1,0:T(8,128)(2,1)} %get-tuple-element.111), channel_id=1, source_target_pairs={{0,4},{1,5},{2,6},{3,7},{16,20},{17,21},{18,22},{19,23}} | collective-permute-start | bytes 2359304 | tf_op jit(solution)/shard_map/ppermute | solution.py:48
  169.9 14.4 %copy-start.26 = (bf16[128,3072]{1,0:T(8,128)(2,1)S(1)}, bf16[128,3072]{1,0:T(8,128)(2,1)}, u32[]{:S(2)}) copy-start(bf16[128,3072]{1,0:T(8,128)(2,1)} %copy-done.25) | copy-start | bytes 2359300
  169.9 17.6 %collective-permute-start.20 = (bf16[128,3072]{1,0:T(8,128)(2,1)S(1)}, bf16[128,3072]{1,0:T(8,128)(2,1)}, u32[]{:S(2)}, u32[]{:S(2)}) collective-permute-start(bf16[128,3072]{1,0:T(8,128)(2,1)S(1)} %get-tuple-element.110), channel_id=1, source_target_pairs={{12,8},{13,9},{14,10},{15,11},{28,24},{29,25},{30,26},{31,27}} | collective-permute-start | bytes 2359304 | tf_op jit(solution)/shard_map/ppermute | solution.py:49
  188.8 113.5 %all-gather.5.cloned.1.call-start = ((), (), s32[]{:S(2)}) async-start(), calls=%async_computation.1 | async-start | bytes 18874368 | tf_op jit(solution)/shard_map/all_gather | solution.py:107
  188.9 2.8 copy-start.22
  188.9 3.7 %copy-start.24 = (bf16[128,3072]{1,0:T(8,128)(2,1)S(1)}, bf16[128,3072]{1,0:T(8,128)(2,1)}, u32[]{:S(2)}) copy-start(bf16[128,3072]{1,0:T(8,128)(2,1)} %copy-done.23) | copy-start | bytes 2359300
  188.9 4.7 %copy-start.14 = (bf16[256,3072]{1,0:T(8,128)(2,1)S(1)}, bf16[256,3072]{1,0:T(8,128)(2,1)}, u32[]{:S(2)}) copy-start(bf16[256,3072]{1,0:T(8,128)(2,1)} %copy-done.13) | copy-start | bytes 4718596
  194.9 6.6 %copy-start.16 = (bf16[256,3072]{1,0:T(8,128)(2,1)S(1)}, bf16[256,3072]{1,0:T(8,128)(2,1)}, u32[]{:S(2)}) copy-start(bf16[256,3072]{1,0:T(8,128)(2,1)} %convolution_convert_fusion.7) | copy-start | bytes 4718596
  194.9 30.0 %collective-permute-start.29 = (bf16[256,3072]{1,0:T(8,128)(2,1)}, bf16[256,3072]{1,0:T(8,128)(2,1)S(1)}, u32[]{:S(2)}, u32[]{:S(2)}) collective-permute-start(bf16[256,3072]{1,0:T(8,128)(2,1)} %convolution_convert_fusion.4), channel_id=1, source_target_pairs={{0,16},{16,0},{1,17},{17,1},{2,18},{18,2},{3,19},{19,3},{4,20},{20... | collective-permute-start | bytes 4718600 | tf_op jit(solution)/shard_map/ppermute | solution.py:60
  195.5 12.8 %copy-start.7 = (bf16[256,3072]{1,0:T(8,128)(2,1)S(1)}, bf16[256,3072]{1,0:T(8,128)(2,1)}, u32[]{:S(2)}) copy-start(bf16[256,3072]{1,0:T(8,128)(2,1)} %copy-done.6) | copy-start | bytes 4718596
  195.5 12.8 %copy-start.9 = (bf16[256,3072]{1,0:T(8,128)(2,1)S(1)}, bf16[256,3072]{1,0:T(8,128)(2,1)}, u32[]{:S(2)}) copy-start(bf16[256,3072]{1,0:T(8,128)(2,1)} %copy-done.8) | copy-start | bytes 4718596
  199.9 8.4 %copy-start = (f32[256,3072]{1,0:T(8,128)S(1)}, f32[256,3072]{1,0:T(8,128)}, u32[]{:S(2)}) copy-start(f32[256,3072]{1,0:T(8,128)} %convert_add_fusion.1) | copy-start | bytes 9437188
  199.9 34.6 %collective-permute-start.30 = (bf16[512,1536]{1,0:T(8,128)(2,1)}, bf16[512,1536]{1,0:T(8,128)(2,1)S(1)}, u32[]{:S(2)}, u32[]{:S(2)}) collective-permute-start(bf16[512,1536]{1,0:T(8,128)(2,1)} %get-tuple-element.94), channel_id=1, source_target_pairs={{0,2},{1,3},{2,0},{3,1},{4,6},{5,7},{6,4},{7,5},{8,10},{9,11},{10,... | collective-permute-start | bytes 4718600 | tf_op jit(solution)/shard_map/ppermute | solution.py:90
  204.8 44.4 %collective-permute-start.22 = (bf16[128,3072]{1,0:T(8,128)(2,1)}, bf16[128,3072]{1,0:T(8,128)(2,1)S(1)}, u32[]{:S(2)}, u32[]{:S(2)}) collective-permute-start(bf16[128,3072]{1,0:T(8,128)(2,1)} %get-tuple-element.108), channel_id=1, source_target_pairs={{0,4},{4,8},{1,5},{5,9},{2,6},{6,10},{3,7},{7,11},{16,20},{20,24},... | collective-permute-start | bytes 2359304 | tf_op jit(solution)/shard_map/ppermute | solution.py:48
  206.7 42.5 %collective-permute-start.24 = (bf16[128,3072]{1,0:T(8,128)(2,1)}, bf16[128,3072]{1,0:T(8,128)(2,1)}, u32[]{:S(2)}, u32[]{:S(2)}) collective-permute-start(bf16[128,3072]{1,0:T(8,128)(2,1)} %get-tuple-element.109), channel_id=1, source_target_pairs={{8,4},{12,8},{9,5},{13,9},{10,6},{14,10},{11,7},{15,11},{24,20},{2... | collective-permute-start | bytes 2359304 | tf_op jit(solution)/shard_map/ppermute | solution.py:49
  219.9 3.1 copy-start.4
  219.9 5.9 %copy-start.15 = (bf16[256,3072]{1,0:T(8,128)(2,1)S(1)}, bf16[256,3072]{1,0:T(8,128)(2,1)}, u32[]{:S(2)}) copy-start(bf16[256,3072]{1,0:T(8,128)(2,1)} %convolution_convert_fusion.4) | copy-start | bytes 4718596
  220.1 16.0 %collective-permute-start.27 = (bf16[128,3072]{1,0:T(8,128)(2,1)S(1)}, bf16[128,3072]{1,0:T(8,128)(2,1)S(1)}, u32[]{:S(2)}, u32[]{:S(2)}) collective-permute-start(bf16[128,3072]{1,0:T(8,128)(2,1)S(1)} %get-tuple-element.105), channel_id=1, source_target_pairs={{0,4},{1,5},{2,6},{3,7},{16,20},{17,21},{18,22},{19,23}} | collective-permute-start | bytes 2359304 | tf_op jit(solution)/shard_map/ppermute | solution.py:48
  224.9 11.1 %collective-permute-start.28 = (bf16[128,3072]{1,0:T(8,128)(2,1)S(1)}, bf16[128,3072]{1,0:T(8,128)(2,1)S(1)}, u32[]{:S(2)}, u32[]{:S(2)}) collective-permute-start(bf16[128,3072]{1,0:T(8,128)(2,1)S(1)} %get-tuple-element.104), channel_id=1, source_target_pairs={{12,8},{13,9},{14,10},{15,11},{28,24},{29,25},{30,26},{31,27}} | collective-permute-start | bytes 2359304 | tf_op jit(solution)/shard_map/ppermute | solution.py:49
  234.5 24.0 %collective-permute-start.37 = (bf16[256,1536]{1,0:T(8,128)(2,1)}, bf16[256,1536]{1,0:T(8,128)(2,1)S(1)}, u32[]{:S(2)}, u32[]{:S(2)}) collective-permute-start(bf16[256,1536]{1,0:T(8,128)(2,1)} %get-tuple-element.99), channel_id=1, source_target_pairs={{0,2},{1,3},{2,0},{3,1},{4,6},{5,7},{6,4},{7,5},{8,10},{9,11},{10,... | collective-permute-start | bytes 2359304 | tf_op jit(solution)/shard_map/ppermute | solution.py:90
  248.5 15.5 %copy-start.18 = (bf16[256,3072]{1,0:T(8,128)(2,1)}, bf16[256,3072]{1,0:T(8,128)(2,1)S(1)}, u32[]{:S(2)}) copy-start(bf16[256,3072]{1,0:T(8,128)(2,1)S(1)} %convolution_convert_fusion.2) | copy-start | bytes 4718596
  248.6 14.9 %collective-permute-start.36 = (bf16[256,1536]{1,0:T(8,128)(2,1)S(1)}, bf16[256,1536]{1,0:T(8,128)(2,1)S(1)}, u32[]{:S(2)}, u32[]{:S(2)}) collective-permute-start(bf16[256,1536]{1,0:T(8,128)(2,1)S(1)} %get-tuple-element.97), channel_id=1, source_target_pairs={{0,2},{1,3},{2,0},{3,1},{4,6},{5,7},{6,4},{7,5},{8,10},{9,11},{10,... | collective-permute-start | bytes 2359304 | tf_op jit(solution)/shard_map/ppermute | solution.py:90
  252.2 17.3 %collective-permute-start.25 = (bf16[128,3072]{1,0:T(8,128)(2,1)S(1)}, bf16[128,3072]{1,0:T(8,128)(2,1)S(1)}, u32[]{:S(2)}, u32[]{:S(2)}) collective-permute-start(bf16[128,3072]{1,0:T(8,128)(2,1)S(1)} %get-tuple-element.107), channel_id=1, source_target_pairs={{4,0},{8,4},{12,8},{5,1},{9,5},{13,9},{6,2},{10,6},{14,10},{7,3},{... | collective-permute-start | bytes 2359304 | tf_op jit(solution)/shard_map/ppermute | solution.py:49
  253.5 18.0 %collective-permute-start.23 = (bf16[128,3072]{1,0:T(8,128)(2,1)S(1)}, bf16[128,3072]{1,0:T(8,128)(2,1)S(1)}, u32[]{:S(2)}, u32[]{:S(2)}) collective-permute-start(bf16[128,3072]{1,0:T(8,128)(2,1)S(1)} %get-tuple-element.106), channel_id=1, source_target_pairs={{0,4},{4,8},{8,12},{1,5},{5,9},{9,13},{2,6},{6,10},{10,14},{3,7},{... | collective-permute-start | bytes 2359304 | tf_op jit(solution)/shard_map/ppermute | solution.py:48
  258.4 14.3 %collective-permute-start.33 = (bf16[1024,768]{1,0:T(8,128)(2,1)S(1)}, bf16[1024,768]{1,0:T(8,128)(2,1)S(1)}, u32[]{:S(2)}, u32[]{:S(2)}) collective-permute-start(bf16[1024,768]{1,0:T(8,128)(2,1)S(1)} %constant_dynamic-slice_fusion.5), channel_id=1, source_target_pairs={{0,1},{1,0},{2,3},{3,2},{4,5},{5,4},{6,7},{7,6},{8,9},{9,8},{10,11... | collective-permute-start | bytes 4718600 | tf_op jit(solution)/shard_map/ppermute | solution.py:100
  263.8 7.7 %copy-start.17 = (bf16[256,3072]{1,0:T(8,128)(2,1)S(1)}, bf16[256,3072]{1,0:T(8,128)(2,1)}, u32[]{:S(2)}) copy-start(bf16[256,3072]{1,0:T(8,128)(2,1)} %convolution_convert_fusion.7) | copy-start | bytes 4718596
  263.9 11.0 %collective-permute-start.38 = (bf16[1024,768]{1,0:T(8,128)(2,1)S(1)}, bf16[1024,768]{1,0:T(8,128)(2,1)S(1)}, u32[]{:S(2)}, u32[]{:S(2)}) collective-permute-start(bf16[1024,768]{1,0:T(8,128)(2,1)S(1)} %constant_dynamic-slice_fusion), channel_id=1, source_target_pairs={{0,1},{1,0},{2,3},{3,2},{4,5},{5,4},{6,7},{7,6},{8,9},{9,8},{10,11... | collective-permute-start | bytes 4718600 | tf_op jit(solution)/shard_map/ppermute | solution.py:100
  266.8 25.4 %collective-permute-start.31 = (bf16[128,3072]{1,0:T(8,128)(2,1)}, bf16[128,3072]{1,0:T(8,128)(2,1)}, u32[]{:S(2)}, u32[]{:S(2)}) collective-permute-start(bf16[128,3072]{1,0:T(8,128)(2,1)} %get-tuple-element.103), channel_id=1, source_target_pairs={{0,4},{4,8},{1,5},{5,9},{2,6},{6,10},{3,7},{7,11},{16,20},{20,24},... | collective-permute-start | bytes 2359304 | tf_op jit(solution)/shard_map/ppermute | solution.py:48
  269.5 22.7 %collective-permute-start.32 = (bf16[128,3072]{1,0:T(8,128)(2,1)}, bf16[128,3072]{1,0:T(8,128)(2,1)}, u32[]{:S(2)}, u32[]{:S(2)}) collective-permute-start(bf16[128,3072]{1,0:T(8,128)(2,1)} %get-tuple-element.102), channel_id=1, source_target_pairs={{8,4},{12,8},{9,5},{13,9},{10,6},{14,10},{11,7},{15,11},{24,20},{2... | collective-permute-start | bytes 2359304 | tf_op jit(solution)/shard_map/ppermute | solution.py:49
  276.8 15.4 %copy-start.5 = (bf16[256,3072]{1,0:T(8,128)(2,1)S(1)}, bf16[256,3072]{1,0:T(8,128)(2,1)}, u32[]{:S(2)}) copy-start(bf16[256,3072]{1,0:T(8,128)(2,1)} %copy-done.4) | copy-start | bytes 4718596
  295.3 22.0 %collective-permute-start.35 = (bf16[128,3072]{1,0:T(8,128)(2,1)}, bf16[128,3072]{1,0:T(8,128)(2,1)}, u32[]{:S(2)}, u32[]{:S(2)}) collective-permute-start(bf16[128,3072]{1,0:T(8,128)(2,1)} %get-tuple-element.101), channel_id=1, source_target_pairs={{4,0},{8,4},{12,8},{5,1},{9,5},{13,9},{6,2},{10,6},{14,10},{7,3},{... | collective-permute-start | bytes 2359304 | tf_op jit(solution)/shard_map/ppermute | solution.py:49
  296.6 20.7 %collective-permute-start.34 = (bf16[128,3072]{1,0:T(8,128)(2,1)}, bf16[128,3072]{1,0:T(8,128)(2,1)}, u32[]{:S(2)}, u32[]{:S(2)}) collective-permute-start(bf16[128,3072]{1,0:T(8,128)(2,1)} %get-tuple-element.100), channel_id=1, source_target_pairs={{0,4},{4,8},{8,12},{1,5},{5,9},{9,13},{2,6},{6,10},{10,14},{3,7},{... | collective-permute-start | bytes 2359304 | tf_op jit(solution)/shard_map/ppermute | solution.py:48
  302.3 15.1 %copy-start.19 = (bf16[256,3072]{1,0:T(8,128)(2,1)S(1)}, bf16[256,3072]{1,0:T(8,128)(2,1)}, u32[]{:S(2)}) copy-start(bf16[256,3072]{1,0:T(8,128)(2,1)} %copy-done.18) | copy-start | bytes 4718596
  (8 other events, 9.7 us)
Sparse Core Ops, SparseCore 0:
  188.9 22.1 all-gather.2
  212.6 26.0 all-gather.4
